TPU v7x, 32 devices: a whole 2x2x4 slice. The times are simulated.
32 devices in a mesh: row: 4 (over y, core), col: 8 (over z, x).
Axes of the slice: x: 2, y: 2, z: 4, core: 2. Of those that a mesh axis runs over, the one named last changes fastest.
Arguments:
- tokens: bfloat16 [64, 8192], P('col', 'row'), may hold values from -6 to 6
- up_blocks: bfloat16 [4, 8, 112, 128, 128], P('row', 'col'), may hold values from -0.1875 to 0.1875
- up_index: int32 [4, 8, 112], P('row', 'col'), may hold values from 0 to 448, as said below
- down_blocks: bfloat16 [4, 8, 112, 128, 128], P('row', 'col'), may hold values from -0.09375 to 0.09375
- down_index: int32 [4, 8, 112], P('row', 'col'), may hold values from 0 to 448, as said below
- out_cot: bfloat16 [64, 8192], P('col', 'row'), may hold values from -1.5 to 1.5
Outputs:
- outputs: bfloat16 [64, 8192], P('col', 'row')
- input_grad: bfloat16 [64, 8192], P('col', 'row')
- up_grad: bfloat16 [4, 8, 112, 128, 128], P('row', 'col')
- down_grad: bfloat16 [4, 8, 112, 128, 128], P('row', 'col')
Inputs may be any that keep to these rules, and one draw needn't show every extreme that they name: `up_index`: each entry names a block of its tile's 16 x 28 grid as row * 28 + column, or is 448 for an empty slot; the named blocks of a tile are distinct and come before its empty slots; every tile names at least one block; the tiles (r, c) with c * 4 // 8 == r name 112 blocks, every other tile fewer. `down_index`: each entry names a block of its tile's 28 x 16 grid (hidden-unit block, width block) as row * 16 + column, or is 448 for an empty slot; the named blocks of a tile are distinct and come before its empty slots; every tile names at least one block; the tiles (r, c) with c * 4 // 8 == r name 112 blocks, every other tile fewer.
All inputs are finite; a program needn't handle non-finite values.
Results may differ from a plain program's by a relative error of at most 0.023.
Values may be sent and summed in bfloat16 or wider, within the bound.
No kernel may reach another device: no remote copies, remote signals or barrier semaphores. Data moves between devices by JAX's collectives and lax.ppermute only.
A program may use at most 64 MiB of HBM per device.

v0:
```python
import jax
import jax.numpy as jnp
from jax import lax
from jax.sharding import PartitionSpec as P

FF = 28672
BS = 128


COEF = 0.7978845608
CUBIC = 0.044715


def gelu_value(values):
    inner = COEF * (values + CUBIC * values * values * values)
    return 0.5 * values * (1.0 + jnp.tanh(inner))


def gelu_slope(values):
    tangent = jnp.tanh(COEF * (values + CUBIC * values * values * values))
    return 0.5 * (1.0 + tangent) + 0.5 * values * (1.0 - tangent * tangent) * COEF * (
        1.0 + 3.0 * CUBIC * values * values
    )


def selectors(indices, leading, trailing):
    lead_pos = indices // trailing
    trail_pos = indices % trailing
    valid = indices < leading * trailing
    lead_sel = (lead_pos[:, None] == jnp.arange(leading, dtype=jnp.int32)[None, :]).astype(
        jnp.bfloat16
    )
    trail_sel = (trail_pos[:, None] == jnp.arange(trailing, dtype=jnp.int32)[None, :]).astype(
        jnp.bfloat16
    )
    return (indices, lead_pos, trail_pos, valid, lead_sel, trail_sel)


def place_blocks(products, positions, valid, width_blocks):
    tok_count = products.shape[0]
    masked = products * valid.astype(jnp.float32)[None, :, None]
    clipped = jnp.clip(positions, 0, width_blocks - 1)
    result = jnp.zeros((tok_count, width_blocks, BS), jnp.float32).at[:, clipped, :].add(masked)
    return result.reshape(tok_count, width_blocks * BS)


def forward_tile(operand, blocks, pattern):
    indices, lead_pos, trail_pos, valid, lead_sel, trail_sel = pattern
    tok_count = operand.shape[0]
    pieces = operand.reshape(tok_count, lead_sel.shape[1], BS)
    picked = jnp.einsum("tab,ka->ktb", pieces, lead_sel, preferred_element_type=jnp.float32).astype(
        jnp.bfloat16
    )
    products = jnp.einsum("ktb,kbd->tkd", picked, blocks, preferred_element_type=jnp.float32)
    return place_blocks(products, trail_pos, valid, trail_sel.shape[1])


def backward_tile(other, blocks, pattern):
    indices, lead_pos, trail_pos, valid, lead_sel, trail_sel = pattern
    tok_count = other.shape[0]
    pieces = other.reshape(tok_count, trail_sel.shape[1], BS)
    picked = jnp.einsum(
        "tcd,kc->ktd", pieces, trail_sel, preferred_element_type=jnp.float32
    ).astype(jnp.bfloat16)
    products = jnp.einsum("ktd,kbd->tkb", picked, blocks, preferred_element_type=jnp.float32)
    return place_blocks(products, lead_pos, valid, lead_sel.shape[1])


def grad_tile(operand, other, pattern):
    indices, lead_pos, trail_pos, valid, lead_sel, trail_sel = pattern
    tok_count = operand.shape[0]
    leading = lead_sel.shape[1]
    trailing = trail_sel.shape[1]
    left_pick = jnp.einsum(
        "tab,ka->ktb",
        operand.reshape(tok_count, leading, BS),
        lead_sel,
        preferred_element_type=jnp.float32,
    ).astype(jnp.bfloat16)
    right_pick = jnp.einsum(
        "tcd,kc->ktd",
        other.reshape(tok_count, trailing, BS),
        trail_sel,
        preferred_element_type=jnp.float32,
    ).astype(jnp.bfloat16)
    return jnp.einsum("ktb,ktd->kbd", left_pick, right_pick, preferred_element_type=jnp.float32)


def shards(tokens, up_blocks, up_index, down_blocks, down_index, out_cot):
    row_blocks = tokens.shape[1] // BS
    col_blocks = FF // (BS * lax.axis_size("col"))
    row_devices = lax.axis_size("row")
    up_weight = up_blocks[0, 0]
    down_weight = down_blocks[0, 0]
    up_pattern = selectors(up_index[0, 0], row_blocks, col_blocks)
    down_pattern = selectors(down_index[0, 0], col_blocks, row_blocks)
    features = lax.all_gather(tokens, "col", axis=0, tiled=True)
    partial_value = forward_tile(features, up_weight, up_pattern)
    tok_count = partial_value.shape[0]
    share_rows = tok_count // row_devices
    hidden_width = partial_value.shape[1]
    received = lax.all_to_all(
        partial_value.astype(jnp.bfloat16).reshape(row_devices, share_rows, hidden_width),
        "row",
        split_axis=0,
        concat_axis=0,
        tiled=True,
    )
    pre_share = jnp.sum(received.astype(jnp.float32), axis=0)
    preact = lax.all_gather(pre_share.astype(jnp.bfloat16), "row", axis=0, tiled=True).astype(
        pre_share.dtype
    )
    hidden = gelu_value(preact).astype(jnp.bfloat16)
    out_terms = forward_tile(hidden, down_weight, down_pattern)
    outputs = lax.psum_scatter(
        out_terms.astype(jnp.bfloat16), "col", scatter_dimension=0, tiled=True
    )
    cotangents = lax.all_gather(out_cot, "col", axis=0, tiled=True)
    act_terms = backward_tile(cotangents, down_weight, down_pattern)
    act_received = lax.all_to_all(
        act_terms.astype(jnp.bfloat16).reshape(row_devices, share_rows, hidden_width),
        "row",
        split_axis=0,
        concat_axis=0,
        tiled=True,
    )
    act_share = jnp.sum(act_received.astype(jnp.float32), axis=0)
    act_grad = lax.all_gather(act_share.astype(jnp.bfloat16), "row", axis=0, tiled=True).astype(
        act_share.dtype
    )
    pre_grad = (act_grad * gelu_slope(preact)).astype(jnp.bfloat16)
    input_terms = backward_tile(pre_grad, up_weight, up_pattern)
    input_grad = lax.psum_scatter(
        input_terms.astype(jnp.bfloat16), "col", scatter_dimension=0, tiled=True
    )
    up_grad = grad_tile(features, pre_grad, up_pattern).astype(jnp.bfloat16)
    down_grad = grad_tile(hidden, cotangents, down_pattern).astype(jnp.bfloat16)
    return (outputs, input_grad, up_grad[None, None], down_grad[None, None])


def solution(mesh):
    placed = (
        P("col", "row"),
        P("row", "col", None, None, None),
        P("row", "col", None),
        P("row", "col", None, None, None),
        P("row", "col", None),
        P("col", "row"),
    )
    return jax.shard_map(
        shards,
        mesh=mesh,
        in_specs=placed,
        out_specs=(
            P("col", "row"),
            P("col", "row"),
            P("row", "col", None, None, None),
            P("row", "col", None, None, None),
        ),
        check_vma=False,
    )
```

profile of v0, /device:TPU:0, one launch (start us, length us, event | category | flops | bytes accessed | tf_op | source)
XLA Modules:
  0.0 291.3 jit_solution(8392222660205617198)
XLA Ops:
  7.2 0.7 fusion.58
  7.8 0.7 fusion.55
  8.5 32.7 %all_gather.12 = bf16[64,2048]{1,0:T(8,128)(2,1)S(1)} all-gather(bf16[8,2048]{1,0:T(8,128)(2,1)} %param.6), channel_id=1, replica_groups=mesh['row'=4,'col'=8] {'col'}, dimensions={0}, use_global_device_ids=true | all-gather | bytes 294912 | tf_op jit(solution)/shard_map/all_gather | solution.py:97
  41.3 0.7 and_select_fusion.2
  41.9 0.7 convolution_convert_fusion.1
  42.6 5.6 %fusion.8 = f32[112,64,128]{2,1,0:T(8,128)} fusion(bf16[1,1,112,128,128]{4,3,2,1,0:T(8,128)(2,1)} %param.7, f32[112]{0:T(128)S(1)} %fusion.55, bf16[112,64,128]{2,0,1:T(8,128)(2,1)S(1)} %convolution_convert_fusion.1), kind=kOutput, calls=%fused_computation.21 | convolution fusion | flops 235798528 | bytes 9175488 | tf_op jit(solution)/shard_map/ktb,kbd->tkd/dot_general | solution.py:54
  48.4 11.9 %scatter_fusion = f32[64,28,128]{2,0,1:T(8,128)S(1)} fusion(f32[64,28,128]{2,0,1:T(8,128)S(1)} %broadcast.362.clone, s32[112]{0:T(128)S(1)} %get-tuple-element.14, f32[112,64,128]{2,1,0:T(8,128)} %fusion.8), kind=kCustom, calls=%fused_computation | custom fusion | flops 917504 | bytes 11010496 | tf_op jit(solution)/shard_map/scatter-add | solution.py:43
  60.4 0.3 copy.19
  60.7 1.0 convert_element_type.91
  61.7 3.5 %all-to-all-start = ((bf16[4,16,3584]{2,1,0:T(8,128)(2,1)}), bf16[4,16,3584]{2,1,0:T(8,128)(2,1)S(1)}, u32[]{:S(2)}, u32[]{:S(2)}) async-start(bf16[4,16,3584]{2,1,0:T(8,128)(2,1)} %convert_element_type.91), calls=%async_computation | async-start | bytes 917504 | tf_op jit(solution)/shard_map/all_to_all | solution.py:102
  65.2 30.8 %all_gather.14 = bf16[64,2048]{1,0:T(8,128)(2,1)S(1)} all-gather(bf16[8,2048]{1,0:T(8,128)(2,1)S(1)} %copy-done.4), channel_id=1, replica_groups=mesh['row'=4,'col'=8] {'col'}, dimensions={0}, use_global_device_ids=true | all-gather | bytes 294912 | tf_op jit(solution)/shard_map/all_gather | solution.py:118
  96.1 0.7 convolution_convert_fusion
  96.8 7.2 %fusion.17 = f32[112,64,128]{2,1,0:T(8,128)} fusion(bf16[1,1,112,128,128]{4,3,2,1,0:T(8,128)(2,1)} %param.9, f32[112]{0:T(128)S(1)} %compare_convert_fusion, bf16[112,64,128]{2,0,1:T(8,128)(2,1)S(1)} %convolution_convert_fusion), kind=kOutput, calls=%fused_computation.24 | convolution fusion | flops 235798528 | bytes 9175488 | tf_op jit(solution)/shard_map/ktd,kbd->tkb/dot_general | solution.py:65
  104.1 11.9 %scatter_fusion.2 = f32[64,28,128]{2,0,1:T(8,128)S(1)} fusion(f32[64,28,128]{2,0,1:T(8,128)S(1)} %broadcast.362.clone.1, s32[112]{0:T(128)S(1)} %get-tuple-element.12, f32[112,64,128]{2,1,0:T(8,128)} %fusion.17), kind=kCustom, calls=%fused_computation.2 | custom fusion | flops 917504 | bytes 11010496 | tf_op jit(solution)/shard_map/scatter-add | solution.py:43
  116.0 0.3 copy.23
  116.3 1.0 convert_element_type.100
  117.4 3.5 %all-to-all-start.1 = ((bf16[4,16,3584]{2,1,0:T(8,128)(2,1)}), bf16[4,16,3584]{2,1,0:T(8,128)(2,1)S(1)}, u32[]{:S(2)}, u32[]{:S(2)}) async-start(bf16[4,16,3584]{2,1,0:T(8,128)(2,1)} %convert_element_type.100), calls=%async_computation.2 | async-start | bytes 917504 | tf_op jit(solution)/shard_map/all_to_all | solution.py:120
  121.0 11.3 %all_gather.13 = bf16[64,3584]{1,0:T(8,128)(2,1)S(1)} all-gather(bf16[16,3584]{1,0:T(8,128)(2,1)S(1)} %reduce_sum.24), channel_id=1, replica_groups=mesh['row'=4,'col'=8] {'row'}, dimensions={0}, use_global_device_ids=true | all-gather | bytes 573440 | tf_op jit(solution)/shard_map/all_gather | solution.py:110
  132.4 6.9 %all_gather.15 = bf16[64,3584]{1,0:T(8,128)(2,1)S(1)} all-gather(bf16[16,3584]{1,0:T(8,128)(2,1)S(1)} %reduce_sum.25), channel_id=1, replica_groups=mesh['row'=4,'col'=8] {'row'}, dimensions={0}, use_global_device_ids=true | all-gather | bytes 573440 | tf_op jit(solution)/shard_map/all_gather | solution.py:128
  139.3 0.7 fusion.35
  140.3 0.7 convolution_convert_fusion.3
  140.9 5.0 %fusion.14 = f32[112,64,128]{2,1,0:T(8,128)} fusion(bf16[1,1,112,128,128]{4,3,2,1,0:T(8,128)(2,1)} %param.9, f32[112]{0:T(128)S(1)} %compare_convert_fusion, bf16[112,64,128]{2,0,1:T(8,128)(2,1)S(1)} %convolution_convert_fusion.3), kind=kOutput, calls=%fused_computation.23 | convolution fusion | flops 235798528 | bytes 9175488 | tf_op jit(solution)/shard_map/ktb,kbd->tkd/dot_general | solution.py:54
  146.0 11.9 %scatter_fusion.1 = f32[64,16,128]{2,0,1:T(8,128)S(1)} fusion(f32[64,16,128]{2,0,1:T(8,128)S(1)} %broadcast.361.clone, s32[112]{0:T(128)S(1)} %get-tuple-element.13, f32[112,64,128]{2,1,0:T(8,128)} %fusion.14), kind=kCustom, calls=%fused_computation.1 | custom fusion | flops 917504 | bytes 11010496 | tf_op jit(solution)/shard_map/scatter-add | solution.py:43
  157.9 0.8 copy_bitcast_fusion.1
  159.1 0.7 convolution_convert_fusion.2
  159.8 7.2 %fusion.11 = f32[112,64,128]{2,1,0:T(8,128)} fusion(bf16[1,1,112,128,128]{4,3,2,1,0:T(8,128)(2,1)} %param.7, f32[112]{0:T(128)S(1)} %fusion.55, bf16[112,64,128]{2,0,1:T(8,128)(2,1)S(1)} %convolution_convert_fusion.2), kind=kOutput, calls=%fused_computation.22 | convolution fusion | flops 235798528 | bytes 9175488 | tf_op jit(solution)/shard_map/ktd,kbd->tkb/dot_general | solution.py:65
  167.0 11.9 %scatter_fusion.3 = f32[64,16,128]{2,0,1:T(8,128)S(1)} fusion(f32[64,16,128]{2,0,1:T(8,128)S(1)} %broadcast.361.clone.1, s32[112]{0:T(128)S(1)} %get-tuple-element.4, f32[112,64,128]{2,1,0:T(8,128)} %fusion.11), kind=kCustom, calls=%fused_computation.3 | custom fusion | flops 917504 | bytes 11010496 | tf_op jit(solution)/shard_map/scatter-add | solution.py:43
  179.0 0.7 copy_bitcast_fusion
  179.7 5.2 %convert_bitcast_fusion.1 = bf16[1,1,112,128,128]{4,3,2,1,0:T(8,128)(2,1)} fusion(bf16[112,64,128]{2,0,1:T(8,128)(2,1)} %copy-done, bf16[112,64,128]{2,0,1:T(8,128)(2,1)} %copy-done.1), kind=kOutput, calls=%fused_computation.13 | convolution fusion | flops 236716032 | bytes 7340032 | tf_op jit(solution)/shard_map/ktb,ktd->kbd/dot_general | solution.py:86
  185.0 3.0 %convert_bitcast_fusion = bf16[1,1,112,128,128]{4,3,2,1,0:T(8,128)(2,1)} fusion(bf16[112,64,128]{2,0,1:T(8,128)(2,1)S(1)} %copy-done.3, bf16[112,64,128]{2,0,1:T(8,128)(2,1)S(1)} %convolution_convert_fusion.3), kind=kOutput, calls=%fused_computation.12 | convolution fusion | flops 236716032 | bytes 7340032 | tf_op jit(solution)/shard_map/ktb,ktd->kbd/dot_general | solution.py:86
  188.0 32.2 %reduce-scatter.3.cloned.1.call-done = bf16[8,2048]{1,0:T(8,128)(2,1)} async-done(((bf16[64,2048]{1,0:T(8,128)(2,1)}), bf16[8,2048]{1,0:T(8,128)(2,1)}) %reduce-scatter.3.cloned.1.call-update) | async-done | bytes 32784 | tf_op jit(solution)/shard_map/reduce_scatter | solution.py:115
  220.2 64.3 %reduce-scatter.5.cloned.1.call-done = bf16[8,2048]{1,0:T(8,128)(2,1)} async-done(((bf16[64,2048]{1,0:T(8,128)(2,1)}), bf16[8,2048]{1,0:T(8,128)(2,1)}) %reduce-scatter.5.cloned.1.call-update) | async-done | bytes 32784 | tf_op jit(solution)/shard_map/reduce_scatter | solution.py:133
  (33 shorter events, 1.5 us)
Async XLA Ops:
  42.6 5.6 %copy-start.1 = (bf16[112,64,128]{2,0,1:T(8,128)(2,1)}, bf16[112,64,128]{2,0,1:T(8,128)(2,1)S(1)}, u32[]{:S(2)}) copy-start(bf16[112,64,128]{2,0,1:T(8,128)(2,1)S(1)} %convolution_convert_fusion.1) | copy-start | bytes 5505028
  60.3 4.9 %copy-start.5 = (s32[1,1,112]{2,1,0:T(1,128)S(1)}, s32[1,1,112]{2,1,0:T(1,128)}, u32[]{:S(2)}) copy-start(s32[1,1,112]{2,1,0:T(1,128)} %param.10) | copy-start | bytes 1348
  60.3 5.0 %copy-start.4 = (bf16[8,2048]{1,0:T(8,128)(2,1)S(1)}, bf16[8,2048]{1,0:T(8,128)(2,1)}, u32[]{:S(2)}) copy-start(bf16[8,2048]{1,0:T(8,128)(2,1)} %param.11) | copy-start | bytes 98308
  61.7 55.7 %all-to-all-start = ((bf16[4,16,3584]{2,1,0:T(8,128)(2,1)}), bf16[4,16,3584]{2,1,0:T(8,128)(2,1)S(1)}, u32[]{:S(2)}, u32[]{:S(2)}) async-start(bf16[4,16,3584]{2,1,0:T(8,128)(2,1)} %convert_element_type.91), calls=%async_computation | async-start | bytes 917504 | tf_op jit(solution)/shard_map/all_to_all | solution.py:102
  96.8 7.2 %copy-start.2 = (bf16[112,64,128]{2,0,1:T(8,128)(2,1)}, bf16[112,64,128]{2,0,1:T(8,128)(2,1)S(1)}, u32[]{:S(2)}) copy-start(bf16[112,64,128]{2,0,1:T(8,128)(2,1)S(1)} %convolution_convert_fusion) | copy-start | bytes 5505028
  117.4 14.9 %all-to-all-start.1 = ((bf16[4,16,3584]{2,1,0:T(8,128)(2,1)}), bf16[4,16,3584]{2,1,0:T(8,128)(2,1)S(1)}, u32[]{:S(2)}, u32[]{:S(2)}) async-start(bf16[4,16,3584]{2,1,0:T(8,128)(2,1)} %convert_element_type.100), calls=%async_computation.2 | async-start | bytes 917504 | tf_op jit(solution)/shard_map/all_to_all | solution.py:120
  120.8 99.3 %reduce-scatter.3.cloned.1.call-start = ((), (), s32[]{:S(2)}) async-start(), calls=%async_computation.4 | async-start | bytes 294912 | tf_op jit(solution)/shard_map/reduce_scatter | solution.py:115
  158.6 125.8 %reduce-scatter.5.cloned.1.call-start = ((), (), s32[]{:S(2)}) async-start(), calls=%async_computation.5 | async-start | bytes 294912 | tf_op jit(solution)/shard_map/reduce_scatter | solution.py:133
  159.8 7.2 %copy-start = (bf16[112,64,128]{2,0,1:T(8,128)(2,1)}, bf16[112,64,128]{2,0,1:T(8,128)(2,1)S(1)}, u32[]{:S(2)}) copy-start(bf16[112,64,128]{2,0,1:T(8,128)(2,1)S(1)} %convolution_convert_fusion.2) | copy-start | bytes 5505028
  179.7 5.2 %copy-start.3 = (bf16[112,64,128]{2,0,1:T(8,128)(2,1)S(1)}, bf16[112,64,128]{2,0,1:T(8,128)(2,1)}, u32[]{:S(2)}) copy-start(bf16[112,64,128]{2,0,1:T(8,128)(2,1)} %copy-done.2) | copy-start | bytes 5505028
Sparse Core Ops, SparseCore 0:
  158.8 61.3 reduce-scatter.2
  224.0 60.3 reduce-scatter.4
where the time goes:
time: 293 us; the launch traced here: 291 us
  waiting for transfers between devices  96.5 us (33%)
  blocking collectives  81.8 us (28%)
  other arithmetic  52 us (18%)
  matrix products  35.9 us (12%)
  between operations  14.3 us (5%)
  starting transfers between devices  7.2 us (2%)
  local copies, waits for them, and re-layouts  3.56 us (1%)
    reduce_scatter x1, waiting for transfers between devices, shards(): lax.psum_scatter(input_terms.astype(jnp.bfloat16), 'col', scatter_dimensi...  64.3 us
    scatter-add x4, other arithmetic, place_blocks(): jnp.zeros((tok_count, width_blocks, BS), jnp.float32).at[:, clipped, :]  47.5 us
    all_gather x1, blocking collectives, shards(): features = lax.all_gather(tokens, 'col', axis=0, tiled=True)  32.7 us
    reduce_scatter x1, waiting for transfers between devices, shards(): lax.psum_scatter(out_terms.astype(jnp.bfloat16), 'col', scatter_dimension...  32.2 us
    all_gather x1, blocking collectives, shards(): cotangents = lax.all_gather(out_cot, 'col', axis=0, tiled=True)  30.8 us
    dot_general x2, matrix products, backward_tile(): jnp.einsum('ktd,kbd->tkb', picked, blocks, preferred_element_type=jnp.flo...  14.3 us
    all_gather x1, blocking collectives, shards(): lax.all_gather(pre_share.astype(jnp.bfloat16), 'row', axis=0, tiled=True)  11.3 us
    dot_general x2, matrix products, forward_tile(): jnp.einsum('ktb,kbd->tkd', picked, blocks, preferred_element_type=jnp.flo...  10.6 us
  transfers between devices with their start and end apart: 4, of which 2 were waited for; matrix products, arithmetic and copies ran while one was open for 17% of the time, Pallas kernels for 0%

commit v1 on v0

v1 whole, which is shorter than its diff:
```python
import functools

import jax
import jax.numpy as jnp
from jax import lax
from jax.experimental import pallas as pl
from jax.experimental.pallas import tpu as pltpu
from jax.sharding import PartitionSpec as P

FF = 28672
BS = 128
COEF = 0.7978845608
CUBIC = 0.044715
F32 = jnp.float32
BF16 = jnp.bfloat16
VMEM = pl.BlockSpec(memory_space=pltpu.VMEM)
SMEM = pl.BlockSpec(memory_space=pltpu.SMEM)


def gelu_value(values):
    inner = COEF * (values + CUBIC * values * values * values)
    return 0.5 * values * (1.0 + jnp.tanh(inner))


def gelu_slope(values):
    tangent = jnp.tanh(COEF * (values + CUBIC * values * values * values))
    return 0.5 * (1.0 + tangent) + 0.5 * values * (1.0 - tangent * tangent) * COEF * (
        1.0 + 3.0 * CUBIC * values * values
    )


def params(megabytes=24):
    return pltpu.CompilerParams(vmem_limit_bytes=megabytes << 20)


def divisor(count, most):
    return max(step for step in range(1, most + 1) if count % step == 0)


def accumulate(index_ref, leading, trailing, forward, operand_ref, blocks_ref, acc):
    acc[...] = jnp.zeros_like(acc)
    slots = index_ref.shape[0]
    step = divisor(slots, 28)
    targets = trailing if forward else leading

    def group(at, carry):
        products = []
        for inner in range(step):
            slot = at * step + inner
            place = index_ref[slot]
            named = place < leading * trailing
            lead, trail = jnp.minimum(place // trailing, leading - 1), place % trailing
            source, target = (lead, trail) if forward else (trail, lead)
            dims = (((1,), (0 if forward else 1,)), ((), ()))
            product = lax.dot_general(
                operand_ref[source], blocks_ref[slot], dims, preferred_element_type=F32
            )
            products.append((jnp.where(named, target, targets), product))
        for target, product in products:
            acc[target] += product
        return carry

    lax.fori_loop(0, slots // step, group, 0)


def split_halves(core, acc, targets, keep_ref, give_ref):
    half = acc.shape[1] // 2
    for at in range(targets):
        keep_ref[at] = acc[at, pl.ds(pl.multiple_of(core * half, half), half), :].astype(BF16)
        give_ref[at] = acc[at, pl.ds(pl.multiple_of((1 - core) * half, half), half), :].astype(BF16)


def up_kernel(leading, trailing, *refs):
    core_ref, index_ref, blocks_ref = refs[:3]
    parts = refs[3:-5]
    tokens_ref, cot_ref, keep_ref, give_ref, acc = refs[-5:]
    rows = parts[0].shape[0] // 2
    for pair in range(len(parts) // 2):
        here = pl.ds(pair * 2 * rows, 2 * rows)
        for at in range(leading):
            lanes = pl.ds(at * BS, BS)
            first = parts[2 * pair][:, lanes].astype(F32)
            second = parts[2 * pair + 1][:, lanes].astype(F32)
            tokens_ref[at, here, :] = jnp.concatenate([first[:rows], second[:rows]]).astype(BF16)
            cot_ref[at, here, :] = jnp.concatenate([first[rows:], second[rows:]]).astype(BF16)
    accumulate(index_ref, leading, trailing, True, tokens_ref, blocks_ref, acc)
    split_halves(core_ref[0], acc, trailing, keep_ref, give_ref)


def act_kernel(leading, trailing, core_ref, index_ref, blocks_ref, cot_ref, keep_ref, give_ref, acc):
    accumulate(index_ref, leading, trailing, False, cot_ref, blocks_ref, acc)
    split_halves(core_ref[0], acc, leading, keep_ref, give_ref)


def join_halves(core, own_ref, other_ref, whole_ref):
    half = own_ref.shape[1]
    for at in range(own_ref.shape[0]):
        whole_ref[at, pl.ds(pl.multiple_of(core * half, half), half), :] = own_ref[at]
        whole_ref[at, pl.ds(pl.multiple_of((1 - core) * half, half), half), :] = other_ref[at]


def down_kernel(
    leading, trailing, core_ref, index_ref, blocks_ref, own_ref, other_ref, hidden_ref, terms_ref, acc
):
    join_halves(core_ref[0], own_ref, other_ref, hidden_ref)
    accumulate(index_ref, leading, trailing, True, hidden_ref, blocks_ref, acc)
    for at in range(trailing):
        terms_ref[at] = acc[at].astype(BF16)


def input_kernel(
    leading, trailing, core_ref, index_ref, blocks_ref, own_ref, other_ref, out_terms_ref, grad_ref, *refs
):
    chunks, acc = refs[:-1], refs[-1]
    join_halves(core_ref[0], own_ref, other_ref, grad_ref)
    accumulate(index_ref, leading, trailing, False, grad_ref, blocks_ref, acc)
    rows = chunks[0].shape[0] // 2
    for at in range(leading):
        for pair in range(len(chunks) // 2):
            here = pl.ds(pair * 2 * rows, 2 * rows)
            outs = out_terms_ref[at, here, :].astype(F32)
            grads = acc[at, here, :]
            for inner in range(2):
                mine = slice(inner * rows, (inner + 1) * rows)
                chunks[2 * pair + inner][:, pl.ds(at * BS, BS)] = jnp.concatenate(
                    [outs[mine], grads[mine]]
                ).astype(BF16)


def grad_kernel(leading, trailing, step, index_ref, left_ref, right_ref, out_ref, turned):
    @pl.when(pl.program_id(0) == 0)
    def _():
        for at in range(leading):
            turned[at] = left_ref[at].T

    for inner in range(step):
        place = index_ref[pl.program_id(0) * step + inner]
        lead, trail = jnp.minimum(place // trailing, leading - 1), place % trailing
        product = jnp.dot(turned[lead], right_ref[trail], preferred_element_type=F32)
        out_ref[inner] = jnp.where(place < leading * trailing, product, 0.0).astype(BF16)


def block_grads(name, index, left, right):
    leading, tok_count, _ = left.shape
    trailing = right.shape[0]
    slots = index.shape[0]
    step = divisor(slots, 16)
    return pl.pallas_call(
        functools.partial(grad_kernel, leading, trailing, step),
        grid=(slots // step,),
        out_shape=jax.ShapeDtypeStruct((slots, BS, BS), BF16),
        in_specs=[SMEM, VMEM, VMEM],
        out_specs=pl.BlockSpec((step, BS, BS), lambda at: (at, 0, 0)),
        scratch_shapes=[pltpu.VMEM((leading, BS, tok_count), BF16)],
        compiler_params=params(),
        cost_estimate=pl.CostEstimate(
            flops=2 * slots * BS * BS * tok_count, bytes_accessed=2 * slots * BS * BS, transcendentals=0
        ),
        name=name,
    )(index, left, right)


def shards(tokens, up_blocks, up_index, down_blocks, down_index, out_cot):
    rows, width = tokens.shape
    col_devices, row_devices = lax.axis_size("col"), lax.axis_size("row")
    row_blocks = width // BS
    col_blocks = FF // (BS * col_devices)
    tok_count = rows * col_devices
    half = tok_count // 2
    slots = up_index.shape[2]
    up_weight, down_weight = up_blocks[0, 0], down_blocks[0, 0]
    up_place, down_place = up_index[0, 0], down_index[0, 0]
    core = (lax.axis_index("row") % 2).astype(jnp.int32).reshape(1)

    def swap(values, axis, bit):
        count = lax.axis_size(axis)
        return lax.ppermute(values, axis, [(at, at ^ bit) for at in range(count)])

    def cost(blocks):
        return pl.CostEstimate(
            flops=2 * slots * BS * BS * tok_count, bytes_accessed=2 * slots * BS * BS, transcendentals=0
        )

    mine = jnp.concatenate([tokens, out_cot], axis=0)
    parts = [mine] + [swap(mine, "col", bit) for bit in range(1, col_devices)]

    tile_rows = jax.ShapeDtypeStruct((row_blocks, tok_count, BS), BF16)
    tile_cols = jax.ShapeDtypeStruct((col_blocks, tok_count, BS), BF16)
    half_cols = jax.ShapeDtypeStruct((col_blocks, half, BS), BF16)
    acc_rows = pltpu.VMEM((row_blocks + 1, tok_count, BS), F32)
    acc_cols = pltpu.VMEM((col_blocks + 1, tok_count, BS), F32)

    def summed(keep, give):
        total = (keep.astype(F32) + swap(give, "row", 1).astype(F32)).astype(BF16)
        bit = 2
        while bit < row_devices:
            other = swap(total, "row", bit)
            whole = total.astype(F32) + other.astype(F32)
            total = whole.astype(BF16)
            bit *= 2
        return whole

    features, cotangents, pre_keep, pre_give = pl.pallas_call(
        functools.partial(up_kernel, row_blocks, col_blocks),
        out_shape=(tile_rows, tile_rows, half_cols, half_cols),
        in_specs=[SMEM, SMEM] + [VMEM] * (1 + len(parts)),
        out_specs=(VMEM,) * 4,
        scratch_shapes=[acc_cols],
        compiler_params=params(),
        cost_estimate=cost(up_weight),
        name="up",
    )(core, up_place, up_weight, *parts)
    preact = summed(pre_keep, pre_give)

    act_keep, act_give = pl.pallas_call(
        functools.partial(act_kernel, col_blocks, row_blocks),
        out_shape=(half_cols, half_cols),
        in_specs=[SMEM, SMEM, VMEM, VMEM],
        out_specs=(VMEM,) * 2,
        scratch_shapes=[acc_cols],
        compiler_params=params(),
        cost_estimate=cost(down_weight),
        name="act",
    )(core, down_place, down_weight, cotangents)
    act_grad = summed(act_keep, act_give)

    hidden_own = gelu_value(preact).astype(BF16)
    slope = gelu_slope(preact)
    hidden, out_terms = pl.pallas_call(
        functools.partial(down_kernel, col_blocks, row_blocks),
        out_shape=(tile_cols, tile_rows),
        in_specs=[SMEM, SMEM, VMEM, VMEM, VMEM],
        out_specs=(VMEM,) * 2,
        scratch_shapes=[acc_rows],
        compiler_params=params(),
        cost_estimate=cost(down_weight),
        name="down",
    )(core, down_place, down_weight, hidden_own, swap(hidden_own, "row", 1))

    grad_own = (act_grad * slope).astype(BF16)
    chunk = jax.ShapeDtypeStruct((2 * rows, width), BF16)
    pre_grad, *chunks = pl.pallas_call(
        functools.partial(input_kernel, row_blocks, col_blocks),
        out_shape=(tile_cols,) + (chunk,) * col_devices,
        in_specs=[SMEM, SMEM, VMEM, VMEM, VMEM, VMEM],
        out_specs=(VMEM,) * (1 + col_devices),
        scratch_shapes=[acc_rows],
        compiler_params=params(),
        cost_estimate=cost(up_weight),
        name="input",
    )(core, up_place, up_weight, grad_own, swap(grad_own, "row", 1), out_terms)
    total = chunks[0].astype(F32)
    for bit in range(1, col_devices):
        total = total + swap(chunks[bit], "col", bit).astype(F32)
    total = total.astype(BF16)

    up_grad = block_grads("up_grad", up_place, features, pre_grad)
    down_grad = block_grads("down_grad", down_place, hidden, cotangents)
    return total[:rows], total[rows:], up_grad[None, None], down_grad[None, None]


def solution(mesh):
    placed = (
        P("col", "row"),
        P("row", "col", None, None, None),
        P("row", "col", None),
        P("row", "col", None, None, None),
        P("row", "col", None),
        P("col", "row"),
    )
    return jax.shard_map(
        shards,
        mesh=mesh,
        in_specs=placed,
        out_specs=(
            P("col", "row"),
            P("col", "row"),
            P("row", "col", None, None, None),
            P("row", "col", None, None, None),
        ),
        check_vma=False,
    )
```

time: 293 us -> 72.5 us (0.25)
  blocking collectives: 81.8 us -> 0 us
  waiting for transfers between devices: 96.5 us -> 15.8 us
  other arithmetic: 52 us -> 0.63 us
  matrix products: 35.9 us -> 0 us
  Pallas kernels: 0 us -> 22.1 us
  starting transfers between devices: 7.2 us -> 28 us
  between operations: 14.3 us -> 0.79 us
    reduce_scatter x2 -> x0, waiting for transfers between devices: 96.4 us -> none  [the longest x1 64.3 us: shards(): lax.psum_scatter(input_terms.astype(jnp.bfloat16), 'col', scatter_dimensi...]
    all_gather x4 -> x0, blocking collectives: 81.8 us -> none  [the longest x1 32.7 us: shards(): features = lax.all_gather(tokens, 'col', axis=0, tiled=True)]
    scatter-add x4 -> x0, other arithmetic: 47.5 us -> none  [place_blocks(): jnp.zeros((tok_count, width_blocks, BS), jnp.float32).at[:, clipped, :]]
    dot_general x10 -> x0, matrix products: 35.9 us -> none  [the longest x2 14.3 us: backward_tile(): jnp.einsum('ktd,kbd->tkb', picked, blocks, preferred_element_type=jnp.flo...]
    ppermute x0 -> x20, starting transfers between devices: none -> 28 us  [swap(): return lax.ppermute(values, axis, [(at, at ^ bit) for at in range(count)])]
    pallas_call x0 -> x6, Pallas kernels: none -> 22.1 us  [the longest x2 10.4 us: block_grads(): pl.pallas_call(functools.partial(grad_kernel, leading, trailing, step), g...]
    ppermute x0 -> x20, waiting for transfers between devices: none -> 15.8 us  [swap(): return lax.ppermute(values, axis, [(at, at ^ bit) for at in range(count)])]
    all_to_all x2 -> x0, starting transfers between devices: 6.93 us -> none  [the longest x1 3.47 us: shards(): lax.all_to_all(act_terms.astype(jnp.bfloat16).reshape(row_devices, share_...]
  transfers between devices with their start and end apart: 4 -> 20, of which waited for: 2 -> 7; matrix products, arithmetic and copies ran while one was open for 17% -> 0% of each run, Pallas kernels for 0% -> 22%
where the time goes in v1:
time: 72.5 us; the launch traced here: 72.2 us
  starting transfers between devices  28 us (39%)
  Pallas kernels  22.1 us (30%)
  waiting for transfers between devices  15.8 us (22%)
  local copies, waits for them, and re-layouts  4.87 us (7%)
  between operations  0.79 us (1%)
    ppermute x20, starting transfers between devices, swap(): return lax.ppermute(values, axis, [(at, at ^ bit) for at in range(count)])  28 us
    ppermute x20, waiting for transfers between devices, swap(): return lax.ppermute(values, axis, [(at, at ^ bit) for at in range(count)])  15.8 us
    pallas_call x2, Pallas kernels, block_grads(): pl.pallas_call(functools.partial(grad_kernel, leading, trailing, step), g...  10.4 us
    pallas_call x1, Pallas kernels, shards(): pl.pallas_call(functools.partial(input_kernel, row_blocks, col_blocks), o...  3.64 us
    pallas_call x1, Pallas kernels, shards(): pl.pallas_call(functools.partial(act_kernel, col_blocks, row_blocks), out...  3.57 us
    unnamed x13, local copies, waits for them, and re-layouts  3.48 us
    pallas_call x1, Pallas kernels, shards(): pl.pallas_call(functools.partial(up_kernel, row_blocks, col_blocks), out_...  2.32 us
    pallas_call x1, Pallas kernels, shards(): pl.pallas_call(functools.partial(down_kernel, col_blocks, row_blocks), ou...  2.23 us
  transfers between devices with their start and end apart: 20, of which 7 were waited for; matrix products, arithmetic and copies ran while one was open for 0% of the time, Pallas kernels for 22%

profile of v1, /device:TPU:0, one launch (start us, length us, event | category | flops | bytes accessed | tf_op | source)
XLA Modules:
  0.0 72.2 jit_solution(15256522328996523653)
XLA Ops:
  0.6 0.8 %constant_dynamic-update-slice_fusion.1 = bf16[16,2048]{1,0:T(8,128)(2,1)S(1)} fusion(bf16[8,2048]{1,0:T(8,128)(2,1)} %param.6), kind=kLoop, calls=%fused_computation.15 | loop fusion | bytes 65536
  1.4 0.8 %constant_dynamic-update-slice_fusion.refs_3_ = bf16[16,2048]{1,0:T(8,128)(2,1)S(1)} fusion(bf16[16,2048]{1,0:T(8,128)(2,1)S(1)} %constant_dynamic-update-slice_fusion.1, bf16[8,2048]{1,0:T(8,128)(2,1)} %param.11), kind=kLoop, calls=%fused_computation.14 | loop fusion | bytes 65536 | tf_op jit(solution)/shard_map/concatenate | solution.py:184
  2.2 6.0 %collective-permute-start.6 = (bf16[16,2048]{1,0:T(8,128)(2,1)S(1)}, bf16[16,2048]{1,0:T(8,128)(2,1)S(1)}, u32[]{:S(2)}, u32[]{:S(2)}) collective-permute-start(bf16[16,2048]{1,0:T(8,128)(2,1)S(1)} %constant_dynamic-update-slice_fusion.refs_3_), channel_id=1, source_target_pairs={{0,7},{1,6},{2,5},{3,4},{4,3},{5,2},{6,1},{7,0},{8,15},{9,14},{10,... | collective-permute-start | bytes 196616 | tf_op jit(solution)/shard_map/ppermute | solution.py:177
  8.4 0.8 %collective-permute-start.4 = (bf16[16,2048]{1,0:T(8,128)(2,1)S(1)}, bf16[16,2048]{1,0:T(8,128)(2,1)S(1)}, u32[]{:S(2)}, u32[]{:S(2)}) collective-permute-start(bf16[16,2048]{1,0:T(8,128)(2,1)S(1)} %constant_dynamic-update-slice_fusion.refs_3_), channel_id=1, source_target_pairs={{0,5},{1,4},{2,7},{3,6},{4,1},{5,0},{6,3},{7,2},{8,13},{9,12},{10,... | collective-permute-start | bytes 196616 | tf_op jit(solution)/shard_map/ppermute | solution.py:177
  9.1 1.9 %collective-permute-start.3 = (bf16[16,2048]{1,0:T(8,128)(2,1)S(1)}, bf16[16,2048]{1,0:T(8,128)(2,1)S(1)}, u32[]{:S(2)}, u32[]{:S(2)}) collective-permute-start(bf16[16,2048]{1,0:T(8,128)(2,1)S(1)} %constant_dynamic-update-slice_fusion.refs_3_), channel_id=1, source_target_pairs={{0,4},{1,5},{2,6},{3,7},{4,0},{5,1},{6,2},{7,3},{8,12},{9,13},{10,... | collective-permute-start | bytes 196616 | tf_op jit(solution)/shard_map/ppermute | solution.py:177
  11.1 2.4 %collective-permute-start.2 = (bf16[16,2048]{1,0:T(8,128)(2,1)S(1)}, bf16[16,2048]{1,0:T(8,128)(2,1)S(1)}, u32[]{:S(2)}, u32[]{:S(2)}) collective-permute-start(bf16[16,2048]{1,0:T(8,128)(2,1)S(1)} %constant_dynamic-update-slice_fusion.refs_3_), channel_id=1, source_target_pairs={{0,3},{1,2},{2,1},{3,0},{4,7},{5,6},{6,5},{7,4},{8,11},{9,10},{10,... | collective-permute-start | bytes 196616 | tf_op jit(solution)/shard_map/ppermute | solution.py:177
  13.4 0.8 %collective-permute-start.1 = (bf16[16,2048]{1,0:T(8,128)(2,1)S(1)}, bf16[16,2048]{1,0:T(8,128)(2,1)S(1)}, u32[]{:S(2)}, u32[]{:S(2)}) collective-permute-start(bf16[16,2048]{1,0:T(8,128)(2,1)S(1)} %constant_dynamic-update-slice_fusion.refs_3_), channel_id=1, source_target_pairs={{0,2},{1,3},{2,0},{3,1},{4,6},{5,7},{6,4},{7,5},{8,10},{9,11},{10,... | collective-permute-start | bytes 196616 | tf_op jit(solution)/shard_map/ppermute | solution.py:177
  14.4 0.5 collective-permute-start
  14.9 2.8 %collective-permute-done.4.refs_8_ = bf16[16,2048]{1,0:T(8,128)(2,1)S(1)} collective-permute-done((bf16[16,2048]{1,0:T(8,128)(2,1)S(1)}, bf16[16,2048]{1,0:T(8,128)(2,1)S(1)}, u32[]{:S(2)}, u32[]{:S(2)}) %collective-permute-start.4) | collective-permute-done | bytes 65568 | tf_op jit(solution)/shard_map/ppermute | solution.py:177
  17.7 1.7 %collective-permute-done.3.refs_7_ = bf16[16,2048]{1,0:T(8,128)(2,1)S(1)} collective-permute-done((bf16[16,2048]{1,0:T(8,128)(2,1)S(1)}, bf16[16,2048]{1,0:T(8,128)(2,1)S(1)}, u32[]{:S(2)}, u32[]{:S(2)}) %collective-permute-start.3) | collective-permute-done | bytes 65568 | tf_op jit(solution)/shard_map/ppermute | solution.py:177
  19.8 2.0 %copy-done = bf16[1,1,112,128,128]{4,3,2,1,0:T(8,128)(2,1)S(1)} copy-done((bf16[1,1,112,128,128]{4,3,2,1,0:T(8,128)(2,1)S(1)}, bf16[1,1,112,128,128]{4,3,2,1,0:T(8,128)(2,1)}, u32[]{:S(2)}) %copy-start) | copy-done | bytes 3670040
  21.8 0.7 copy-done.4
  22.5 2.3 %up.1 = (bf16[16,64,128]{2,1,0:T(8,128)(2,1)S(1)}, bf16[16,64,128]{2,1,0:T(8,128)(2,1)S(1)}, bf16[28,32,128]{2,1,0:T(8,128)(2,1)S(1)}, bf16[28,32,128]{2,1,0:T(8,128)(2,1)S(1)}) custom-call(s32[1]{0:T(128)} %bitcast.refs_0_.core_ref, s32[112]{0:T(128)S(1)} %bitcast.14, bf16[112,128,128]{2,1,0:T(8,128)(2,1)S(1)} %bitcast.7, ...), custom_call_target="tpu_custom_call" | custom-call | flops 234881024 | bytes 3670016 | tf_op jit(solution)/shard_map/up/pallas_call | solution.py:203
  24.9 3.6 %act.1 = (bf16[28,32,128]{2,1,0:T(8,128)(2,1)S(1)}, bf16[28,32,128]{2,1,0:T(8,128)(2,1)S(1)}) custom-call(s32[1]{0:T(128)} %bitcast.refs_0_.core_ref, s32[112]{0:T(128)S(1)} %bitcast.11, bf16[112,128,128]{2,1,0:T(8,128)(2,1)S(1)} %bitcast.9, bf16[16,64,128]{2,1,0:T(8,128)(2,1)S(1)} %get-tuple-element.21.cot_ref.right_ref), custom_call_target="tpu_custom_call" | custom-call | flops 234881024 | bytes 3670016 | tf_op jit(solution)/shard_map/act/pallas_call | solution.py:215
  28.5 0.5 collective-permute-start.7
  29.1 1.6 %collective-permute-start.10 = (bf16[28,32,128]{2,1,0:T(8,128)(2,1)S(1)}, bf16[28,32,128]{2,1,0:T(8,128)(2,1)S(1)}, u32[]{:S(2)}, u32[]{:S(2)}) collective-permute-start(bf16[28,32,128]{2,1,0:T(8,128)(2,1)S(1)} %add_convert_fusion), channel_id=1, source_target_pairs={{0,16},{8,24},{16,0},{24,8},{1,17},{9,25},{17,1},{25,9},{2,18},{10... | collective-permute-start | bytes 688136 | tf_op jit(solution)/shard_map/ppermute | solution.py:177
  30.8 1.1 %collective-permute-start.8 = (bf16[28,32,128]{2,1,0:T(8,128)(2,1)S(1)}, bf16[28,32,128]{2,1,0:T(8,128)(2,1)S(1)}, u32[]{:S(2)}, u32[]{:S(2)}) collective-permute-start(bf16[28,32,128]{2,1,0:T(8,128)(2,1)S(1)} %add_convert_fusion.1), channel_id=1, source_target_pairs={{0,16},{8,24},{16,0},{24,8},{1,17},{9,25},{17,1},{25,9},{2,18},{10... | collective-permute-start | bytes 688136 | tf_op jit(solution)/shard_map/ppermute | solution.py:177
  31.8 5.8 %collective-permute-done.10 = bf16[28,32,128]{2,1,0:T(8,128)(2,1)S(1)} collective-permute-done((bf16[28,32,128]{2,1,0:T(8,128)(2,1)S(1)}, bf16[28,32,128]{2,1,0:T(8,128)(2,1)S(1)}, u32[]{:S(2)}, u32[]{:S(2)}) %collective-permute-start.10) | collective-permute-done | bytes 229408 | tf_op jit(solution)/shard_map/ppermute | solution.py:177
  37.6 4.0 %collective-permute-done.8 = bf16[28,32,128]{2,1,0:T(8,128)(2,1)S(1)} collective-permute-done((bf16[28,32,128]{2,1,0:T(8,128)(2,1)S(1)}, bf16[28,32,128]{2,1,0:T(8,128)(2,1)S(1)}, u32[]{:S(2)}, u32[]{:S(2)}) %collective-permute-start.8) | collective-permute-done | bytes 229408 | tf_op jit(solution)/shard_map/ppermute | solution.py:177
  42.1 0.5 collective-permute-start.11
  42.6 1.0 %collective-permute-done.12.other_ref = bf16[28,32,128]{2,1,0:T(8,128)(2,1)S(1)} collective-permute-done((bf16[28,32,128]{2,1,0:T(8,128)(2,1)S(1)}, bf16[28,32,128]{2,1,0:T(8,128)(2,1)S(1)}, u32[]{:S(2)}, u32[]{:S(2)}) %collective-permute-start.12) | collective-permute-done | bytes 229408 | tf_op jit(solution)/shard_map/ppermute | solution.py:177
  43.6 2.2 %down.1 = (bf16[28,64,128]{2,1,0:T(8,128)(2,1)S(1)}, bf16[16,64,128]{2,1,0:T(8,128)(2,1)S(1)}) custom-call(s32[1]{0:T(128)} %bitcast.refs_0_.core_ref, s32[112]{0:T(128)S(1)} %bitcast.12, bf16[112,128,128]{2,1,0:T(8,128)(2,1)S(1)} %bitcast.10, bf16[28,32,128]{2,1,0:T(8,128)(2,1)S(1)} %get-tuple-element.38.own_ref, ...), custom_call_target="tpu_custom_call" | custom-call | flops 234881024 | bytes 3670016 | tf_op jit(solution)/shard_map/down/pallas_call | solution.py:229
  45.9 3.6 %input.1 = (bf16[28,64,128]{2,1,0:T(8,128)(2,1)S(1)}, bf16[16,2048]{1,0:T(8,128)(2,1)S(1)}, bf16[16,2048]{1,0:T(8,128)(2,1)S(1)}, bf16[16,2048]{1,0:T(8,128)(2,1...) custom-call(s32[1]{0:T(128)} %bitcast.refs_0_.core_ref, ...), custom_call_target="tpu_custom_call" | custom-call | flops 234881024 | bytes 3670016 | tf_op jit(solution)/shard_map/input/pallas_call | solution.py:242
  49.5 0.7 %collective-permute-start.13 = (bf16[16,2048]{1,0:T(8,128)(2,1)S(1)}, bf16[16,2048]{1,0:T(8,128)(2,1)S(1)}, u32[]{:S(2)}, u32[]{:S(2)}) collective-permute-start(bf16[16,2048]{1,0:T(8,128)(2,1)S(1)} %get-tuple-element.28), channel_id=1, source_target_pairs={{0,1},{1,0},{2,3},{3,2},{4,5},{5,4},{6,7},{7,6},{8,9},{9,8},{10,11... | collective-permute-start | bytes 196616 | tf_op jit(solution)/shard_map/ppermute | solution.py:177
  50.3 1.1 %collective-permute-start.14 = (bf16[16,2048]{1,0:T(8,128)(2,1)S(1)}, bf16[16,2048]{1,0:T(8,128)(2,1)S(1)}, u32[]{:S(2)}, u32[]{:S(2)}) collective-permute-start(bf16[16,2048]{1,0:T(8,128)(2,1)S(1)} %get-tuple-element.29), channel_id=1, source_target_pairs={{0,2},{1,3},{2,0},{3,1},{4,6},{5,7},{6,4},{7,5},{8,10},{9,11},{10,... | collective-permute-start | bytes 196616 | tf_op jit(solution)/shard_map/ppermute | solution.py:177
  51.3 1.8 %collective-permute-start.15 = (bf16[16,2048]{1,0:T(8,128)(2,1)S(1)}, bf16[16,2048]{1,0:T(8,128)(2,1)S(1)}, u32[]{:S(2)}, u32[]{:S(2)}) collective-permute-start(bf16[16,2048]{1,0:T(8,128)(2,1)S(1)} %get-tuple-element.30), channel_id=1, source_target_pairs={{0,3},{1,2},{2,1},{3,0},{4,7},{5,6},{6,5},{7,4},{8,11},{9,10},{10,... | collective-permute-start | bytes 196616 | tf_op jit(solution)/shard_map/ppermute | solution.py:177
  53.1 3.3 %collective-permute-start.16 = (bf16[16,2048]{1,0:T(8,128)(2,1)S(1)}, bf16[16,2048]{1,0:T(8,128)(2,1)S(1)}, u32[]{:S(2)}, u32[]{:S(2)}) collective-permute-start(bf16[16,2048]{1,0:T(8,128)(2,1)S(1)} %get-tuple-element.31), channel_id=1, source_target_pairs={{0,4},{1,5},{2,6},{3,7},{4,0},{5,1},{6,2},{7,3},{8,12},{9,13},{10,... | collective-permute-start | bytes 196616 | tf_op jit(solution)/shard_map/ppermute | solution.py:177
  56.4 3.6 %collective-permute-start.18 = (bf16[16,2048]{1,0:T(8,128)(2,1)S(1)}, bf16[16,2048]{1,0:T(8,128)(2,1)S(1)}, u32[]{:S(2)}, u32[]{:S(2)}) collective-permute-start(bf16[16,2048]{1,0:T(8,128)(2,1)S(1)} %get-tuple-element.33), channel_id=1, source_target_pairs={{0,6},{1,7},{2,4},{3,5},{4,2},{5,3},{6,0},{7,1},{8,14},{9,15},{10,... | collective-permute-start | bytes 196616 | tf_op jit(solution)/shard_map/ppermute | solution.py:177
  59.9 1.1 %collective-permute-start.19 = (bf16[16,2048]{1,0:T(8,128)(2,1)S(1)}, bf16[16,2048]{1,0:T(8,128)(2,1)S(1)}, u32[]{:S(2)}, u32[]{:S(2)}) collective-permute-start(bf16[16,2048]{1,0:T(8,128)(2,1)S(1)} %get-tuple-element.34), channel_id=1, source_target_pairs={{0,7},{1,6},{2,5},{3,4},{4,3},{5,2},{6,1},{7,0},{8,15},{9,14},{10,... | collective-permute-start | bytes 196616 | tf_op jit(solution)/shard_map/ppermute | solution.py:177
  61.1 5.2 %down_grad.1 = bf16[112,128,128]{2,1,0:T(8,128)(2,1)} custom-call(s32[112]{0:T(128)S(1)} %bitcast.13, bf16[28,64,128]{2,1,0:T(8,128)(2,1)S(1)} %get-tuple-element.37.left_ref, bf16[16,64,128]{2,1,0:T(8,128)(2,1)S(1)} %get-tuple-element.21.cot_ref.right_ref), custom_call_target="tpu_custom_call" | custom-call | flops 234881024 | bytes 3670016 | tf_op jit(solution)/shard_map/down_grad/pallas_call | solution.py:148
  66.3 5.2 %up_grad.1 = bf16[112,128,128]{2,1,0:T(8,128)(2,1)} custom-call(s32[112]{0:T(128)S(1)} %bitcast.16, bf16[16,64,128]{2,1,0:T(8,128)(2,1)S(1)} %get-tuple-element.35.left_ref, bf16[28,64,128]{2,1,0:T(8,128)(2,1)S(1)} %get-tuple-element.36.right_ref), custom_call_target="tpu_custom_call" | custom-call | flops 234881024 | bytes 3670016 | tf_op jit(solution)/shard_map/up_grad/pallas_call | solution.py:148
  71.6 0.6 fusion.7
  (33 shorter events, 1.6 us)
Async XLA Ops:
  0.6 24.3 %copy-start.3 = (s32[1,1,112]{2,1,0:T(1,128)S(1)}, s32[1,1,112]{2,1,0:T(1,128)}, u32[]{:S(2)}) copy-start(s32[1,1,112]{2,1,0:T(1,128)} %param.10) | copy-start | bytes 1348
  2.2 11.3 %collective-permute-start.6 = (bf16[16,2048]{1,0:T(8,128)(2,1)S(1)}, bf16[16,2048]{1,0:T(8,128)(2,1)S(1)}, u32[]{:S(2)}, u32[]{:S(2)}) collective-permute-start(bf16[16,2048]{1,0:T(8,128)(2,1)S(1)} %constant_dynamic-update-slice_fusion.refs_3_), channel_id=1, source_target_pairs={{0,7},{1,6},{2,5},{3,4},{4,3},{5,2},{6,1},{7,0},{8,15},{9,14},{10,... | collective-permute-start | bytes 196616 | tf_op jit(solution)/shard_map/ppermute | solution.py:177
  8.1 6.3 %collective-permute-start.5 = (bf16[16,2048]{1,0:T(8,128)(2,1)S(1)}, bf16[16,2048]{1,0:T(8,128)(2,1)S(1)}, u32[]{:S(2)}, u32[]{:S(2)}) collective-permute-start(bf16[16,2048]{1,0:T(8,128)(2,1)S(1)} %constant_dynamic-update-slice_fusion.refs_3_), channel_id=1, source_target_pairs={{0,6},{1,7},{2,4},{3,5},{4,2},{5,3},{6,0},{7,1},{8,14},{9,15},{10,... | collective-permute-start | bytes 196616 | tf_op jit(solution)/shard_map/ppermute | solution.py:177
  8.4 9.3 %collective-permute-start.4 = (bf16[16,2048]{1,0:T(8,128)(2,1)S(1)}, bf16[16,2048]{1,0:T(8,128)(2,1)S(1)}, u32[]{:S(2)}, u32[]{:S(2)}) collective-permute-start(bf16[16,2048]{1,0:T(8,128)(2,1)S(1)} %constant_dynamic-update-slice_fusion.refs_3_), channel_id=1, source_target_pairs={{0,5},{1,4},{2,7},{3,6},{4,1},{5,0},{6,3},{7,2},{8,13},{9,12},{10,... | collective-permute-start | bytes 196616 | tf_op jit(solution)/shard_map/ppermute | solution.py:177
  9.1 10.2 %collective-permute-start.3 = (bf16[16,2048]{1,0:T(8,128)(2,1)S(1)}, bf16[16,2048]{1,0:T(8,128)(2,1)S(1)}, u32[]{:S(2)}, u32[]{:S(2)}) collective-permute-start(bf16[16,2048]{1,0:T(8,128)(2,1)S(1)} %constant_dynamic-update-slice_fusion.refs_3_), channel_id=1, source_target_pairs={{0,4},{1,5},{2,6},{3,7},{4,0},{5,1},{6,2},{7,3},{8,12},{9,13},{10,... | collective-permute-start | bytes 196616 | tf_op jit(solution)/shard_map/ppermute | solution.py:177
  11.1 8.3 %collective-permute-start.2 = (bf16[16,2048]{1,0:T(8,128)(2,1)S(1)}, bf16[16,2048]{1,0:T(8,128)(2,1)S(1)}, u32[]{:S(2)}, u32[]{:S(2)}) collective-permute-start(bf16[16,2048]{1,0:T(8,128)(2,1)S(1)} %constant_dynamic-update-slice_fusion.refs_3_), channel_id=1, source_target_pairs={{0,3},{1,2},{2,1},{3,0},{4,7},{5,6},{6,5},{7,4},{8,11},{9,10},{10,... | collective-permute-start | bytes 196616 | tf_op jit(solution)/shard_map/ppermute | solution.py:177
  13.4 6.3 %collective-permute-start.1 = (bf16[16,2048]{1,0:T(8,128)(2,1)S(1)}, bf16[16,2048]{1,0:T(8,128)(2,1)S(1)}, u32[]{:S(2)}, u32[]{:S(2)}) collective-permute-start(bf16[16,2048]{1,0:T(8,128)(2,1)S(1)} %constant_dynamic-update-slice_fusion.refs_3_), channel_id=1, source_target_pairs={{0,2},{1,3},{2,0},{3,1},{4,6},{5,7},{6,4},{7,5},{8,10},{9,11},{10,... | collective-permute-start | bytes 196616 | tf_op jit(solution)/shard_map/ppermute | solution.py:177
  14.4 5.4 %collective-permute-start = (bf16[16,2048]{1,0:T(8,128)(2,1)S(1)}, bf16[16,2048]{1,0:T(8,128)(2,1)S(1)}, u32[]{:S(2)}, u32[]{:S(2)}) collective-permute-start(bf16[16,2048]{1,0:T(8,128)(2,1)S(1)} %constant_dynamic-update-slice_fusion.refs_3_), channel_id=1, source_target_pairs={{0,1},{1,0},{2,3},{3,2},{4,5},{5,4},{6,7},{7,6},{8,9},{9,8},{10,11... | collective-permute-start | bytes 196616 | tf_op jit(solution)/shard_map/ppermute | solution.py:177
  19.8 2.0 %copy-start = (bf16[1,1,112,128,128]{4,3,2,1,0:T(8,128)(2,1)S(1)}, bf16[1,1,112,128,128]{4,3,2,1,0:T(8,128)(2,1)}, u32[]{:S(2)}) copy-start(bf16[1,1,112,128,128]{4,3,2,1,0:T(8,128)(2,1)} %param.7) | copy-start | bytes 11010052
  21.8 0.7 copy-start.4
  22.5 2.4 %copy-start.2 = (bf16[1,1,112,128,128]{4,3,2,1,0:T(8,128)(2,1)S(1)}, bf16[1,1,112,128,128]{4,3,2,1,0:T(8,128)(2,1)}, u32[]{:S(2)}) copy-start(bf16[1,1,112,128,128]{4,3,2,1,0:T(8,128)(2,1)} %param.9) | copy-start | bytes 11010052
  24.8 4.2 %collective-permute-start.9 = (bf16[28,32,128]{2,1,0:T(8,128)(2,1)S(1)}, bf16[28,32,128]{2,1,0:T(8,128)(2,1)S(1)}, u32[]{:S(2)}, u32[]{:S(2)}) collective-permute-start(bf16[28,32,128]{2,1,0:T(8,128)(2,1)S(1)} %get-tuple-element.25), channel_id=1, source_target_pairs={{0,8},{8,0},{16,24},{24,16},{1,9},{9,1},{17,25},{25,17},{2,10},{10... | collective-permute-start | bytes 688136 | tf_op jit(solution)/shard_map/ppermute | solution.py:177
  28.5 17.4 %copy-start.1 = (bf16[1,1,112,128,128]{4,3,2,1,0:T(8,128)(2,1)S(1)}, bf16[1,1,112,128,128]{4,3,2,1,0:T(8,128)(2,1)}, u32[]{:S(2)}) copy-start(bf16[1,1,112,128,128]{4,3,2,1,0:T(8,128)(2,1)} %param.7) | copy-start | bytes 11010052
  28.5 17.4 %copy-start.5 = (s32[1,1,112]{2,1,0:T(1,128)S(1)}, s32[1,1,112]{2,1,0:T(1,128)}, u32[]{:S(2)}) copy-start(s32[1,1,112]{2,1,0:T(1,128)} %param.8) | copy-start | bytes 1348
  28.5 2.2 %collective-permute-start.7 = (bf16[28,32,128]{2,1,0:T(8,128)(2,1)S(1)}, bf16[28,32,128]{2,1,0:T(8,128)(2,1)S(1)}, u32[]{:S(2)}, u32[]{:S(2)}) collective-permute-start(bf16[28,32,128]{2,1,0:T(8,128)(2,1)S(1)} %get-tuple-element.23), channel_id=1, source_target_pairs={{0,8},{8,0},{16,24},{24,16},{1,9},{9,1},{17,25},{25,17},{2,10},{10... | collective-permute-start | bytes 688136 | tf_op jit(solution)/shard_map/ppermute | solution.py:177
  29.1 8.5 %collective-permute-start.10 = (bf16[28,32,128]{2,1,0:T(8,128)(2,1)S(1)}, bf16[28,32,128]{2,1,0:T(8,128)(2,1)S(1)}, u32[]{:S(2)}, u32[]{:S(2)}) collective-permute-start(bf16[28,32,128]{2,1,0:T(8,128)(2,1)S(1)} %add_convert_fusion), channel_id=1, source_target_pairs={{0,16},{8,24},{16,0},{24,8},{1,17},{9,25},{17,1},{25,9},{2,18},{10... | collective-permute-start | bytes 688136 | tf_op jit(solution)/shard_map/ppermute | solution.py:177
  30.8 10.9 %collective-permute-start.8 = (bf16[28,32,128]{2,1,0:T(8,128)(2,1)S(1)}, bf16[28,32,128]{2,1,0:T(8,128)(2,1)S(1)}, u32[]{:S(2)}, u32[]{:S(2)}) collective-permute-start(bf16[28,32,128]{2,1,0:T(8,128)(2,1)S(1)} %add_convert_fusion.1), channel_id=1, source_target_pairs={{0,16},{8,24},{16,0},{24,8},{1,17},{9,25},{17,1},{25,9},{2,18},{10... | collective-permute-start | bytes 688136 | tf_op jit(solution)/shard_map/ppermute | solution.py:177
  42.1 1.6 %collective-permute-start.12 = (bf16[28,32,128]{2,1,0:T(8,128)(2,1)S(1)}, bf16[28,32,128]{2,1,0:T(8,128)(2,1)S(1)}, u32[]{:S(2)}, u32[]{:S(2)}) collective-permute-start(bf16[28,32,128]{2,1,0:T(8,128)(2,1)S(1)} %get-tuple-element.38.own_ref), channel_id=1, source_target_pairs={{0,8},{8,0},{16,24},{24,16},{1,9},{9,1},{17,25},{25,17},{2,10},{10... | collective-permute-start | bytes 688136 | tf_op jit(solution)/shard_map/ppermute | solution.py:177
  42.1 3.7 %collective-permute-start.11 = (bf16[28,32,128]{2,1,0:T(8,128)(2,1)S(1)}, bf16[28,32,128]{2,1,0:T(8,128)(2,1)S(1)}, u32[]{:S(2)}, u32[]{:S(2)}) collective-permute-start(bf16[28,32,128]{2,1,0:T(8,128)(2,1)S(1)} %get-tuple-element.39.own_ref), channel_id=1, source_target_pairs={{0,8},{8,0},{16,24},{24,16},{1,9},{9,1},{17,25},{25,17},{2,10},{10... | collective-permute-start | bytes 688136 | tf_op jit(solution)/shard_map/ppermute | solution.py:177
  49.5 6.8 %collective-permute-start.13 = (bf16[16,2048]{1,0:T(8,128)(2,1)S(1)}, bf16[16,2048]{1,0:T(8,128)(2,1)S(1)}, u32[]{:S(2)}, u32[]{:S(2)}) collective-permute-start(bf16[16,2048]{1,0:T(8,128)(2,1)S(1)} %get-tuple-element.28), channel_id=1, source_target_pairs={{0,1},{1,0},{2,3},{3,2},{4,5},{5,4},{6,7},{7,6},{8,9},{9,8},{10,11... | collective-permute-start | bytes 196616 | tf_op jit(solution)/shard_map/ppermute | solution.py:177
  50.3 9.7 %collective-permute-start.14 = (bf16[16,2048]{1,0:T(8,128)(2,1)S(1)}, bf16[16,2048]{1,0:T(8,128)(2,1)S(1)}, u32[]{:S(2)}, u32[]{:S(2)}) collective-permute-start(bf16[16,2048]{1,0:T(8,128)(2,1)S(1)} %get-tuple-element.29), channel_id=1, source_target_pairs={{0,2},{1,3},{2,0},{3,1},{4,6},{5,7},{6,4},{7,5},{8,10},{9,11},{10,... | collective-permute-start | bytes 196616 | tf_op jit(solution)/shard_map/ppermute | solution.py:177
  51.3 20.2 %collective-permute-start.15 = (bf16[16,2048]{1,0:T(8,128)(2,1)S(1)}, bf16[16,2048]{1,0:T(8,128)(2,1)S(1)}, u32[]{:S(2)}, u32[]{:S(2)}) collective-permute-start(bf16[16,2048]{1,0:T(8,128)(2,1)S(1)} %get-tuple-element.30), channel_id=1, source_target_pairs={{0,3},{1,2},{2,1},{3,0},{4,7},{5,6},{6,5},{7,4},{8,11},{9,10},{10,... | collective-permute-start | bytes 196616 | tf_op jit(solution)/shard_map/ppermute | solution.py:177
  53.1 18.4 %collective-permute-start.16 = (bf16[16,2048]{1,0:T(8,128)(2,1)S(1)}, bf16[16,2048]{1,0:T(8,128)(2,1)S(1)}, u32[]{:S(2)}, u32[]{:S(2)}) collective-permute-start(bf16[16,2048]{1,0:T(8,128)(2,1)S(1)} %get-tuple-element.31), channel_id=1, source_target_pairs={{0,4},{1,5},{2,6},{3,7},{4,0},{5,1},{6,2},{7,3},{8,12},{9,13},{10,... | collective-permute-start | bytes 196616 | tf_op jit(solution)/shard_map/ppermute | solution.py:177
  56.4 15.1 %collective-permute-start.17 = (bf16[16,2048]{1,0:T(8,128)(2,1)S(1)}, bf16[16,2048]{1,0:T(8,128)(2,1)S(1)}, u32[]{:S(2)}, u32[]{:S(2)}) collective-permute-start(bf16[16,2048]{1,0:T(8,128)(2,1)S(1)} %get-tuple-element.32), channel_id=1, source_target_pairs={{0,5},{1,4},{2,7},{3,6},{4,1},{5,0},{6,3},{7,2},{8,13},{9,12},{10,... | collective-permute-start | bytes 196616 | tf_op jit(solution)/shard_map/ppermute | solution.py:177
  56.4 15.1 %collective-permute-start.18 = (bf16[16,2048]{1,0:T(8,128)(2,1)S(1)}, bf16[16,2048]{1,0:T(8,128)(2,1)S(1)}, u32[]{:S(2)}, u32[]{:S(2)}) collective-permute-start(bf16[16,2048]{1,0:T(8,128)(2,1)S(1)} %get-tuple-element.33), channel_id=1, source_target_pairs={{0,6},{1,7},{2,4},{3,5},{4,2},{5,3},{6,0},{7,1},{8,14},{9,15},{10,... | collective-permute-start | bytes 196616 | tf_op jit(solution)/shard_map/ppermute | solution.py:177
  59.9 11.6 %collective-permute-start.19 = (bf16[16,2048]{1,0:T(8,128)(2,1)S(1)}, bf16[16,2048]{1,0:T(8,128)(2,1)S(1)}, u32[]{:S(2)}, u32[]{:S(2)}) collective-permute-start(bf16[16,2048]{1,0:T(8,128)(2,1)S(1)} %get-tuple-element.34), channel_id=1, source_target_pairs={{0,7},{1,6},{2,5},{3,4},{4,3},{5,2},{6,1},{7,0},{8,15},{9,14},{10,... | collective-permute-start | bytes 196616 | tf_op jit(solution)/shard_map/ppermute | solution.py:177

commit v2 on v0

v2 whole, which is shorter than its diff:
```python
import functools

import jax
import jax.numpy as jnp
from jax import lax
from jax.experimental import pallas as pl
from jax.experimental.pallas import tpu as pltpu
from jax.sharding import PartitionSpec as P

FF = 28672
BS = 128
COEF = 0.7978845608
CUBIC = 0.044715
F32 = jnp.float32
BF16 = jnp.bfloat16
VMEM = pl.BlockSpec(memory_space=pltpu.VMEM)
SMEM = pl.BlockSpec(memory_space=pltpu.SMEM)
HBM = pl.BlockSpec(memory_space=pltpu.HBM)


def gelu_value(values):
    inner = COEF * (values + CUBIC * values * values * values)
    return 0.5 * values * (1.0 + jnp.tanh(inner))


def gelu_slope(values):
    tangent = jnp.tanh(COEF * (values + CUBIC * values * values * values))
    return 0.5 * (1.0 + tangent) + 0.5 * values * (1.0 - tangent * tangent) * COEF * (
        1.0 + 3.0 * CUBIC * values * values
    )


def params(megabytes=24):
    return pltpu.CompilerParams(vmem_limit_bytes=megabytes << 20)


def divisor(count, most):
    return max(step for step in range(1, most + 1) if count % step == 0)


class Stream:
    def __init__(self, index_hbm, blocks_hbm, index_ref, blocks_ref, index_sem, sems):
        self.index, self.blocks = index_ref, blocks_ref
        self.index_copy = pltpu.make_async_copy(index_hbm, index_ref, index_sem)
        self.step = blocks_ref.shape[0] // sems.shape[0]
        self.copies = lambda at: pltpu.make_async_copy(
            blocks_hbm.at[pl.ds(at * self.step, self.step)],
            blocks_ref.at[pl.ds(at * self.step, self.step)],
            sems.at[at],
        )
        self.index_copy.start()
        for at in range(sems.shape[0]):
            self.copies(at).start()

    @staticmethod
    def scratch(slots, most):
        return [
            pltpu.SMEM((slots,), jnp.int32),
            pltpu.VMEM((slots, BS, BS), BF16),
            pltpu.SemaphoreType.DMA,
            pltpu.SemaphoreType.DMA((slots // divisor(slots, most),)),
        ]

    def prepare(self):
        self.index_copy.wait()

    def group(self, at):
        self.copies(at).wait()


class Held:
    def __init__(self, index_ref, blocks_ref, most):
        self.index, self.blocks = index_ref, blocks_ref
        self.step = divisor(blocks_ref.shape[0], most)

    def prepare(self):
        pass

    def group(self, at):
        pass


def accumulate(source, leading, trailing, operand_ref, acc):
    acc[...] = jnp.zeros_like(acc)
    source.prepare()

    def group(at, carry):
        source.group(at)
        products = []
        for inner in range(source.step):
            slot = at * source.step + inner
            place = source.index[slot]
            lead = jnp.minimum(place // trailing, leading - 1)
            trail = jnp.where(place < leading * trailing, place % trailing, trailing)
            products.append(
                (trail, jnp.dot(operand_ref[lead], source.blocks[slot], preferred_element_type=F32))
            )
        for trail, product in products:
            acc[trail] += product
        return carry

    lax.fori_loop(0, source.blocks.shape[0] // source.step, group, 0)


def accumulate_turned(source, leading, trailing, operand_ref, turned, acc):
    for at in range(trailing):
        turned[at] = operand_ref[at].T
    acc[...] = jnp.zeros_like(acc)
    source.prepare()

    def group(at, carry):
        source.group(at)
        products = []
        for inner in range(source.step):
            slot = at * source.step + inner
            place = source.index[slot]
            named = place < leading * trailing
            lead = jnp.where(named, place // trailing, leading)
            products.append(
                (lead, jnp.dot(source.blocks[slot], turned[place % trailing], preferred_element_type=F32))
            )
        for lead, product in products:
            acc[lead] += product
        return carry

    lax.fori_loop(0, source.blocks.shape[0] // source.step, group, 0)


def split_halves(core, read, targets, keep_ref, give_ref):
    half = keep_ref.shape[1]
    for at in range(targets):
        low, high = read(at, 0), read(at, half)
        keep_ref[at] = jnp.where(core == 0, low, high).astype(BF16)
        give_ref[at] = jnp.where(core == 0, high, low).astype(BF16)


def position(axis):
    return lax.axis_index(axis).astype(jnp.int32)


def core():
    return position("row") % 2


def pack_kernel(tokens_ref, cot_ref, mine_ref, held, sems):
    copies = [
        pltpu.make_async_copy(source, held.at[at], sems.at[at])
        for at, source in enumerate((tokens_ref, cot_ref))
    ]
    for copy in copies:
        copy.start()
    for copy in copies:
        copy.wait()
    mine_ref[...] = jnp.concatenate([held[0].astype(F32), held[1].astype(F32)]).astype(BF16)


def up_kernel(leading, trailing, index_hbm, blocks_hbm, *refs):
    parts = refs[:-9]
    tokens_ref, cot_ref, keep_ref, give_ref, acc = refs[-9:-4]
    source = Stream(index_hbm, blocks_hbm, *refs[-4:])
    rows = parts[0].shape[0] // 2
    for pair in range(len(parts) // 2):
        here = pl.ds(pair * 2 * rows, 2 * rows)
        for at in range(leading):
            lanes = pl.ds(at * BS, BS)
            first = parts[2 * pair][:, lanes].astype(F32)
            second = parts[2 * pair + 1][:, lanes].astype(F32)
            tokens_ref[at, here, :] = jnp.concatenate([first[:rows], second[:rows]]).astype(BF16)
            cot_ref[at, here, :] = jnp.concatenate([first[rows:], second[rows:]]).astype(BF16)
    accumulate(source, leading, trailing, tokens_ref, acc)
    half = keep_ref.shape[1]
    split_halves(core(), lambda at, low: acc[at, low : low + half, :], trailing, keep_ref, give_ref)


def act_kernel(
    leading, trailing, index_ref, blocks_ref, cot_ref, after_ref, keep_ref, give_ref, turned, acc
):
    accumulate_turned(Held(index_ref, blocks_ref, 56), leading, trailing, cot_ref, turned, acc)
    half = keep_ref.shape[1]

    def read(at, low):
        return acc[at].T[low : low + half]

    split_halves(core(), read, leading, keep_ref, give_ref)


def join_halves(core, own_ref, other_ref, whole_ref):
    half = own_ref.shape[1]
    for at in range(own_ref.shape[0]):
        own, other = own_ref[at], other_ref[at]
        whole_ref[at, :half, :] = jnp.where(core == 0, own, other)
        whole_ref[at, half:, :] = jnp.where(core == 0, other, own)


def gelu_kernel(own_ref, other_ref, hidden_ref, slope_ref):
    for at in range(own_ref.shape[0]):
        preact = own_ref[at].astype(F32) + other_ref[at].astype(F32)
        hidden_ref[at] = gelu_value(preact).astype(BF16)
        slope_ref[at] = gelu_slope(preact)


def slope_kernel(own_ref, other_ref, slope_ref, grad_ref):
    for at in range(own_ref.shape[0]):
        act_grad = own_ref[at].astype(F32) + other_ref[at].astype(F32)
        grad_ref[at] = (act_grad * slope_ref[at]).astype(BF16)


def down_kernel(
    leading, trailing, index_ref, blocks_ref, own_ref, other_ref, hidden_ref, terms_ref, acc
):
    join_halves(core(), own_ref, other_ref, hidden_ref)
    accumulate(Held(index_ref, blocks_ref, 56), leading, trailing, hidden_ref, acc)
    devices, rows, _ = terms_ref.shape
    for device in range(devices):
        here = pl.multiple_of(jnp.bitwise_xor(position("col"), device) * rows, rows)
        for at in range(trailing):
            terms_ref[device, :, pl.ds(at * BS, BS)] = acc[at, pl.ds(here, rows), :].astype(BF16)


def input_kernel(
    leading, trailing, index_hbm, blocks_hbm, own_ref, other_ref, grad_ref, terms_ref, turned, acc, flat, *stream
):
    source = Stream(index_hbm, blocks_hbm, *stream)
    join_halves(core(), own_ref, other_ref, grad_ref)
    accumulate_turned(source, leading, trailing, grad_ref, turned, acc)
    for at in range(leading):
        flat[at] = acc[at].T
    devices, rows, _ = terms_ref.shape
    for device in range(devices):
        here = pl.multiple_of(jnp.bitwise_xor(position("col"), device) * rows, rows)
        for at in range(leading):
            terms_ref[device, :, pl.ds(at * BS, BS)] = flat[at, pl.ds(here, rows), :].astype(BF16)


def block_grads(leading, trailing, index_ref, left_ref, right_ref, out_ref, turned, held, sems):
    slots = index_ref.shape[0]
    step = divisor(slots, 56)

    def out_copy(at):
        here = pl.ds(at * step, step)
        return pltpu.make_async_copy(held.at[here], out_ref.at[here], sems.at[at])

    for at in range(leading):
        turned[at] = left_ref[at].T

    def group(at, carry):
        for inner in range(step):
            slot = at * step + inner
            place = index_ref[slot]
            lead = jnp.minimum(place // trailing, leading - 1)
            product = jnp.dot(turned[lead], right_ref[place % trailing], preferred_element_type=F32)
            held[slot] = jnp.where(place < leading * trailing, product, 0.0).astype(BF16)
        out_copy(at).start()
        return carry

    lax.fori_loop(0, slots // step, group, 0)
    return [out_copy(at) for at in range(slots // step)]


def tail_kernel(
    up_index,
    down_index,
    tokens_ref,
    pre_grad_ref,
    hidden_ref,
    cot_ref,
    received_ref,
    up_ref,
    down_ref,
    outputs_ref,
    up_turned,
    down_turned,
    up_held,
    down_held,
    up_sems,
    down_sems,
):
    rows, cols = tokens_ref.shape[0], hidden_ref.shape[0]
    copies = block_grads(
        cols, rows, down_index, hidden_ref, cot_ref, down_ref, down_turned, down_held, down_sems
    )
    copies += block_grads(
        rows, cols, up_index, tokens_ref, pre_grad_ref, up_ref, up_turned, up_held, up_sems
    )
    total = received_ref[0].astype(F32)
    for device in range(1, received_ref.shape[0]):
        total += received_ref[device].astype(F32)
    outputs_ref[...] = total.astype(BF16)
    for copy in copies:
        copy.wait()


def shards(tokens, up_blocks, up_index, down_blocks, down_index, out_cot):
    rows, width = tokens.shape
    col_devices, row_devices = lax.axis_size("col"), lax.axis_size("row")
    row_blocks = width // BS
    col_blocks = FF // (BS * col_devices)
    tok_count = rows * col_devices
    half = tok_count // 2
    slots = up_index.shape[2]
    up_weight = pltpu.with_memory_space_constraint(up_blocks[0, 0], pltpu.HBM)
    down_weight = down_blocks[0, 0]
    up_place = pltpu.with_memory_space_constraint(up_index[0, 0], pltpu.HBM)
    down_place = down_index[0, 0]
    cost = pl.CostEstimate(
        flops=2 * slots * BS * BS * tok_count, bytes_accessed=2 * slots * BS * BS, transcendentals=0
    )

    def swap(values, axis, bit):
        count = lax.axis_size(axis)
        return lax.ppermute(values, axis, [(at, at ^ bit) for at in range(count)])

    def call(body, name, outs, ins, scratch, *args, out_specs=None, **more):
        return pl.pallas_call(
            body,
            out_shape=outs,
            in_specs=ins,
            out_specs=out_specs or jax.tree.map(lambda _: VMEM, outs),
            scratch_shapes=scratch,
            compiler_params=params(),
            name=name,
            **more,
        )(*args)

    def shape(*dims, dtype=BF16):
        return jax.ShapeDtypeStruct(dims, dtype)

    long = pl.CostEstimate(flops=0, bytes_accessed=1 << 25, transcendentals=0)
    mine = call(
        pack_kernel,
        "pack",
        shape(2 * rows, width),
        [HBM] * 2,
        [pltpu.VMEM((2, rows, width), BF16), pltpu.SemaphoreType.DMA((2,))],
        pltpu.with_memory_space_constraint(tokens, pltpu.HBM),
        pltpu.with_memory_space_constraint(out_cot, pltpu.HBM),
        cost_estimate=long,
    )
    parts = {0: mine}
    for bit in sorted(range(1, col_devices), key=lambda bit: (bit < 4, bit % 2 if bit >= 4 else 0, bit)):
        relayed = bit >= 4 and bit % 2 == 1
        parts[bit] = swap(parts[bit - 1] if relayed else mine, "col", 1 if relayed else bit)
    parts = [parts[bit] for bit in range(col_devices)]

    tile_rows = shape(row_blocks, tok_count, BS)
    tile_cols = shape(col_blocks, tok_count, BS)
    half_cols = shape(col_blocks, half, BS)
    terms = shape(col_devices, rows, width)
    acc_rows = pltpu.VMEM((row_blocks + 1, tok_count, BS), F32)
    acc_cols = pltpu.VMEM((col_blocks + 1, tok_count, BS), F32)
    acc_rows_turned = pltpu.VMEM((row_blocks + 1, BS, tok_count), F32)
    acc_cols_turned = pltpu.VMEM((col_blocks + 1, BS, tok_count), F32)
    rows_turned = pltpu.VMEM((row_blocks, BS, tok_count), BF16)
    cols_turned = pltpu.VMEM((col_blocks, BS, tok_count), BF16)
    ANY = pl.BlockSpec(memory_space=pl.ANY)

    def pair_sum(keep, give, cut=1):
        parts = [swap(part, "row", 1) for part in jnp.split(give, cut)]
        total = (keep.astype(F32) + jnp.concatenate(parts).astype(F32)).astype(BF16)
        bit = 2
        while 2 * bit < row_devices:
            total = (total.astype(F32) + swap(total, "row", bit).astype(F32)).astype(BF16)
            bit *= 2
        return total

    last = row_devices // 2
    features, cotangents, pre_keep, pre_give = call(
        functools.partial(up_kernel, row_blocks, col_blocks),
        "up",
        (tile_rows, tile_rows, half_cols, half_cols),
        [HBM, HBM] + [VMEM] * len(parts),
        [acc_cols] + Stream.scratch(slots, 28),
        up_place,
        up_weight,
        *parts,
        cost_estimate=cost,
    )
    pre_own = pair_sum(pre_keep, pre_give)
    pre_other = swap(pre_own, "row", last)

    act_keep, act_give = call(
        functools.partial(act_kernel, col_blocks, row_blocks),
        "act",
        (half_cols, half_cols),
        [SMEM, VMEM, VMEM, ANY],
        [rows_turned, acc_cols_turned],
        down_place,
        down_weight,
        cotangents,
        pre_own,
        cost_estimate=cost,
    )
    act_own = pair_sum(act_keep, act_give)
    act_other = swap(act_own, "row", last)

    hidden_own, slope = call(
        gelu_kernel,
        "gelu",
        (half_cols, shape(col_blocks, half, BS, dtype=F32)),
        [VMEM, VMEM],
        [],
        pre_own,
        pre_other,
    )
    hidden, out_terms = call(
        functools.partial(down_kernel, col_blocks, row_blocks),
        "down",
        (tile_cols, terms),
        [SMEM, VMEM, VMEM, VMEM],
        [acc_rows],
        down_place,
        down_weight,
        hidden_own,
        swap(hidden_own, "row", 1),
        cost_estimate=cost,
    )

    def exchanged(values):
        return lax.all_to_all(values, "col", split_axis=0, concat_axis=0, tiled=True)

    out_received = exchanged(out_terms)
    grad_own = call(
        slope_kernel, "slope", half_cols, [VMEM] * 3, [], act_own, act_other, slope, cost_estimate=long
    )
    pre_grad, input_terms = call(
        functools.partial(input_kernel, row_blocks, col_blocks),
        "input",
        (tile_cols, terms),
        [HBM, HBM, VMEM, VMEM],
        [cols_turned, acc_rows_turned, pltpu.VMEM((row_blocks, tok_count, BS), F32)]
        + Stream.scratch(slots, 28),
        up_place,
        up_weight,
        grad_own,
        swap(grad_own, "row", 1),
        cost_estimate=cost,
    )
    input_grad = jnp.sum(exchanged(input_terms).astype(F32), axis=0).astype(BF16)
    chunks = pltpu.SemaphoreType.DMA((slots // divisor(slots, 56),))
    blocks = shape(slots, BS, BS)
    held = pltpu.VMEM((slots, BS, BS), BF16)
    up_grad, down_grad, outputs = call(
        tail_kernel,
        "tail",
        (blocks, blocks, shape(rows, width)),
        [SMEM, SMEM] + [VMEM] * 5,
        [rows_turned, cols_turned, held, held, chunks, chunks],
        up_index[0, 0],
        down_place,
        features,
        pre_grad,
        hidden,
        cotangents,
        out_received,
        out_specs=(HBM, HBM, VMEM),
        cost_estimate=pl.CostEstimate(
            flops=4 * slots * BS * BS * tok_count, bytes_accessed=4 * slots * BS * BS, transcendentals=0
        ),
    )
    return outputs, input_grad, up_grad[None, None], down_grad[None, None]


def solution(mesh):
    placed = (
        P("col", "row"),
        P("row", "col", None, None, None),
        P("row", "col", None),
        P("row", "col", None, None, None),
        P("row", "col", None),
        P("col", "row"),
    )
    return jax.shard_map(
        shards,
        mesh=mesh,
        in_specs=placed,
        out_specs=(
            P("col", "row"),
            P("col", "row"),
            P("row", "col", None, None, None),
            P("row", "col", None, None, None),
        ),
        check_vma=False,
    )
```

time: 293 us -> 61.5 us (0.21)
  blocking collectives: 81.8 us -> 0 us
  waiting for transfers between devices: 96.5 us -> 16.5 us
  other arithmetic: 52 us -> 0.8 us
  matrix products: 35.9 us -> 0 us
  Pallas kernels: 0 us -> 19.5 us
  starting transfers between devices: 7.2 us -> 23.6 us
  between operations: 14.3 us -> 0.77 us
  local copies, waits for them, and re-layouts: 3.56 us -> 0.01 us
    reduce_scatter x2 -> x0, waiting for transfers between devices: 96.4 us -> none  [the longest x1 64.3 us: shards(): lax.psum_scatter(input_terms.astype(jnp.bfloat16), 'col', scatter_dimensi...]
    all_gather x4 -> x0, blocking collectives: 81.8 us -> none  [the longest x1 32.7 us: shards(): features = lax.all_gather(tokens, 'col', axis=0, tiled=True)]
    scatter-add x4 -> x0, other arithmetic: 47.5 us -> none  [place_blocks(): jnp.zeros((tok_count, width_blocks, BS), jnp.float32).at[:, clipped, :]]
    dot_general x10 -> x0, matrix products: 35.9 us -> none  [the longest x2 14.3 us: backward_tile(): jnp.einsum('ktd,kbd->tkb', picked, blocks, preferred_element_type=jnp.flo...]
    pallas_call x0 -> x8, Pallas kernels: none -> 19.5 us  [call(): pl.pallas_call(body, out_shape=outs, in_specs=ins, out_specs=out_specs or...]
    ppermute x0 -> x13, starting transfers between devices: none -> 15.1 us  [swap(): return lax.ppermute(values, axis, [(at, at ^ bit) for at in range(count)])]
    ppermute x0 -> x13, waiting for transfers between devices: none -> 9.77 us  [swap(): return lax.ppermute(values, axis, [(at, at ^ bit) for at in range(count)])]
    all_to_all x2, waiting for transfers between devices: 0.01 us -> 6.69 us  [exchanged(): lax.all_to_all(values, 'col', split_axis=0, concat_axis=0, tiled=True)]
  transfers between devices with their start and end apart: 4 -> 15, of which waited for: 2 -> 10; matrix products, arithmetic and copies ran while one was open for 17% -> 0% of each run, Pallas kernels for 0% -> 26%
where the time goes in v2:
time: 61.5 us; the launch traced here: 61.1 us
  starting transfers between devices  23.6 us (38%)
  Pallas kernels  19.5 us (32%)
  waiting for transfers between devices  16.5 us (27%)
  other arithmetic  0.8 us (1%)
  between operations  0.77 us (1%)
    pallas_call x8, Pallas kernels, call(): pl.pallas_call(body, out_shape=outs, in_specs=ins, out_specs=out_specs or...  19.5 us
    ppermute x13, starting transfers between devices, swap(): return lax.ppermute(values, axis, [(at, at ^ bit) for at in range(count)])  15.1 us
    ppermute x13, waiting for transfers between devices, swap(): return lax.ppermute(values, axis, [(at, at ^ bit) for at in range(count)])  9.77 us
    all_to_all x2, starting transfers between devices, exchanged(): lax.all_to_all(values, 'col', split_axis=0, concat_axis=0, tiled=True)  8.53 us
    all_to_all x2, waiting for transfers between devices, exchanged(): lax.all_to_all(values, 'col', split_axis=0, concat_axis=0, tiled=True)  6.69 us
  transfers between devices with their start and end apart: 15, of which 10 were waited for; matrix products, arithmetic and copies ran while one was open for 0% of the time, Pallas kernels for 26%

profile of v2, /device:TPU:0, one launch (start us, length us, event | category | flops | bytes accessed | tf_op | source)
XLA Modules:
  0.0 61.1 jit_solution(8789239144813037326)
XLA Ops:
  0.7 0.9 %pack.1.refs_0_ = bf16[16,2048]{1,0:T(8,128)(2,1)S(1)} custom-call(bf16[8,2048]{1,0:T(8,128)(2,1)} %tokens_ref.1, bf16[8,2048]{1,0:T(8,128)(2,1)} %cot_ref.1), custom_call_target="tpu_custom_call" | custom-call | bytes 33554432 | tf_op jit(solution)/shard_map/pack/pallas_call | solution.py:314
  1.6 5.1 %collective-permute-start.5 = (bf16[16,2048]{1,0:T(8,128)(2,1)S(1)}, bf16[16,2048]{1,0:T(8,128)(2,1)S(1)}, u32[]{:S(2)}, u32[]{:S(2)}) collective-permute-start(bf16[16,2048]{1,0:T(8,128)(2,1)S(1)} %pack.1.refs_0_), channel_id=1, source_target_pairs={{0,6},{1,7},{2,4},{3,5},{4,2},{5,3},{6,0},{7,1},{8,14},{9,15},{10,... | collective-permute-start | bytes 196616 | tf_op jit(solution)/shard_map/ppermute | solution.py:311
  6.7 1.7 %collective-permute-start.2 = (bf16[16,2048]{1,0:T(8,128)(2,1)S(1)}, bf16[16,2048]{1,0:T(8,128)(2,1)S(1)}, u32[]{:S(2)}, u32[]{:S(2)}) collective-permute-start(bf16[16,2048]{1,0:T(8,128)(2,1)S(1)} %pack.1.refs_0_), channel_id=1, source_target_pairs={{0,3},{1,2},{2,1},{3,0},{4,7},{5,6},{6,5},{7,4},{8,11},{9,10},{10,... | collective-permute-start | bytes 196616 | tf_op jit(solution)/shard_map/ppermute | solution.py:311
  8.4 1.2 %collective-permute-start.1 = (bf16[16,2048]{1,0:T(8,128)(2,1)S(1)}, bf16[16,2048]{1,0:T(8,128)(2,1)S(1)}, u32[]{:S(2)}, u32[]{:S(2)}) collective-permute-start(bf16[16,2048]{1,0:T(8,128)(2,1)S(1)} %pack.1.refs_0_), channel_id=1, source_target_pairs={{0,2},{1,3},{2,0},{3,1},{4,6},{5,7},{6,4},{7,5},{8,10},{9,11},{10,... | collective-permute-start | bytes 196616 | tf_op jit(solution)/shard_map/ppermute | solution.py:311
  9.7 0.5 collective-permute-start
  10.2 1.5 %collective-permute-start.6 = (bf16[16,2048]{1,0:T(8,128)(2,1)S(1)}, bf16[16,2048]{1,0:T(8,128)(2,1)S(1)}, u32[]{:S(2)}, u32[]{:S(2)}) collective-permute-start(bf16[16,2048]{1,0:T(8,128)(2,1)S(1)} %collective-permute-done.5.refs_6_), channel_id=1, source_target_pairs={{0,1},{1,0},{2,3},{3,2},{4,5},{5,4},{6,7},{7,6},{8,9},{9,8},{10,11... | collective-permute-start | bytes 196616 | tf_op jit(solution)/shard_map/ppermute | solution.py:311
  11.7 0.7 %collective-permute-done.3.refs_4_ = bf16[16,2048]{1,0:T(8,128)(2,1)S(1)} collective-permute-done((bf16[16,2048]{1,0:T(8,128)(2,1)S(1)}, bf16[16,2048]{1,0:T(8,128)(2,1)S(1)}, u32[]{:S(2)}, u32[]{:S(2)}) %collective-permute-start.3) | collective-permute-done | bytes 65568 | tf_op jit(solution)/shard_map/ppermute | solution.py:311
  12.4 1.5 %collective-permute-start.4 = (bf16[16,2048]{1,0:T(8,128)(2,1)S(1)}, bf16[16,2048]{1,0:T(8,128)(2,1)S(1)}, u32[]{:S(2)}, u32[]{:S(2)}) collective-permute-start(bf16[16,2048]{1,0:T(8,128)(2,1)S(1)} %collective-permute-done.3.refs_4_), channel_id=1, source_target_pairs={{0,1},{1,0},{2,3},{3,2},{4,5},{5,4},{6,7},{7,6},{8,9},{9,8},{10,11... | collective-permute-start | bytes 196616 | tf_op jit(solution)/shard_map/ppermute | solution.py:311
  13.9 0.1 collective-permute-done.1.refs_2_
  14.0 0.2 collective-permute-done.refs_1_
  14.2 1.0 %collective-permute-done.6.refs_7_ = bf16[16,2048]{1,0:T(8,128)(2,1)S(1)} collective-permute-done((bf16[16,2048]{1,0:T(8,128)(2,1)S(1)}, bf16[16,2048]{1,0:T(8,128)(2,1)S(1)}, u32[]{:S(2)}, u32[]{:S(2)}) %collective-permute-start.6) | collective-permute-done | bytes 65568 | tf_op jit(solution)/shard_map/ppermute | solution.py:311
  15.3 1.4 %collective-permute-done.4.refs_5_ = bf16[16,2048]{1,0:T(8,128)(2,1)S(1)} collective-permute-done((bf16[16,2048]{1,0:T(8,128)(2,1)S(1)}, bf16[16,2048]{1,0:T(8,128)(2,1)S(1)}, u32[]{:S(2)}, u32[]{:S(2)}) %collective-permute-start.4) | collective-permute-done | bytes 65568 | tf_op jit(solution)/shard_map/ppermute | solution.py:311
  16.7 2.9 %up.1 = (bf16[16,64,128]{2,1,0:T(8,128)(2,1)S(1)}, bf16[16,64,128]{2,1,0:T(8,128)(2,1)S(1)}, bf16[28,32,128]{2,1,0:T(8,128)(2,1)S(1)}, bf16[28,32,128]{2,1,0:T(8,128)(2,1)S(1)}) custom-call(s32[112]{0:T(128)} %bitcast.8, bf16[112,128,128]{2,1,0:T(8,128)(2,1)} %bitcast.14, bf16[16,2048]{1,0:T(8,128)(2,1)S(1)} %pack.1.refs_0_, ...), custom_call_target="tpu_custom_call" | custom-call | flops 234881024 | bytes 3670016 | tf_op jit(solution)/shard_map/up/pallas_call | solution.py:314
  19.6 0.1 collective-permute-start.7
  19.7 1.5 %collective-permute-done.7 = bf16[28,32,128]{2,1,0:T(8,128)(2,1)S(1)} collective-permute-done((bf16[28,32,128]{2,1,0:T(8,128)(2,1)S(1)}, bf16[28,32,128]{2,1,0:T(8,128)(2,1)S(1)}, u32[]{:S(2)}, u32[]{:S(2)}) %collective-permute-start.7) | collective-permute-done | bytes 229408 | tf_op jit(solution)/shard_map/ppermute | solution.py:311
  21.1 0.1 add_convert_fusion.1.after_ref.own_ref
  21.2 1.6 %collective-permute-start.10 = (bf16[28,32,128]{2,1,0:T(8,128)(2,1)S(1)}, bf16[28,32,128]{2,1,0:T(8,128)(2,1)S(1)}, u32[]{:S(2)}, u32[]{:S(2)}) collective-permute-start(bf16[28,32,128]{2,1,0:T(8,128)(2,1)S(1)} %add_convert_fusion.1.after_ref.own_ref), channel_id=1, source_target_pairs={{0,16},{8,24},{16,0},{24,8},{1,17},{9,25},{17,1},{25,9},{2,18},{10... | collective-permute-start | bytes 688136 | tf_op jit(solution)/shard_map/ppermute | solution.py:311
  22.8 2.7 %act.1 = (bf16[28,32,128]{2,1,0:T(8,128)(2,1)S(1)}, bf16[28,32,128]{2,1,0:T(8,128)(2,1)S(1)}) custom-call(s32[112]{0:T(128)S(1)} %bitcast.11, bf16[112,128,128]{2,1,0:T(8,128)(2,1)S(1)} %bitcast.6, bf16[16,64,128]{2,1,0:T(8,128)(2,1)S(1)} %get-tuple-element.20.cot_ref, bf16[28,32,128]{2,1,0:T(8,128)(2,1)S(1)} %add_convert_fusion.1.after_ref.own_ref), custom_call_target="tpu_custom_call" | custom-call | flops 234881024 | bytes 3670016 | tf_op jit(solution)/shard_map/act/pallas_call | solution.py:314
  25.6 3.3 %collective-permute-done.10.other_ref = bf16[28,32,128]{2,1,0:T(8,128)(2,1)S(1)} collective-permute-done((bf16[28,32,128]{2,1,0:T(8,128)(2,1)S(1)}, bf16[28,32,128]{2,1,0:T(8,128)(2,1)S(1)}, u32[]{:S(2)}, u32[]{:S(2)}) %collective-permute-start.10) | collective-permute-done | bytes 229408 | tf_op jit(solution)/shard_map/ppermute | solution.py:311
  28.9 0.3 gelu.1
  29.3 0.1 add_convert_fusion.own_ref
  29.4 1.6 %collective-permute-start.9 = (bf16[28,32,128]{2,1,0:T(8,128)(2,1)S(1)}, bf16[28,32,128]{2,1,0:T(8,128)(2,1)S(1)}, u32[]{:S(2)}, u32[]{:S(2)}) collective-permute-start(bf16[28,32,128]{2,1,0:T(8,128)(2,1)S(1)} %add_convert_fusion.own_ref), channel_id=1, source_target_pairs={{0,16},{8,24},{16,0},{24,8},{1,17},{9,25},{17,1},{25,9},{2,18},{10... | collective-permute-start | bytes 688136 | tf_op jit(solution)/shard_map/ppermute | solution.py:311
  31.0 2.8 %down.1 = (bf16[28,64,128]{2,1,0:T(8,128)(2,1)S(1)}, bf16[8,8,2048]{2,1,0:T(8,128)(2,1)}) custom-call(s32[112]{0:T(128)S(1)} %bitcast.12, bf16[112,128,128]{2,1,0:T(8,128)(2,1)S(1)} %bitcast.7, bf16[28,32,128]{2,1,0:T(8,128)(2,1)S(1)} %get-tuple-element.27.own_ref, bf16[28,32,128]{2,1,0:T(8,128)(2,1)S(1)} %collective-permute-done.12.other_ref), custom_call_target="tpu_custom_call" | custom-call | flops 234881024 | bytes 3670016 | tf_op jit(solution)/shard_map/down/pallas_call | solution.py:314
  33.8 4.9 %all-to-all-start = ((bf16[8,8,2048]{2,1,0:T(8,128)(2,1)}), bf16[8,8,2048]{2,1,0:T(8,128)(2,1)S(1)}, u32[]{:S(2)}, u32[]{:S(2)}) async-start(bf16[8,8,2048]{2,1,0:T(8,128)(2,1)} %get-tuple-element.29), calls=%async_computation | async-start | bytes 524288 | tf_op jit(solution)/shard_map/all_to_all | solution.py:419
  38.8 0.1 slope.1.own_ref
  38.9 1.5 %collective-permute-done.11.other_ref = bf16[28,32,128]{2,1,0:T(8,128)(2,1)S(1)} collective-permute-done((bf16[28,32,128]{2,1,0:T(8,128)(2,1)S(1)}, bf16[28,32,128]{2,1,0:T(8,128)(2,1)S(1)}, u32[]{:S(2)}, u32[]{:S(2)}) %collective-permute-start.11) | collective-permute-done | bytes 229408 | tf_op jit(solution)/shard_map/ppermute | solution.py:311
  40.4 4.3 %input.1 = (bf16[28,64,128]{2,1,0:T(8,128)(2,1)S(1)}, bf16[8,8,2048]{2,1,0:T(8,128)(2,1)}) custom-call(s32[112]{0:T(128)} %bitcast.9, bf16[112,128,128]{2,1,0:T(8,128)(2,1)} %bitcast.15, bf16[28,32,128]{2,1,0:T(8,128)(2,1)S(1)} %slope.1.own_ref, bf16[28,32,128]{2,1,0:T(8,128)(2,1)S(1)} %collective-permute-done.11.other_ref), custom_call_target="tpu_custom_call" | custom-call | flops 234881024 | bytes 3670016 | tf_op jit(solution)/shard_map/input/pallas_call | solution.py:314
  44.7 3.4 %all-to-all-done.received_ref = bf16[8,8,2048]{2,1,0:T(8,128)(2,1)S(1)} async-done(((bf16[8,8,2048]{2,1,0:T(8,128)(2,1)}), bf16[8,8,2048]{2,1,0:T(8,128)(2,1)S(1)}, u32[]{:S(2)}, u32[]{:S(2)}) %all-to-all-start) | async-done | bytes 262176 | tf_op jit(solution)/shard_map/all_to_all | solution.py:419
  48.0 3.6 %all-to-all-start.1 = ((bf16[8,8,2048]{2,1,0:T(8,128)(2,1)}), bf16[8,8,2048]{2,1,0:T(8,128)(2,1)S(1)}, u32[]{:S(2)}, u32[]{:S(2)}) async-start(bf16[8,8,2048]{2,1,0:T(8,128)(2,1)} %get-tuple-element.31), calls=%async_computation.1 | async-start | bytes 524288 | tf_op jit(solution)/shard_map/all_to_all | solution.py:419
  51.6 5.5 %tail.1 = (bf16[112,128,128]{2,1,0:T(8,128)(2,1)}, bf16[112,128,128]{2,1,0:T(8,128)(2,1)}, bf16[8,2048]{1,0:T(8,128)(2,1)}) custom-call(s32[112]{0:T(128)S(1)} %bitcast.10, s32[112]{0:T(128)S(1)} %bitcast.13, bf16[16,64,128]{2,1,0:T(8,128)(2,1)S(1)} %get-tuple-element.19.tokens_ref, bf16[28,64,128]{2,1,0:T(8,128)(2,1)S(1)} %get-tuple-element.26.pre_grad_ref, ...), custom_call_target="tpu_custom_call" | custom-call | flops 469762048 | bytes 7340032 | tf_op jit(solution)/shard_map/tail/pallas_call | solution.py:314
  57.2 3.3 %all-to-all-done.1 = bf16[8,8,2048]{2,1,0:T(8,128)(2,1)S(1)} async-done(((bf16[8,8,2048]{2,1,0:T(8,128)(2,1)}), bf16[8,8,2048]{2,1,0:T(8,128)(2,1)S(1)}, u32[]{:S(2)}, u32[]{:S(2)}) %all-to-all-start.1) | async-done | bytes 262176 | tf_op jit(solution)/shard_map/all_to_all | solution.py:419
  60.5 0.7 %reduce_sum.12 = bf16[8,2048]{1,0:T(8,128)(2,1)} reduce(bf16[8,8,2048]{2,1,0:T(8,128)(2,1)S(1)} %all-to-all-done.1, bf16[]{:T(256)} %constant.2.clone.1), dimensions={0}, to_apply=%region_0.0 | reduce | flops 114688 | bytes 294914 | tf_op jit(solution)/shard_map/reduce_sum | solution.py:438
  (15 shorter events, 0.2 us)
Async XLA Ops:
  0.6 22.2 %copy-start.2 = (s32[1,1,112]{2,1,0:T(1,128)S(1)}, s32[1,1,112]{2,1,0:T(1,128)}, u32[]{:S(2)}) copy-start(s32[1,1,112]{2,1,0:T(1,128)} %param.10) | copy-start | bytes 1348
  0.6 22.2 %copy-start = (bf16[1,1,112,128,128]{4,3,2,1,0:T(8,128)(2,1)S(1)}, bf16[1,1,112,128,128]{4,3,2,1,0:T(8,128)(2,1)}, u32[]{:S(2)}) copy-start(bf16[1,1,112,128,128]{4,3,2,1,0:T(8,128)(2,1)} %param.9) | copy-start | bytes 11010052
  1.6 8.6 %collective-permute-start.5 = (bf16[16,2048]{1,0:T(8,128)(2,1)S(1)}, bf16[16,2048]{1,0:T(8,128)(2,1)S(1)}, u32[]{:S(2)}, u32[]{:S(2)}) collective-permute-start(bf16[16,2048]{1,0:T(8,128)(2,1)S(1)} %pack.1.refs_0_), channel_id=1, source_target_pairs={{0,6},{1,7},{2,4},{3,5},{4,2},{5,3},{6,0},{7,1},{8,14},{9,15},{10,... | collective-permute-start | bytes 196616 | tf_op jit(solution)/shard_map/ppermute | solution.py:311
  6.7 5.7 %collective-permute-start.3 = (bf16[16,2048]{1,0:T(8,128)(2,1)S(1)}, bf16[16,2048]{1,0:T(8,128)(2,1)S(1)}, u32[]{:S(2)}, u32[]{:S(2)}) collective-permute-start(bf16[16,2048]{1,0:T(8,128)(2,1)S(1)} %pack.1.refs_0_), channel_id=1, source_target_pairs={{0,4},{1,5},{2,6},{3,7},{4,0},{5,1},{6,2},{7,3},{8,12},{9,13},{10,... | collective-permute-start | bytes 196616 | tf_op jit(solution)/shard_map/ppermute | solution.py:311
  6.7 7.2 %collective-permute-start.2 = (bf16[16,2048]{1,0:T(8,128)(2,1)S(1)}, bf16[16,2048]{1,0:T(8,128)(2,1)S(1)}, u32[]{:S(2)}, u32[]{:S(2)}) collective-permute-start(bf16[16,2048]{1,0:T(8,128)(2,1)S(1)} %pack.1.refs_0_), channel_id=1, source_target_pairs={{0,3},{1,2},{2,1},{3,0},{4,7},{5,6},{6,5},{7,4},{8,11},{9,10},{10,... | collective-permute-start | bytes 196616 | tf_op jit(solution)/shard_map/ppermute | solution.py:311
  8.4 5.6 %collective-permute-start.1 = (bf16[16,2048]{1,0:T(8,128)(2,1)S(1)}, bf16[16,2048]{1,0:T(8,128)(2,1)S(1)}, u32[]{:S(2)}, u32[]{:S(2)}) collective-permute-start(bf16[16,2048]{1,0:T(8,128)(2,1)S(1)} %pack.1.refs_0_), channel_id=1, source_target_pairs={{0,2},{1,3},{2,0},{3,1},{4,6},{5,7},{6,4},{7,5},{8,10},{9,11},{10,... | collective-permute-start | bytes 196616 | tf_op jit(solution)/shard_map/ppermute | solution.py:311
  9.7 4.6 %collective-permute-start = (bf16[16,2048]{1,0:T(8,128)(2,1)S(1)}, bf16[16,2048]{1,0:T(8,128)(2,1)S(1)}, u32[]{:S(2)}, u32[]{:S(2)}) collective-permute-start(bf16[16,2048]{1,0:T(8,128)(2,1)S(1)} %pack.1.refs_0_), channel_id=1, source_target_pairs={{0,1},{1,0},{2,3},{3,2},{4,5},{5,4},{6,7},{7,6},{8,9},{9,8},{10,11... | collective-permute-start | bytes 196616 | tf_op jit(solution)/shard_map/ppermute | solution.py:311
  10.2 5.0 %collective-permute-start.6 = (bf16[16,2048]{1,0:T(8,128)(2,1)S(1)}, bf16[16,2048]{1,0:T(8,128)(2,1)S(1)}, u32[]{:S(2)}, u32[]{:S(2)}) collective-permute-start(bf16[16,2048]{1,0:T(8,128)(2,1)S(1)} %collective-permute-done.5.refs_6_), channel_id=1, source_target_pairs={{0,1},{1,0},{2,3},{3,2},{4,5},{5,4},{6,7},{7,6},{8,9},{9,8},{10,11... | collective-permute-start | bytes 196616 | tf_op jit(solution)/shard_map/ppermute | solution.py:311
  12.4 4.3 %collective-permute-start.4 = (bf16[16,2048]{1,0:T(8,128)(2,1)S(1)}, bf16[16,2048]{1,0:T(8,128)(2,1)S(1)}, u32[]{:S(2)}, u32[]{:S(2)}) collective-permute-start(bf16[16,2048]{1,0:T(8,128)(2,1)S(1)} %collective-permute-done.3.refs_4_), channel_id=1, source_target_pairs={{0,1},{1,0},{2,3},{3,2},{4,5},{5,4},{6,7},{7,6},{8,9},{9,8},{10,11... | collective-permute-start | bytes 196616 | tf_op jit(solution)/shard_map/ppermute | solution.py:311
  19.6 1.6 %collective-permute-start.7 = (bf16[28,32,128]{2,1,0:T(8,128)(2,1)S(1)}, bf16[28,32,128]{2,1,0:T(8,128)(2,1)S(1)}, u32[]{:S(2)}, u32[]{:S(2)}) collective-permute-start(bf16[28,32,128]{2,1,0:T(8,128)(2,1)S(1)} %get-tuple-element.22), channel_id=1, source_target_pairs={{0,8},{8,0},{16,24},{24,16},{1,9},{9,1},{17,25},{25,17},{2,10},{10... | collective-permute-start | bytes 688136 | tf_op jit(solution)/shard_map/ppermute | solution.py:311
  21.2 7.7 %collective-permute-start.10 = (bf16[28,32,128]{2,1,0:T(8,128)(2,1)S(1)}, bf16[28,32,128]{2,1,0:T(8,128)(2,1)S(1)}, u32[]{:S(2)}, u32[]{:S(2)}) collective-permute-start(bf16[28,32,128]{2,1,0:T(8,128)(2,1)S(1)} %add_convert_fusion.1.after_ref.own_ref), channel_id=1, source_target_pairs={{0,16},{8,24},{16,0},{24,8},{1,17},{9,25},{17,1},{25,9},{2,18},{10... | collective-permute-start | bytes 688136 | tf_op jit(solution)/shard_map/ppermute | solution.py:311
  25.5 3.8 %collective-permute-start.8 = (bf16[28,32,128]{2,1,0:T(8,128)(2,1)S(1)}, bf16[28,32,128]{2,1,0:T(8,128)(2,1)S(1)}, u32[]{:S(2)}, u32[]{:S(2)}) collective-permute-start(bf16[28,32,128]{2,1,0:T(8,128)(2,1)S(1)} %get-tuple-element.24), channel_id=1, source_target_pairs={{0,8},{8,0},{16,24},{24,16},{1,9},{9,1},{17,25},{25,17},{2,10},{10... | collective-permute-start | bytes 688136 | tf_op jit(solution)/shard_map/ppermute | solution.py:311
  29.3 1.8 %collective-permute-start.12 = (bf16[28,32,128]{2,1,0:T(8,128)(2,1)S(1)}, bf16[28,32,128]{2,1,0:T(8,128)(2,1)S(1)}, u32[]{:S(2)}, u32[]{:S(2)}) collective-permute-start(bf16[28,32,128]{2,1,0:T(8,128)(2,1)S(1)} %get-tuple-element.27.own_ref), channel_id=1, source_target_pairs={{0,8},{8,0},{16,24},{24,16},{1,9},{9,1},{17,25},{25,17},{2,10},{10... | collective-permute-start | bytes 688136 | tf_op jit(solution)/shard_map/ppermute | solution.py:311
  29.4 9.3 %collective-permute-start.9 = (bf16[28,32,128]{2,1,0:T(8,128)(2,1)S(1)}, bf16[28,32,128]{2,1,0:T(8,128)(2,1)S(1)}, u32[]{:S(2)}, u32[]{:S(2)}) collective-permute-start(bf16[28,32,128]{2,1,0:T(8,128)(2,1)S(1)} %add_convert_fusion.own_ref), channel_id=1, source_target_pairs={{0,16},{8,24},{16,0},{24,8},{1,17},{9,25},{17,1},{25,9},{2,18},{10... | collective-permute-start | bytes 688136 | tf_op jit(solution)/shard_map/ppermute | solution.py:311
  33.8 17.8 %copy-start.1 = (s32[1,1,112]{2,1,0:T(1,128)S(1)}, s32[1,1,112]{2,1,0:T(1,128)}, u32[]{:S(2)}) copy-start(s32[1,1,112]{2,1,0:T(1,128)} %param.8) | copy-start | bytes 1348
  33.8 14.2 %all-to-all-start = ((bf16[8,8,2048]{2,1,0:T(8,128)(2,1)}), bf16[8,8,2048]{2,1,0:T(8,128)(2,1)S(1)}, u32[]{:S(2)}, u32[]{:S(2)}) async-start(bf16[8,8,2048]{2,1,0:T(8,128)(2,1)} %get-tuple-element.29), calls=%async_computation | async-start | bytes 524288 | tf_op jit(solution)/shard_map/all_to_all | solution.py:419
  38.8 1.6 %collective-permute-start.11 = (bf16[28,32,128]{2,1,0:T(8,128)(2,1)S(1)}, bf16[28,32,128]{2,1,0:T(8,128)(2,1)S(1)}, u32[]{:S(2)}, u32[]{:S(2)}) collective-permute-start(bf16[28,32,128]{2,1,0:T(8,128)(2,1)S(1)} %slope.1.own_ref), channel_id=1, source_target_pairs={{0,8},{8,0},{16,24},{24,16},{1,9},{9,1},{17,25},{25,17},{2,10},{10... | collective-permute-start | bytes 688136 | tf_op jit(solution)/shard_map/ppermute | solution.py:311
  48.0 12.4 %all-to-all-start.1 = ((bf16[8,8,2048]{2,1,0:T(8,128)(2,1)}), bf16[8,8,2048]{2,1,0:T(8,128)(2,1)S(1)}, u32[]{:S(2)}, u32[]{:S(2)}) async-start(bf16[8,8,2048]{2,1,0:T(8,128)(2,1)} %get-tuple-element.31), calls=%async_computation.1 | async-start | bytes 524288 | tf_op jit(solution)/shard_map/all_to_all | solution.py:419

commit v3 on v2

--- a/solution.py
+++ b/solution.py
@@ -199,7 +199,7 @@
         slope_ref[at] = gelu_slope(preact)
 
 
-def slope_kernel(own_ref, other_ref, slope_ref, grad_ref):
+def slope_kernel(own_ref, other_ref, slope_ref, after_ref, grad_ref):
     for at in range(own_ref.shape[0]):
         act_grad = own_ref[at].astype(F32) + other_ref[at].astype(F32)
         grad_ref[at] = (act_grad * slope_ref[at]).astype(BF16)
@@ -210,26 +210,29 @@
 ):
     join_halves(core(), own_ref, other_ref, hidden_ref)
     accumulate(Held(index_ref, blocks_ref, 56), leading, trailing, hidden_ref, acc)
-    devices, rows, _ = terms_ref.shape
-    for device in range(devices):
-        here = pl.multiple_of(jnp.bitwise_xor(position("col"), device) * rows, rows)
-        for at in range(trailing):
-            terms_ref[device, :, pl.ds(at * BS, BS)] = acc[at, pl.ds(here, rows), :].astype(BF16)
+    for at in range(trailing):
+        terms_ref[at] = acc[at].astype(BF16)
+
+
+def relayed(bit):
+    return bit >= 4 and bit % 2 == 1
 
 
 def input_kernel(
-    leading, trailing, index_hbm, blocks_hbm, own_ref, other_ref, grad_ref, terms_ref, turned, acc, flat, *stream
+    leading, trailing, index_ref, blocks_ref, own_ref, other_ref, out_terms_ref, grad_ref, relay_ref, *refs
 ):
-    source = Stream(index_hbm, blocks_hbm, *stream)
+    chunks, turned, acc = refs[:-2], refs[-2], refs[-1]
     join_halves(core(), own_ref, other_ref, grad_ref)
-    accumulate_turned(source, leading, trailing, grad_ref, turned, acc)
+    accumulate_turned(Held(index_ref, blocks_ref, 56), leading, trailing, grad_ref, turned, acc)
+    devices = relay_ref.shape[0] + len(chunks)
+    rows = grad_ref.shape[1] // devices
     for at in range(leading):
-        flat[at] = acc[at].T
-    devices, rows, _ = terms_ref.shape
-    for device in range(devices):
-        here = pl.multiple_of(jnp.bitwise_xor(position("col"), device) * rows, rows)
-        for at in range(leading):
-            terms_ref[device, :, pl.ds(at * BS, BS)] = flat[at, pl.ds(here, rows), :].astype(BF16)
+        outs, grads = out_terms_ref[at].astype(F32), acc[at].T
+        direct, relays = list(chunks), [relay_ref.at[slot] for slot in range(relay_ref.shape[0])]
+        for bit in range(devices):
+            mine = slice(bit * rows, (bit + 1) * rows)
+            target = (relays if relayed(bit) else direct).pop(0)
+            target[:, pl.ds(at * BS, BS)] = jnp.concatenate([outs[mine], grads[mine]]).astype(BF16)
 
 
 def block_grads(leading, trailing, index_ref, left_ref, right_ref, out_ref, turned, held, sems):
@@ -257,37 +260,23 @@
     return [out_copy(at) for at in range(slots // step)]
 
 
-def tail_kernel(
-    up_index,
-    down_index,
-    tokens_ref,
-    pre_grad_ref,
-    hidden_ref,
-    cot_ref,
-    received_ref,
-    up_ref,
-    down_ref,
-    outputs_ref,
-    up_turned,
-    down_turned,
-    up_held,
-    down_held,
-    up_sems,
-    down_sems,
-):
-    rows, cols = tokens_ref.shape[0], hidden_ref.shape[0]
+def grad_kernel(index_ref, left_ref, right_ref, out_ref, mark_ref, turned, held, sems):
     copies = block_grads(
-        cols, rows, down_index, hidden_ref, cot_ref, down_ref, down_turned, down_held, down_sems
-    )
-    copies += block_grads(
-        rows, cols, up_index, tokens_ref, pre_grad_ref, up_ref, up_turned, up_held, up_sems
-    )
-    total = received_ref[0].astype(F32)
-    for device in range(1, received_ref.shape[0]):
-        total += received_ref[device].astype(F32)
-    outputs_ref[...] = total.astype(BF16)
+        left_ref.shape[0], right_ref.shape[0], index_ref, left_ref, right_ref, out_ref, turned, held, sems
+    )
+    mark_ref[...] = jnp.zeros_like(mark_ref)
     for copy in copies:
         copy.wait()
+
+
+def merge_kernel(count, *refs):
+    relay_ref, ins, outs = refs[0], refs[2 : 2 + count], refs[2 + count :]
+    slots = relay_ref.shape[0]
+    for at in range(count):
+        value = ins[at][...]
+        if at >= count - slots:
+            value = (value.astype(F32) + relay_ref[at - count + slots].astype(F32)).astype(BF16)
+        outs[at][...] = value
 
 
 def shards(tokens, up_blocks, up_index, down_blocks, down_index, out_cot):
@@ -338,14 +327,13 @@
     )
     parts = {0: mine}
     for bit in sorted(range(1, col_devices), key=lambda bit: (bit < 4, bit % 2 if bit >= 4 else 0, bit)):
-        relayed = bit >= 4 and bit % 2 == 1
-        parts[bit] = swap(parts[bit - 1] if relayed else mine, "col", 1 if relayed else bit)
+        parts[bit] = swap(parts[bit - 1], "col", 1) if relayed(bit) else swap(mine, "col", bit)
     parts = [parts[bit] for bit in range(col_devices)]
 
     tile_rows = shape(row_blocks, tok_count, BS)
     tile_cols = shape(col_blocks, tok_count, BS)
     half_cols = shape(col_blocks, half, BS)
-    terms = shape(col_devices, rows, width)
+    chunk = shape(2 * rows, width)
     acc_rows = pltpu.VMEM((row_blocks + 1, tok_count, BS), F32)
     acc_cols = pltpu.VMEM((col_blocks + 1, tok_count, BS), F32)
     acc_rows_turned = pltpu.VMEM((row_blocks + 1, BS, tok_count), F32)
@@ -405,7 +393,7 @@
     hidden, out_terms = call(
         functools.partial(down_kernel, col_blocks, row_blocks),
         "down",
-        (tile_cols, terms),
+        (tile_cols, tile_rows),
         [SMEM, VMEM, VMEM, VMEM],
         [acc_rows],
         down_place,
@@ -415,49 +403,61 @@
         cost_estimate=cost,
     )
 
-    def exchanged(values):
-        return lax.all_to_all(values, "col", split_axis=0, concat_axis=0, tiled=True)
-
-    out_received = exchanged(out_terms)
+    def grads(name, index, left, right):
+        return call(
+            grad_kernel,
+            name,
+            (shape(slots, BS, BS), shape(8, BS, dtype=F32)),
+            [SMEM, VMEM, VMEM],
+            [
+                pltpu.VMEM((left.shape[0], BS, tok_count), BF16),
+                pltpu.VMEM((slots, BS, BS), BF16),
+                pltpu.SemaphoreType.DMA((slots // divisor(slots, 56),)),
+            ],
+            index,
+            left,
+            right,
+            out_specs=(HBM, VMEM),
+            cost_estimate=cost,
+        )
+
+    down_grad, down_mark = grads("down_grad", down_place, hidden, cotangents)
     grad_own = call(
-        slope_kernel, "slope", half_cols, [VMEM] * 3, [], act_own, act_other, slope, cost_estimate=long
-    )
-    pre_grad, input_terms = call(
+        slope_kernel, "slope", half_cols, [VMEM] * 4, [], act_own, act_other, slope, down_mark
+    )
+    by_way = [bit for bit in range(col_devices) if relayed(bit)]
+    direct = [bit for bit in range(col_devices) if not relayed(bit)]
+    pre_grad, relay, *chunks = call(
         functools.partial(input_kernel, row_blocks, col_blocks),
         "input",
-        (tile_cols, terms),
-        [HBM, HBM, VMEM, VMEM],
-        [cols_turned, acc_rows_turned, pltpu.VMEM((row_blocks, tok_count, BS), F32)]
-        + Stream.scratch(slots, 28),
-        up_place,
-        up_weight,
+        (tile_cols, shape(len(by_way), 2 * rows, width)) + (chunk,) * len(direct),
+        [SMEM, VMEM, VMEM, VMEM, VMEM],
+        [cols_turned, acc_rows_turned],
+        up_index[0, 0],
+        up_blocks[0, 0],
         grad_own,
         swap(grad_own, "row", 1),
+        out_terms,
         cost_estimate=cost,
     )
-    input_grad = jnp.sum(exchanged(input_terms).astype(F32), axis=0).astype(BF16)
-    chunks = pltpu.SemaphoreType.DMA((slots // divisor(slots, 56),))
-    blocks = shape(slots, BS, BS)
-    held = pltpu.VMEM((slots, BS, BS), BF16)
-    up_grad, down_grad, outputs = call(
-        tail_kernel,
-        "tail",
-        (blocks, blocks, shape(rows, width)),
-        [SMEM, SMEM] + [VMEM] * 5,
-        [rows_turned, cols_turned, held, held, chunks, chunks],
-        up_index[0, 0],
-        down_place,
-        features,
-        pre_grad,
-        hidden,
-        cotangents,
-        out_received,
-        out_specs=(HBM, HBM, VMEM),
-        cost_estimate=pl.CostEstimate(
-            flops=4 * slots * BS * BS * tok_count, bytes_accessed=4 * slots * BS * BS, transcendentals=0
-        ),
-    )
-    return outputs, input_grad, up_grad[None, None], down_grad[None, None]
+    up_grad, up_mark = grads("up_grad", up_index[0, 0], features, pre_grad)
+    later = [bit for bit in direct if bit not in (2,)]
+    merged = call(
+        functools.partial(merge_kernel, len(later)),
+        "merge",
+        (chunk,) * len(later),
+        [VMEM] * (2 + len(later)),
+        [],
+        swap(relay, "col", 1),
+        down_mark,
+        *(chunks[direct.index(bit)] for bit in later),
+    )
+    chunks = dict(zip(direct, chunks)) | dict(zip(later, merged))
+    total = chunks[0].astype(F32)
+    for bit in sorted(direct[1:], key=lambda bit: -bit):
+        total = total + swap(chunks[bit], "col", bit).astype(F32)
+    total = total.astype(BF16)
+    return total[:rows], total[rows:], up_grad[None, None], down_grad[None, None]
 
 
 def solution(mesh):

time: 61.5 us -> 58.2 us (0.946)
  waiting for transfers between devices: 16.5 us -> 14.8 us
  starting transfers between devices: 23.6 us -> 22.6 us
  local copies, waits for them, and re-layouts: 0.01 us -> 0.65 us
    all_to_all x2 -> x0, starting transfers between devices: 8.53 us -> none  [exchanged(): lax.all_to_all(values, 'col', split_axis=0, concat_axis=0, tiled=True)]
    ppermute x13 -> x19, starting transfers between devices: 15.1 us -> 22.6 us  [swap(): return lax.ppermute(values, axis, [(at, at ^ bit) for at in range(count)])]
    all_to_all x2 -> x0, waiting for transfers between devices: 6.69 us -> none  [exchanged(): lax.all_to_all(values, 'col', split_axis=0, concat_axis=0, tiled=True)]
    ppermute x13 -> x19, waiting for transfers between devices: 9.77 us -> 14.8 us  [swap(): return lax.ppermute(values, axis, [(at, at ^ bit) for at in range(count)])]
    reduce_sum x1 -> x0, other arithmetic: 0.65 us -> none  [shards(): jnp.sum(exchanged(input_terms).astype(F32), axis=0).astype(BF16)]
    slice x0 -> x1, local copies, waits for them, and re-layouts: none -> 0.63 us  [shards(): total[rows:]]
    pallas_call x8 -> x10, Pallas kernels: 19.5 us -> 19 us  [call(): pl.pallas_call(body, out_shape=outs, in_specs=ins, out_specs=out_specs or...]
  transfers between devices with their start and end apart: 15 -> 19, of which waited for: 10 -> 10; matrix products, arithmetic and copies ran while one was open for 0% -> 0% of each run, Pallas kernels for 26% -> 21%
where the time goes in v3:
time: 58.2 us; the launch traced here: 58 us
  starting transfers between devices  22.6 us (39%)
  Pallas kernels  19 us (33%)
  waiting for transfers between devices  14.8 us (25%)
  between operations  0.84 us (1%)
  local copies, waits for them, and re-layouts  0.65 us (1%)
    ppermute x19, starting transfers between devices, swap(): return lax.ppermute(values, axis, [(at, at ^ bit) for at in range(count)])  22.6 us
    pallas_call x10, Pallas kernels, call(): pl.pallas_call(body, out_shape=outs, in_specs=ins, out_specs=out_specs or...  19 us
    ppermute x19, waiting for transfers between devices, swap(): return lax.ppermute(values, axis, [(at, at ^ bit) for at in range(count)])  14.8 us
  transfers between devices with their start and end apart: 19, of which 10 were waited for; matrix products, arithmetic and copies ran while one was open for 0% of the time, Pallas kernels for 21%

profile of v3, /device:TPU:0, one launch (start us, length us, event | category | flops | bytes accessed | tf_op | source)
XLA Modules:
  0.0 58.0 jit_solution(6623087015829195951)
XLA Ops:
  0.7 0.9 %pack.1.refs_0_ = bf16[16,2048]{1,0:T(8,128)(2,1)S(1)} custom-call(bf16[8,2048]{1,0:T(8,128)(2,1)} %tokens_ref.1, bf16[8,2048]{1,0:T(8,128)(2,1)} %cot_ref.1), custom_call_target="tpu_custom_call" | custom-call | bytes 33554432 | tf_op jit(solution)/shard_map/pack/pallas_call | solution.py:303
  1.6 5.1 %collective-permute-start.5 = (bf16[16,2048]{1,0:T(8,128)(2,1)S(1)}, bf16[16,2048]{1,0:T(8,128)(2,1)S(1)}, u32[]{:S(2)}, u32[]{:S(2)}) collective-permute-start(bf16[16,2048]{1,0:T(8,128)(2,1)S(1)} %pack.1.refs_0_), channel_id=1, source_target_pairs={{0,6},{1,7},{2,4},{3,5},{4,2},{5,3},{6,0},{7,1},{8,14},{9,15},{10,... | collective-permute-start | bytes 196616 | tf_op jit(solution)/shard_map/ppermute | solution.py:300
  6.7 1.7 %collective-permute-start.2 = (bf16[16,2048]{1,0:T(8,128)(2,1)S(1)}, bf16[16,2048]{1,0:T(8,128)(2,1)S(1)}, u32[]{:S(2)}, u32[]{:S(2)}) collective-permute-start(bf16[16,2048]{1,0:T(8,128)(2,1)S(1)} %pack.1.refs_0_), channel_id=1, source_target_pairs={{0,3},{1,2},{2,1},{3,0},{4,7},{5,6},{6,5},{7,4},{8,11},{9,10},{10,... | collective-permute-start | bytes 196616 | tf_op jit(solution)/shard_map/ppermute | solution.py:300
  8.4 1.2 %collective-permute-start.1 = (bf16[16,2048]{1,0:T(8,128)(2,1)S(1)}, bf16[16,2048]{1,0:T(8,128)(2,1)S(1)}, u32[]{:S(2)}, u32[]{:S(2)}) collective-permute-start(bf16[16,2048]{1,0:T(8,128)(2,1)S(1)} %pack.1.refs_0_), channel_id=1, source_target_pairs={{0,2},{1,3},{2,0},{3,1},{4,6},{5,7},{6,4},{7,5},{8,10},{9,11},{10,... | collective-permute-start | bytes 196616 | tf_op jit(solution)/shard_map/ppermute | solution.py:300
  9.7 0.5 collective-permute-start
  10.2 1.5 %collective-permute-start.6 = (bf16[16,2048]{1,0:T(8,128)(2,1)S(1)}, bf16[16,2048]{1,0:T(8,128)(2,1)S(1)}, u32[]{:S(2)}, u32[]{:S(2)}) collective-permute-start(bf16[16,2048]{1,0:T(8,128)(2,1)S(1)} %collective-permute-done.5.refs_6_), channel_id=1, source_target_pairs={{0,1},{1,0},{2,3},{3,2},{4,5},{5,4},{6,7},{7,6},{8,9},{9,8},{10,11... | collective-permute-start | bytes 196616 | tf_op jit(solution)/shard_map/ppermute | solution.py:300
  11.7 0.7 %collective-permute-done.3.refs_4_ = bf16[16,2048]{1,0:T(8,128)(2,1)S(1)} collective-permute-done((bf16[16,2048]{1,0:T(8,128)(2,1)S(1)}, bf16[16,2048]{1,0:T(8,128)(2,1)S(1)}, u32[]{:S(2)}, u32[]{:S(2)}) %collective-permute-start.3) | collective-permute-done | bytes 65568 | tf_op jit(solution)/shard_map/ppermute | solution.py:300
  12.4 1.5 %collective-permute-start.4 = (bf16[16,2048]{1,0:T(8,128)(2,1)S(1)}, bf16[16,2048]{1,0:T(8,128)(2,1)S(1)}, u32[]{:S(2)}, u32[]{:S(2)}) collective-permute-start(bf16[16,2048]{1,0:T(8,128)(2,1)S(1)} %collective-permute-done.3.refs_4_), channel_id=1, source_target_pairs={{0,1},{1,0},{2,3},{3,2},{4,5},{5,4},{6,7},{7,6},{8,9},{9,8},{10,11... | collective-permute-start | bytes 196616 | tf_op jit(solution)/shard_map/ppermute | solution.py:300
  13.9 0.1 collective-permute-done.1.refs_2_
  14.0 0.2 collective-permute-done.refs_1_
  14.2 1.0 %collective-permute-done.6.refs_7_ = bf16[16,2048]{1,0:T(8,128)(2,1)S(1)} collective-permute-done((bf16[16,2048]{1,0:T(8,128)(2,1)S(1)}, bf16[16,2048]{1,0:T(8,128)(2,1)S(1)}, u32[]{:S(2)}, u32[]{:S(2)}) %collective-permute-start.6) | collective-permute-done | bytes 65568 | tf_op jit(solution)/shard_map/ppermute | solution.py:300
  15.3 1.4 %collective-permute-done.4.refs_5_ = bf16[16,2048]{1,0:T(8,128)(2,1)S(1)} collective-permute-done((bf16[16,2048]{1,0:T(8,128)(2,1)S(1)}, bf16[16,2048]{1,0:T(8,128)(2,1)S(1)}, u32[]{:S(2)}, u32[]{:S(2)}) %collective-permute-start.4) | collective-permute-done | bytes 65568 | tf_op jit(solution)/shard_map/ppermute | solution.py:300
  16.7 2.9 %up.1 = (bf16[16,64,128]{2,1,0:T(8,128)(2,1)S(1)}, bf16[16,64,128]{2,1,0:T(8,128)(2,1)S(1)}, bf16[28,32,128]{2,1,0:T(8,128)(2,1)S(1)}, bf16[28,32,128]{2,1,0:T(8,128)(2,1)S(1)}) custom-call(s32[112]{0:T(128)} %bitcast.13, bf16[112,128,128]{2,1,0:T(8,128)(2,1)} %bitcast.8, bf16[16,2048]{1,0:T(8,128)(2,1)S(1)} %pack.1.refs_0_, ...), custom_call_target="tpu_custom_call" | custom-call | flops 234881024 | bytes 3670016 | tf_op jit(solution)/shard_map/up/pallas_call | solution.py:303
  19.7 1.5 %collective-permute-done.7 = bf16[28,32,128]{2,1,0:T(8,128)(2,1)S(1)} collective-permute-done((bf16[28,32,128]{2,1,0:T(8,128)(2,1)S(1)}, bf16[28,32,128]{2,1,0:T(8,128)(2,1)S(1)}, u32[]{:S(2)}, u32[]{:S(2)}) %collective-permute-start.7) | collective-permute-done | bytes 229408 | tf_op jit(solution)/shard_map/ppermute | solution.py:300
  21.2 1.6 %collective-permute-start.10 = (bf16[28,32,128]{2,1,0:T(8,128)(2,1)S(1)}, bf16[28,32,128]{2,1,0:T(8,128)(2,1)S(1)}, u32[]{:S(2)}, u32[]{:S(2)}) collective-permute-start(bf16[28,32,128]{2,1,0:T(8,128)(2,1)S(1)} %add_convert_fusion.1.after_ref.own_ref), channel_id=1, source_target_pairs={{0,16},{8,24},{16,0},{24,8},{1,17},{9,25},{17,1},{25,9},{2,18},{10... | collective-permute-start | bytes 688136 | tf_op jit(solution)/shard_map/ppermute | solution.py:300
  22.8 2.7 %act.1 = (bf16[28,32,128]{2,1,0:T(8,128)(2,1)S(1)}, bf16[28,32,128]{2,1,0:T(8,128)(2,1)S(1)}) custom-call(s32[112]{0:T(128)S(1)} %bitcast.10, bf16[112,128,128]{2,1,0:T(8,128)(2,1)S(1)} %bitcast.6, bf16[16,64,128]{2,1,0:T(8,128)(2,1)S(1)} %get-tuple-element.30.cot_ref.right_ref, bf16[28,32,128]{2,1,0:T(8,128)(2,1)S(1)} %add_convert_fusion.1.after_ref.own_ref), custom_call_target="tpu_custom_call" | custom-call | flops 234881024 | bytes 3670016 | tf_op jit(solution)/shard_map/act/pallas_call | solution.py:303
  25.6 3.3 %collective-permute-done.10.other_ref = bf16[28,32,128]{2,1,0:T(8,128)(2,1)S(1)} collective-permute-done((bf16[28,32,128]{2,1,0:T(8,128)(2,1)S(1)}, bf16[28,32,128]{2,1,0:T(8,128)(2,1)S(1)}, u32[]{:S(2)}, u32[]{:S(2)}) %collective-permute-start.10) | collective-permute-done | bytes 229408 | tf_op jit(solution)/shard_map/ppermute | solution.py:300
  28.9 0.3 gelu.1
  29.3 0.1 add_convert_fusion.own_ref
  29.4 1.6 %collective-permute-start.9 = (bf16[28,32,128]{2,1,0:T(8,128)(2,1)S(1)}, bf16[28,32,128]{2,1,0:T(8,128)(2,1)S(1)}, u32[]{:S(2)}, u32[]{:S(2)}) collective-permute-start(bf16[28,32,128]{2,1,0:T(8,128)(2,1)S(1)} %add_convert_fusion.own_ref), channel_id=1, source_target_pairs={{0,16},{8,24},{16,0},{24,8},{1,17},{9,25},{17,1},{25,9},{2,18},{10... | collective-permute-start | bytes 688136 | tf_op jit(solution)/shard_map/ppermute | solution.py:300
  31.0 2.0 %down.1 = (bf16[28,64,128]{2,1,0:T(8,128)(2,1)S(1)}, bf16[16,64,128]{2,1,0:T(8,128)(2,1)S(1)}) custom-call(s32[112]{0:T(128)S(1)} %bitcast.11, bf16[112,128,128]{2,1,0:T(8,128)(2,1)S(1)} %bitcast.7, bf16[28,32,128]{2,1,0:T(8,128)(2,1)S(1)} %get-tuple-element.36.own_ref, bf16[28,32,128]{2,1,0:T(8,128)(2,1)S(1)} %collective-permute-done.11.other_ref), custom_call_target="tpu_custom_call" | custom-call | flops 234881024 | bytes 3670016 | tf_op jit(solution)/shard_map/down/pallas_call | solution.py:303
  33.1 3.4 %down_grad.1 = (bf16[112,128,128]{2,1,0:T(8,128)(2,1)}, f32[8,128]{1,0:T(8,128)S(1)}) custom-call(s32[112]{0:T(128)S(1)} %bitcast.12, bf16[28,64,128]{2,1,0:T(8,128)(2,1)S(1)} %get-tuple-element.37.left_ref, bf16[16,64,128]{2,1,0:T(8,128)(2,1)S(1)} %get-tuple-element.30.cot_ref.right_ref), custom_call_target="tpu_custom_call" | custom-call | flops 234881024 | bytes 3670016 | tf_op jit(solution)/shard_map/down_grad/pallas_call | solution.py:303
  36.5 1.0 %collective-permute-done.9.other_ref = bf16[28,32,128]{2,1,0:T(8,128)(2,1)S(1)} collective-permute-done((bf16[28,32,128]{2,1,0:T(8,128)(2,1)S(1)}, bf16[28,32,128]{2,1,0:T(8,128)(2,1)S(1)}, u32[]{:S(2)}, u32[]{:S(2)}) %collective-permute-start.9) | collective-permute-done | bytes 229408 | tf_op jit(solution)/shard_map/ppermute | solution.py:300
  37.6 1.5 %collective-permute-done.12.other_ref = bf16[28,32,128]{2,1,0:T(8,128)(2,1)S(1)} collective-permute-done((bf16[28,32,128]{2,1,0:T(8,128)(2,1)S(1)}, bf16[28,32,128]{2,1,0:T(8,128)(2,1)S(1)}, u32[]{:S(2)}, u32[]{:S(2)}) %collective-permute-start.12) | collective-permute-done | bytes 229408 | tf_op jit(solution)/shard_map/ppermute | solution.py:300
  39.1 2.7 %input.1 = (bf16[28,64,128]{2,1,0:T(8,128)(2,1)S(1)}, bf16[2,16,2048]{2,1,0:T(8,128)(2,1)S(1)}, bf16[16,2048]{1,0:T(8,128)(2,1)S(1)}, bf16[16,2048]{1,0:T(8,128)...) custom-call(s32[112]{0:T(128)S(1)} %bitcast.14, ...), custom_call_target="tpu_custom_call" | custom-call | flops 234881024 | bytes 3670016 | tf_op jit(solution)/shard_map/input/pallas_call | solution.py:303
  41.8 1.5 %collective-permute-start.13 = (bf16[2,16,2048]{2,1,0:T(8,128)(2,1)S(1)}, bf16[2,16,2048]{2,1,0:T(8,128)(2,1)S(1)}, u32[]{:S(2)}, u32[]{:S(2)}) collective-permute-start(bf16[2,16,2048]{2,1,0:T(8,128)(2,1)S(1)} %get-tuple-element.40), channel_id=1, source_target_pairs={{0,1},{1,0},{2,3},{3,2},{4,5},{5,4},{6,7},{7,6},{8,9},{9,8},{10,11... | collective-permute-start | bytes 393224 | tf_op jit(solution)/shard_map/ppermute | solution.py:300
  43.4 4.0 %collective-permute-done.13.refs_0_ = bf16[2,16,2048]{2,1,0:T(8,128)(2,1)S(1)} collective-permute-done((bf16[2,16,2048]{2,1,0:T(8,128)(2,1)S(1)}, bf16[2,16,2048]{2,1,0:T(8,128)(2,1)S(1)}, u32[]{:S(2)}, u32[]{:S(2)}) %collective-permute-start.13) | collective-permute-done | bytes 131104 | tf_op jit(solution)/shard_map/ppermute | solution.py:300
  47.5 2.7 %collective-permute-start.14 = (bf16[16,2048]{1,0:T(8,128)(2,1)S(1)}, bf16[16,2048]{1,0:T(8,128)(2,1)S(1)}, u32[]{:S(2)}, u32[]{:S(2)}) collective-permute-start(bf16[16,2048]{1,0:T(8,128)(2,1)S(1)} %get-tuple-element.47), channel_id=1, source_target_pairs={{0,6},{1,7},{2,4},{3,5},{4,2},{5,3},{6,0},{7,1},{8,14},{9,15},{10,... | collective-permute-start | bytes 196616 | tf_op jit(solution)/shard_map/ppermute | solution.py:300
  50.2 2.7 %collective-permute-start.16 = (bf16[16,2048]{1,0:T(8,128)(2,1)S(1)}, bf16[16,2048]{1,0:T(8,128)(2,1)S(1)}, u32[]{:S(2)}, u32[]{:S(2)}) collective-permute-start(bf16[16,2048]{1,0:T(8,128)(2,1)S(1)} %get-tuple-element.49), channel_id=1, source_target_pairs={{0,3},{1,2},{2,1},{3,0},{4,7},{5,6},{6,5},{7,4},{8,11},{9,10},{10,... | collective-permute-start | bytes 196616 | tf_op jit(solution)/shard_map/ppermute | solution.py:300
  52.9 0.5 collective-permute-start.18
  53.4 3.9 %up_grad.1 = (bf16[112,128,128]{2,1,0:T(8,128)(2,1)}, f32[8,128]{1,0:T(8,128)}) custom-call(s32[112]{0:T(128)S(1)} %bitcast.15, bf16[16,64,128]{2,1,0:T(8,128)(2,1)S(1)} %get-tuple-element.52.left_ref, bf16[28,64,128]{2,1,0:T(8,128)(2,1)S(1)} %get-tuple-element.53.right_ref), custom_call_target="tpu_custom_call" | custom-call | flops 234881024 | bytes 3670016 | tf_op jit(solution)/shard_map/up_grad/pallas_call | solution.py:303
  57.4 0.6 %fusion = (bf16[8,2048]{1,0:T(8,128)(2,1)}, bf16[8,2048]{1,0:T(8,128)(2,1)}) fusion(bf16[16,2048]{1,0:T(8,128)(2,1)S(1)} %add_convert_fusion.2), kind=kLoop, calls=%fused_computation.3 | loop fusion | bytes 131072 | tf_op jit(solution)/shard_map/slice | solution.py:460
  (28 shorter events, 0.6 us)
Async XLA Ops:
  0.6 22.2 %copy-start.2 = (s32[1,1,112]{2,1,0:T(1,128)S(1)}, s32[1,1,112]{2,1,0:T(1,128)}, u32[]{:S(2)}) copy-start(s32[1,1,112]{2,1,0:T(1,128)} %param.10) | copy-start | bytes 1348
  0.6 22.2 %copy-start = (bf16[1,1,112,128,128]{4,3,2,1,0:T(8,128)(2,1)S(1)}, bf16[1,1,112,128,128]{4,3,2,1,0:T(8,128)(2,1)}, u32[]{:S(2)}) copy-start(bf16[1,1,112,128,128]{4,3,2,1,0:T(8,128)(2,1)} %param.9) | copy-start | bytes 11010052
  1.6 8.6 %collective-permute-start.5 = (bf16[16,2048]{1,0:T(8,128)(2,1)S(1)}, bf16[16,2048]{1,0:T(8,128)(2,1)S(1)}, u32[]{:S(2)}, u32[]{:S(2)}) collective-permute-start(bf16[16,2048]{1,0:T(8,128)(2,1)S(1)} %pack.1.refs_0_), channel_id=1, source_target_pairs={{0,6},{1,7},{2,4},{3,5},{4,2},{5,3},{6,0},{7,1},{8,14},{9,15},{10,... | collective-permute-start | bytes 196616 | tf_op jit(solution)/shard_map/ppermute | solution.py:300
  6.7 5.7 %collective-permute-start.3 = (bf16[16,2048]{1,0:T(8,128)(2,1)S(1)}, bf16[16,2048]{1,0:T(8,128)(2,1)S(1)}, u32[]{:S(2)}, u32[]{:S(2)}) collective-permute-start(bf16[16,2048]{1,0:T(8,128)(2,1)S(1)} %pack.1.refs_0_), channel_id=1, source_target_pairs={{0,4},{1,5},{2,6},{3,7},{4,0},{5,1},{6,2},{7,3},{8,12},{9,13},{10,... | collective-permute-start | bytes 196616 | tf_op jit(solution)/shard_map/ppermute | solution.py:300
  6.7 7.2 %collective-permute-start.2 = (bf16[16,2048]{1,0:T(8,128)(2,1)S(1)}, bf16[16,2048]{1,0:T(8,128)(2,1)S(1)}, u32[]{:S(2)}, u32[]{:S(2)}) collective-permute-start(bf16[16,2048]{1,0:T(8,128)(2,1)S(1)} %pack.1.refs_0_), channel_id=1, source_target_pairs={{0,3},{1,2},{2,1},{3,0},{4,7},{5,6},{6,5},{7,4},{8,11},{9,10},{10,... | collective-permute-start | bytes 196616 | tf_op jit(solution)/shard_map/ppermute | solution.py:300
  8.4 5.6 %collective-permute-start.1 = (bf16[16,2048]{1,0:T(8,128)(2,1)S(1)}, bf16[16,2048]{1,0:T(8,128)(2,1)S(1)}, u32[]{:S(2)}, u32[]{:S(2)}) collective-permute-start(bf16[16,2048]{1,0:T(8,128)(2,1)S(1)} %pack.1.refs_0_), channel_id=1, source_target_pairs={{0,2},{1,3},{2,0},{3,1},{4,6},{5,7},{6,4},{7,5},{8,10},{9,11},{10,... | collective-permute-start | bytes 196616 | tf_op jit(solution)/shard_map/ppermute | solution.py:300
  9.7 4.6 %collective-permute-start = (bf16[16,2048]{1,0:T(8,128)(2,1)S(1)}, bf16[16,2048]{1,0:T(8,128)(2,1)S(1)}, u32[]{:S(2)}, u32[]{:S(2)}) collective-permute-start(bf16[16,2048]{1,0:T(8,128)(2,1)S(1)} %pack.1.refs_0_), channel_id=1, source_target_pairs={{0,1},{1,0},{2,3},{3,2},{4,5},{5,4},{6,7},{7,6},{8,9},{9,8},{10,11... | collective-permute-start | bytes 196616 | tf_op jit(solution)/shard_map/ppermute | solution.py:300
  10.2 5.0 %collective-permute-start.6 = (bf16[16,2048]{1,0:T(8,128)(2,1)S(1)}, bf16[16,2048]{1,0:T(8,128)(2,1)S(1)}, u32[]{:S(2)}, u32[]{:S(2)}) collective-permute-start(bf16[16,2048]{1,0:T(8,128)(2,1)S(1)} %collective-permute-done.5.refs_6_), channel_id=1, source_target_pairs={{0,1},{1,0},{2,3},{3,2},{4,5},{5,4},{6,7},{7,6},{8,9},{9,8},{10,11... | collective-permute-start | bytes 196616 | tf_op jit(solution)/shard_map/ppermute | solution.py:300
  12.4 4.3 %collective-permute-start.4 = (bf16[16,2048]{1,0:T(8,128)(2,1)S(1)}, bf16[16,2048]{1,0:T(8,128)(2,1)S(1)}, u32[]{:S(2)}, u32[]{:S(2)}) collective-permute-start(bf16[16,2048]{1,0:T(8,128)(2,1)S(1)} %collective-permute-done.3.refs_4_), channel_id=1, source_target_pairs={{0,1},{1,0},{2,3},{3,2},{4,5},{5,4},{6,7},{7,6},{8,9},{9,8},{10,11... | collective-permute-start | bytes 196616 | tf_op jit(solution)/shard_map/ppermute | solution.py:300
  19.6 1.6 %collective-permute-start.7 = (bf16[28,32,128]{2,1,0:T(8,128)(2,1)S(1)}, bf16[28,32,128]{2,1,0:T(8,128)(2,1)S(1)}, u32[]{:S(2)}, u32[]{:S(2)}) collective-permute-start(bf16[28,32,128]{2,1,0:T(8,128)(2,1)S(1)} %get-tuple-element.32), channel_id=1, source_target_pairs={{0,8},{8,0},{16,24},{24,16},{1,9},{9,1},{17,25},{25,17},{2,10},{10... | collective-permute-start | bytes 688136 | tf_op jit(solution)/shard_map/ppermute | solution.py:300
  21.2 7.7 %collective-permute-start.10 = (bf16[28,32,128]{2,1,0:T(8,128)(2,1)S(1)}, bf16[28,32,128]{2,1,0:T(8,128)(2,1)S(1)}, u32[]{:S(2)}, u32[]{:S(2)}) collective-permute-start(bf16[28,32,128]{2,1,0:T(8,128)(2,1)S(1)} %add_convert_fusion.1.after_ref.own_ref), channel_id=1, source_target_pairs={{0,16},{8,24},{16,0},{24,8},{1,17},{9,25},{17,1},{25,9},{2,18},{10... | collective-permute-start | bytes 688136 | tf_op jit(solution)/shard_map/ppermute | solution.py:300
  25.5 13.6 %copy-start.1 = (bf16[1,1,112,128,128]{4,3,2,1,0:T(8,128)(2,1)S(1)}, bf16[1,1,112,128,128]{4,3,2,1,0:T(8,128)(2,1)}, u32[]{:S(2)}) copy-start(bf16[1,1,112,128,128]{4,3,2,1,0:T(8,128)(2,1)} %param.7) | copy-start | bytes 11010052
  25.5 13.6 %copy-start.3 = (s32[1,1,112]{2,1,0:T(1,128)S(1)}, s32[1,1,112]{2,1,0:T(1,128)}, u32[]{:S(2)}) copy-start(s32[1,1,112]{2,1,0:T(1,128)} %param.8) | copy-start | bytes 1348
  25.5 3.8 %collective-permute-start.8 = (bf16[28,32,128]{2,1,0:T(8,128)(2,1)S(1)}, bf16[28,32,128]{2,1,0:T(8,128)(2,1)S(1)}, u32[]{:S(2)}, u32[]{:S(2)}) collective-permute-start(bf16[28,32,128]{2,1,0:T(8,128)(2,1)S(1)} %get-tuple-element.34), channel_id=1, source_target_pairs={{0,8},{8,0},{16,24},{24,16},{1,9},{9,1},{17,25},{25,17},{2,10},{10... | collective-permute-start | bytes 688136 | tf_op jit(solution)/shard_map/ppermute | solution.py:300
  29.3 1.8 %collective-permute-start.11 = (bf16[28,32,128]{2,1,0:T(8,128)(2,1)S(1)}, bf16[28,32,128]{2,1,0:T(8,128)(2,1)S(1)}, u32[]{:S(2)}, u32[]{:S(2)}) collective-permute-start(bf16[28,32,128]{2,1,0:T(8,128)(2,1)S(1)} %get-tuple-element.36.own_ref), channel_id=1, source_target_pairs={{0,8},{8,0},{16,24},{24,16},{1,9},{9,1},{17,25},{25,17},{2,10},{10... | collective-permute-start | bytes 688136 | tf_op jit(solution)/shard_map/ppermute | solution.py:300
  29.4 8.1 %collective-permute-start.9 = (bf16[28,32,128]{2,1,0:T(8,128)(2,1)S(1)}, bf16[28,32,128]{2,1,0:T(8,128)(2,1)S(1)}, u32[]{:S(2)}, u32[]{:S(2)}) collective-permute-start(bf16[28,32,128]{2,1,0:T(8,128)(2,1)S(1)} %add_convert_fusion.own_ref), channel_id=1, source_target_pairs={{0,16},{8,24},{16,0},{24,8},{1,17},{9,25},{17,1},{25,9},{2,18},{10... | collective-permute-start | bytes 688136 | tf_op jit(solution)/shard_map/ppermute | solution.py:300
  37.6 1.6 %collective-permute-start.12 = (bf16[28,32,128]{2,1,0:T(8,128)(2,1)S(1)}, bf16[28,32,128]{2,1,0:T(8,128)(2,1)S(1)}, u32[]{:S(2)}, u32[]{:S(2)}) collective-permute-start(bf16[28,32,128]{2,1,0:T(8,128)(2,1)S(1)} %slope.1.own_ref), channel_id=1, source_target_pairs={{0,8},{8,0},{16,24},{24,16},{1,9},{9,1},{17,25},{25,17},{2,10},{10... | collective-permute-start | bytes 688136 | tf_op jit(solution)/shard_map/ppermute | solution.py:300
  41.8 5.6 %collective-permute-start.13 = (bf16[2,16,2048]{2,1,0:T(8,128)(2,1)S(1)}, bf16[2,16,2048]{2,1,0:T(8,128)(2,1)S(1)}, u32[]{:S(2)}, u32[]{:S(2)}) collective-permute-start(bf16[2,16,2048]{2,1,0:T(8,128)(2,1)S(1)} %get-tuple-element.40), channel_id=1, source_target_pairs={{0,1},{1,0},{2,3},{3,2},{4,5},{5,4},{6,7},{7,6},{8,9},{9,8},{10,11... | collective-permute-start | bytes 393224 | tf_op jit(solution)/shard_map/ppermute | solution.py:300
  43.4 13.9 %collective-permute-start.17 = (bf16[16,2048]{1,0:T(8,128)(2,1)S(1)}, bf16[16,2048]{1,0:T(8,128)(2,1)S(1)}, u32[]{:S(2)}, u32[]{:S(2)}) collective-permute-start(bf16[16,2048]{1,0:T(8,128)(2,1)S(1)} %get-tuple-element.50), channel_id=1, source_target_pairs={{0,2},{1,3},{2,0},{3,1},{4,6},{5,7},{6,4},{7,5},{8,10},{9,11},{10,... | collective-permute-start | bytes 196616 | tf_op jit(solution)/shard_map/ppermute | solution.py:300
  47.5 9.8 %collective-permute-start.14 = (bf16[16,2048]{1,0:T(8,128)(2,1)S(1)}, bf16[16,2048]{1,0:T(8,128)(2,1)S(1)}, u32[]{:S(2)}, u32[]{:S(2)}) collective-permute-start(bf16[16,2048]{1,0:T(8,128)(2,1)S(1)} %get-tuple-element.47), channel_id=1, source_target_pairs={{0,6},{1,7},{2,4},{3,5},{4,2},{5,3},{6,0},{7,1},{8,14},{9,15},{10,... | collective-permute-start | bytes 196616 | tf_op jit(solution)/shard_map/ppermute | solution.py:300
  50.2 7.2 %collective-permute-start.15 = (bf16[16,2048]{1,0:T(8,128)(2,1)S(1)}, bf16[16,2048]{1,0:T(8,128)(2,1)S(1)}, u32[]{:S(2)}, u32[]{:S(2)}) collective-permute-start(bf16[16,2048]{1,0:T(8,128)(2,1)S(1)} %get-tuple-element.48), channel_id=1, source_target_pairs={{0,4},{1,5},{2,6},{3,7},{4,0},{5,1},{6,2},{7,3},{8,12},{9,13},{10,... | collective-permute-start | bytes 196616 | tf_op jit(solution)/shard_map/ppermute | solution.py:300
  50.2 7.2 %collective-permute-start.16 = (bf16[16,2048]{1,0:T(8,128)(2,1)S(1)}, bf16[16,2048]{1,0:T(8,128)(2,1)S(1)}, u32[]{:S(2)}, u32[]{:S(2)}) collective-permute-start(bf16[16,2048]{1,0:T(8,128)(2,1)S(1)} %get-tuple-element.49), channel_id=1, source_target_pairs={{0,3},{1,2},{2,1},{3,0},{4,7},{5,6},{6,5},{7,4},{8,11},{9,10},{10,... | collective-permute-start | bytes 196616 | tf_op jit(solution)/shard_map/ppermute | solution.py:300
  52.9 4.5 %collective-permute-start.18 = (bf16[16,2048]{1,0:T(8,128)(2,1)S(1)}, bf16[16,2048]{1,0:T(8,128)(2,1)S(1)}, u32[]{:S(2)}, u32[]{:S(2)}) collective-permute-start(bf16[16,2048]{1,0:T(8,128)(2,1)S(1)} %get-tuple-element.51), channel_id=1, source_target_pairs={{0,1},{1,0},{2,3},{3,2},{4,5},{5,4},{6,7},{7,6},{8,9},{9,8},{10,11... | collective-permute-start | bytes 196616 | tf_op jit(solution)/shard_map/ppermute | solution.py:300

commit v4 on v3

--- a/solution.py
+++ b/solution.py
@@ -173,7 +173,7 @@
 
 
 def act_kernel(
-    leading, trailing, index_ref, blocks_ref, cot_ref, after_ref, keep_ref, give_ref, turned, acc
+    leading, trailing, index_ref, blocks_ref, cot_ref, keep_ref, give_ref, turned, acc
 ):
     accumulate_turned(Held(index_ref, blocks_ref, 56), leading, trailing, cot_ref, turned, acc)
     half = keep_ref.shape[1]
@@ -184,19 +184,30 @@
     split_halves(core(), read, leading, keep_ref, give_ref)
 
 
-def join_halves(core, own_ref, other_ref, whole_ref):
-    half = own_ref.shape[1]
-    for at in range(own_ref.shape[0]):
-        own, other = own_ref[at], other_ref[at]
-        whole_ref[at, :half, :] = jnp.where(core == 0, own, other)
-        whole_ref[at, half:, :] = jnp.where(core == 0, other, own)
-
-
-def gelu_kernel(own_ref, other_ref, hidden_ref, slope_ref):
-    for at in range(own_ref.shape[0]):
-        preact = own_ref[at].astype(F32) + other_ref[at].astype(F32)
-        hidden_ref[at] = gelu_value(preact).astype(BF16)
-        slope_ref[at] = gelu_slope(preact)
+def join_halves(core, pieces, whole_ref):
+    half = whole_ref.shape[1] // 2
+    base = 0
+    for own_ref, other_ref in pieces:
+        for at in range(own_ref.shape[0]):
+            own, other = own_ref[at], other_ref[at]
+            whole_ref[base + at, :half, :] = jnp.where(core == 0, own, other)
+            whole_ref[base + at, half:, :] = jnp.where(core == 0, other, own)
+        base += own_ref.shape[0]
+
+
+def add_kernel(keep_ref, other_ref, after_ref, out_ref):
+    for at in range(keep_ref.shape[0]):
+        out_ref[at] = (keep_ref[at].astype(F32) + other_ref[at].astype(F32)).astype(BF16)
+
+
+def gelu_kernel(own_ref, other_ref, after_ref, slope_ref, *pieces):
+    base = 0
+    for hidden_ref in pieces:
+        for at in range(hidden_ref.shape[0]):
+            preact = own_ref[base + at].astype(F32) + other_ref[base + at].astype(F32)
+            hidden_ref[at] = gelu_value(preact).astype(BF16)
+            slope_ref[base + at] = gelu_slope(preact)
+        base += hidden_ref.shape[0]
 
 
 def slope_kernel(own_ref, other_ref, slope_ref, after_ref, grad_ref):
@@ -205,10 +216,9 @@
         grad_ref[at] = (act_grad * slope_ref[at]).astype(BF16)
 
 
-def down_kernel(
-    leading, trailing, index_ref, blocks_ref, own_ref, other_ref, hidden_ref, terms_ref, acc
-):
-    join_halves(core(), own_ref, other_ref, hidden_ref)
+def down_kernel(leading, trailing, index_ref, blocks_ref, *refs):
+    pieces, (hidden_ref, terms_ref, acc) = refs[:-3], refs[-3:]
+    join_halves(core(), list(zip(pieces[::2], pieces[1::2])), hidden_ref)
     accumulate(Held(index_ref, blocks_ref, 56), leading, trailing, hidden_ref, acc)
     for at in range(trailing):
         terms_ref[at] = acc[at].astype(BF16)
@@ -222,7 +232,7 @@
     leading, trailing, index_ref, blocks_ref, own_ref, other_ref, out_terms_ref, grad_ref, relay_ref, *refs
 ):
     chunks, turned, acc = refs[:-2], refs[-2], refs[-1]
-    join_halves(core(), own_ref, other_ref, grad_ref)
+    join_halves(core(), [(own_ref, other_ref)], grad_ref)
     accumulate_turned(Held(index_ref, blocks_ref, 56), leading, trailing, grad_ref, turned, acc)
     devices = relay_ref.shape[0] + len(chunks)
     rows = grad_ref.shape[1] // devices
@@ -342,9 +352,10 @@
     cols_turned = pltpu.VMEM((col_blocks, BS, tok_count), BF16)
     ANY = pl.BlockSpec(memory_space=pl.ANY)
 
-    def pair_sum(keep, give, cut=1):
-        parts = [swap(part, "row", 1) for part in jnp.split(give, cut)]
-        total = (keep.astype(F32) + jnp.concatenate(parts).astype(F32)).astype(BF16)
+    def pair_sum(keep, give, after):
+        total = call(
+            add_kernel, "add", half_cols, [VMEM, VMEM, ANY], [], keep, swap(give, "row", 1), after
+        )
         bit = 2
         while 2 * bit < row_devices:
             total = (total.astype(F32) + swap(total, "row", bit).astype(F32)).astype(BF16)
@@ -363,43 +374,43 @@
         *parts,
         cost_estimate=cost,
     )
-    pre_own = pair_sum(pre_keep, pre_give)
-    pre_other = swap(pre_own, "row", last)
-
     act_keep, act_give = call(
         functools.partial(act_kernel, col_blocks, row_blocks),
         "act",
         (half_cols, half_cols),
-        [SMEM, VMEM, VMEM, ANY],
+        [SMEM, VMEM, VMEM],
         [rows_turned, acc_cols_turned],
         down_place,
         down_weight,
         cotangents,
-        pre_own,
         cost_estimate=cost,
     )
-    act_own = pair_sum(act_keep, act_give)
+    pre_own = pair_sum(pre_keep, pre_give, act_keep)
+    pre_other = swap(pre_own, "row", last)
+    act_own = pair_sum(act_keep, act_give, act_keep)
     act_other = swap(act_own, "row", last)
 
-    hidden_own, slope = call(
+    cut = (col_blocks + 1) // 2
+    slope, *hidden_own = call(
         gelu_kernel,
         "gelu",
-        (half_cols, shape(col_blocks, half, BS, dtype=F32)),
-        [VMEM, VMEM],
+        (shape(col_blocks, half, BS, dtype=F32),)
+        + tuple(shape(count, half, BS) for count in (cut, col_blocks - cut)),
+        [VMEM, VMEM, ANY],
         [],
         pre_own,
         pre_other,
+        act_own,
     )
     hidden, out_terms = call(
         functools.partial(down_kernel, col_blocks, row_blocks),
         "down",
         (tile_cols, tile_rows),
-        [SMEM, VMEM, VMEM, VMEM],
+        [SMEM] + [VMEM] * (1 + 2 * len(hidden_own)),
         [acc_rows],
         down_place,
         down_weight,
-        hidden_own,
-        swap(hidden_own, "row", 1),
+        *(each for piece in hidden_own for each in (piece, swap(piece, "row", 1))),
         cost_estimate=cost,
     )
 
@@ -423,7 +434,7 @@
 
     down_grad, down_mark = grads("down_grad", down_place, hidden, cotangents)
     grad_own = call(
-        slope_kernel, "slope", half_cols, [VMEM] * 4, [], act_own, act_other, slope, down_mark
+        slope_kernel, "slope", half_cols, [VMEM] * 3 + [ANY], [], act_own, act_other, slope, out_terms
     )
     by_way = [bit for bit in range(col_devices) if relayed(bit)]
     direct = [bit for bit in range(col_devices) if not relayed(bit)]

time: 58.2 us -> 56.4 us (0.969)
  waiting for transfers between devices: 14.8 us -> 12.2 us
  starting transfers between devices: 22.6 us -> 23.4 us
    ppermute x19 -> x20, waiting for transfers between devices: 14.8 us -> 12.2 us  [swap(): return lax.ppermute(values, axis, [(at, at ^ bit) for at in range(count)])]
    ppermute x19 -> x20, starting transfers between devices: 22.6 us -> 23.4 us  [swap(): return lax.ppermute(values, axis, [(at, at ^ bit) for at in range(count)])]
    pallas_call x10 -> x12, Pallas kernels: 19 us -> 19 us  [call(): pl.pallas_call(body, out_shape=outs, in_specs=ins, out_specs=out_specs or...]
  transfers between devices with their start and end apart: 19 -> 20, of which waited for: 10 -> 11; matrix products, arithmetic and copies ran while one was open for 0% -> 0% of each run, Pallas kernels for 21% -> 22%
where the time goes in v4:
time: 56.4 us; the launch traced here: 56.2 us
  starting transfers between devices  23.4 us (41%)
  Pallas kernels  19 us (34%)
  waiting for transfers between devices  12.2 us (22%)
  between operations  0.83 us (1%)
  local copies, waits for them, and re-layouts  0.65 us (1%)
    ppermute x20, starting transfers between devices, swap(): return lax.ppermute(values, axis, [(at, at ^ bit) for at in range(count)])  23.4 us
    pallas_call x12, Pallas kernels, call(): pl.pallas_call(body, out_shape=outs, in_specs=ins, out_specs=out_specs or...  19 us
    ppermute x20, waiting for transfers between devices, swap(): return lax.ppermute(values, axis, [(at, at ^ bit) for at in range(count)])  12.2 us
  transfers between devices with their start and end apart: 20, of which 11 were waited for; matrix products, arithmetic and copies ran while one was open for 0% of the time, Pallas kernels for 22%

profile of v4, /device:TPU:0, one launch (start us, length us, event | category | flops | bytes accessed | tf_op | source)
XLA Modules:
  0.0 56.2 jit_solution(14797319926385172241)
XLA Ops:
  0.7 0.9 %pack.1.refs_0_ = bf16[16,2048]{1,0:T(8,128)(2,1)S(1)} custom-call(bf16[8,2048]{1,0:T(8,128)(2,1)} %tokens_ref.1, bf16[8,2048]{1,0:T(8,128)(2,1)} %cot_ref.1), custom_call_target="tpu_custom_call" | custom-call | bytes 33554432 | tf_op jit(solution)/shard_map/pack/pallas_call | solution.py:313
  1.6 5.1 %collective-permute-start.5 = (bf16[16,2048]{1,0:T(8,128)(2,1)S(1)}, bf16[16,2048]{1,0:T(8,128)(2,1)S(1)}, u32[]{:S(2)}, u32[]{:S(2)}) collective-permute-start(bf16[16,2048]{1,0:T(8,128)(2,1)S(1)} %pack.1.refs_0_), channel_id=1, source_target_pairs={{0,6},{1,7},{2,4},{3,5},{4,2},{5,3},{6,0},{7,1},{8,14},{9,15},{10,... | collective-permute-start | bytes 196616 | tf_op jit(solution)/shard_map/ppermute | solution.py:310
  6.7 1.7 %collective-permute-start.2 = (bf16[16,2048]{1,0:T(8,128)(2,1)S(1)}, bf16[16,2048]{1,0:T(8,128)(2,1)S(1)}, u32[]{:S(2)}, u32[]{:S(2)}) collective-permute-start(bf16[16,2048]{1,0:T(8,128)(2,1)S(1)} %pack.1.refs_0_), channel_id=1, source_target_pairs={{0,3},{1,2},{2,1},{3,0},{4,7},{5,6},{6,5},{7,4},{8,11},{9,10},{10,... | collective-permute-start | bytes 196616 | tf_op jit(solution)/shard_map/ppermute | solution.py:310
  8.4 1.2 %collective-permute-start.1 = (bf16[16,2048]{1,0:T(8,128)(2,1)S(1)}, bf16[16,2048]{1,0:T(8,128)(2,1)S(1)}, u32[]{:S(2)}, u32[]{:S(2)}) collective-permute-start(bf16[16,2048]{1,0:T(8,128)(2,1)S(1)} %pack.1.refs_0_), channel_id=1, source_target_pairs={{0,2},{1,3},{2,0},{3,1},{4,6},{5,7},{6,4},{7,5},{8,10},{9,11},{10,... | collective-permute-start | bytes 196616 | tf_op jit(solution)/shard_map/ppermute | solution.py:310
  9.7 0.5 collective-permute-start
  10.2 1.5 %collective-permute-start.6 = (bf16[16,2048]{1,0:T(8,128)(2,1)S(1)}, bf16[16,2048]{1,0:T(8,128)(2,1)S(1)}, u32[]{:S(2)}, u32[]{:S(2)}) collective-permute-start(bf16[16,2048]{1,0:T(8,128)(2,1)S(1)} %collective-permute-done.5.refs_6_), channel_id=1, source_target_pairs={{0,1},{1,0},{2,3},{3,2},{4,5},{5,4},{6,7},{7,6},{8,9},{9,8},{10,11... | collective-permute-start | bytes 196616 | tf_op jit(solution)/shard_map/ppermute | solution.py:310
  11.7 0.7 %collective-permute-done.3.refs_4_ = bf16[16,2048]{1,0:T(8,128)(2,1)S(1)} collective-permute-done((bf16[16,2048]{1,0:T(8,128)(2,1)S(1)}, bf16[16,2048]{1,0:T(8,128)(2,1)S(1)}, u32[]{:S(2)}, u32[]{:S(2)}) %collective-permute-start.3) | collective-permute-done | bytes 65568 | tf_op jit(solution)/shard_map/ppermute | solution.py:310
  12.4 1.5 %collective-permute-start.4 = (bf16[16,2048]{1,0:T(8,128)(2,1)S(1)}, bf16[16,2048]{1,0:T(8,128)(2,1)S(1)}, u32[]{:S(2)}, u32[]{:S(2)}) collective-permute-start(bf16[16,2048]{1,0:T(8,128)(2,1)S(1)} %collective-permute-done.3.refs_4_), channel_id=1, source_target_pairs={{0,1},{1,0},{2,3},{3,2},{4,5},{5,4},{6,7},{7,6},{8,9},{9,8},{10,11... | collective-permute-start | bytes 196616 | tf_op jit(solution)/shard_map/ppermute | solution.py:310
  14.0 0.2 collective-permute-done.refs_1_
  14.2 1.0 %collective-permute-done.6.refs_7_ = bf16[16,2048]{1,0:T(8,128)(2,1)S(1)} collective-permute-done((bf16[16,2048]{1,0:T(8,128)(2,1)S(1)}, bf16[16,2048]{1,0:T(8,128)(2,1)S(1)}, u32[]{:S(2)}, u32[]{:S(2)}) %collective-permute-start.6) | collective-permute-done | bytes 65568 | tf_op jit(solution)/shard_map/ppermute | solution.py:310
  15.3 1.4 %collective-permute-done.4.refs_5_ = bf16[16,2048]{1,0:T(8,128)(2,1)S(1)} collective-permute-done((bf16[16,2048]{1,0:T(8,128)(2,1)S(1)}, bf16[16,2048]{1,0:T(8,128)(2,1)S(1)}, u32[]{:S(2)}, u32[]{:S(2)}) %collective-permute-start.4) | collective-permute-done | bytes 65568 | tf_op jit(solution)/shard_map/ppermute | solution.py:310
  16.7 2.9 %up.1 = (bf16[16,64,128]{2,1,0:T(8,128)(2,1)S(1)}, bf16[16,64,128]{2,1,0:T(8,128)(2,1)S(1)}, bf16[28,32,128]{2,1,0:T(8,128)(2,1)S(1)}, bf16[28,32,128]{2,1,0:T(8,128)(2,1)S(1)}) custom-call(s32[112]{0:T(128)} %bitcast.13, bf16[112,128,128]{2,1,0:T(8,128)(2,1)} %bitcast.8, bf16[16,2048]{1,0:T(8,128)(2,1)S(1)} %pack.1.refs_0_, ...), custom_call_target="tpu_custom_call" | custom-call | flops 234881024 | bytes 3670016 | tf_op jit(solution)/shard_map/up/pallas_call | solution.py:313
  19.7 2.7 %act.1 = (bf16[28,32,128]{2,1,0:T(8,128)(2,1)S(1)}, bf16[28,32,128]{2,1,0:T(8,128)(2,1)S(1)}) custom-call(s32[112]{0:T(128)S(1)} %bitcast.10, bf16[112,128,128]{2,1,0:T(8,128)(2,1)S(1)} %bitcast.6, bf16[16,64,128]{2,1,0:T(8,128)(2,1)S(1)} %get-tuple-element.31.cot_ref.right_ref), custom_call_target="tpu_custom_call" | custom-call | flops 234881024 | bytes 3670016 | tf_op jit(solution)/shard_map/act/pallas_call | solution.py:313
  22.4 0.5 collective-permute-start.7
  23.0 1.6 %collective-permute-start.10 = (bf16[28,32,128]{2,1,0:T(8,128)(2,1)S(1)}, bf16[28,32,128]{2,1,0:T(8,128)(2,1)S(1)}, u32[]{:S(2)}, u32[]{:S(2)}) collective-permute-start(bf16[28,32,128]{2,1,0:T(8,128)(2,1)S(1)} %add.28.own_ref), channel_id=1, source_target_pairs={{0,16},{8,24},{16,0},{24,8},{1,17},{9,25},{17,1},{25,9},{2,18},{10... | collective-permute-start | bytes 688136 | tf_op jit(solution)/shard_map/ppermute | solution.py:310
  24.7 1.0 %collective-permute-start.8 = (bf16[28,32,128]{2,1,0:T(8,128)(2,1)S(1)}, bf16[28,32,128]{2,1,0:T(8,128)(2,1)S(1)}, u32[]{:S(2)}, u32[]{:S(2)}) collective-permute-start(bf16[28,32,128]{2,1,0:T(8,128)(2,1)S(1)} %add.27.after_ref.own_ref), channel_id=1, source_target_pairs={{0,16},{8,24},{16,0},{24,8},{1,17},{9,25},{17,1},{25,9},{2,18},{10... | collective-permute-start | bytes 688136 | tf_op jit(solution)/shard_map/ppermute | solution.py:310
  25.7 5.8 %collective-permute-done.10.other_ref = bf16[28,32,128]{2,1,0:T(8,128)(2,1)S(1)} collective-permute-done((bf16[28,32,128]{2,1,0:T(8,128)(2,1)S(1)}, bf16[28,32,128]{2,1,0:T(8,128)(2,1)S(1)}, u32[]{:S(2)}, u32[]{:S(2)}) %collective-permute-start.10) | collective-permute-done | bytes 229408 | tf_op jit(solution)/shard_map/ppermute | solution.py:310
  31.5 0.3 gelu.1
  31.9 0.5 collective-permute-start.12
  32.4 0.8 %collective-permute-done.11.refs_1_ = bf16[14,32,128]{2,1,0:T(8,128)(2,1)S(1)} collective-permute-done((bf16[14,32,128]{2,1,0:T(8,128)(2,1)S(1)}, bf16[14,32,128]{2,1,0:T(8,128)(2,1)S(1)}, u32[]{:S(2)}, u32[]{:S(2)}) %collective-permute-start.11) | collective-permute-done | bytes 114720 | tf_op jit(solution)/shard_map/ppermute | solution.py:310
  33.4 2.0 %down.1 = (bf16[28,64,128]{2,1,0:T(8,128)(2,1)S(1)}, bf16[16,64,128]{2,1,0:T(8,128)(2,1)S(1)}) custom-call(s32[112]{0:T(128)S(1)} %bitcast.11, bf16[112,128,128]{2,1,0:T(8,128)(2,1)S(1)} %bitcast.7, bf16[14,32,128]{2,1,0:T(8,128)(2,1)S(1)} %get-tuple-element.37.refs_0_, bf16[14,32,128]{2,1,0:T(8,128)(2,1)S(1)} %collective-permute-done.11.refs_1_, ...), custom_call_target="tpu_custom_call" | custom-call | flops 234881024 | bytes 3670016 | tf_op jit(solution)/shard_map/down/pallas_call | solution.py:313
  35.6 0.4 collective-permute-start.13
  35.9 1.2 %collective-permute-done.13.other_ref = bf16[28,32,128]{2,1,0:T(8,128)(2,1)S(1)} collective-permute-done((bf16[28,32,128]{2,1,0:T(8,128)(2,1)S(1)}, bf16[28,32,128]{2,1,0:T(8,128)(2,1)S(1)}, u32[]{:S(2)}, u32[]{:S(2)}) %collective-permute-start.13) | collective-permute-done | bytes 229408 | tf_op jit(solution)/shard_map/ppermute | solution.py:310
  37.2 2.7 %input.1 = (bf16[28,64,128]{2,1,0:T(8,128)(2,1)S(1)}, bf16[2,16,2048]{2,1,0:T(8,128)(2,1)S(1)}, bf16[16,2048]{1,0:T(8,128)(2,1)S(1)}, bf16[16,2048]{1,0:T(8,128)...) custom-call(s32[112]{0:T(128)S(1)} %bitcast.14, ...), custom_call_target="tpu_custom_call" | custom-call | flops 234881024 | bytes 3670016 | tf_op jit(solution)/shard_map/input/pallas_call | solution.py:313
  39.8 1.6 %collective-permute-start.14 = (bf16[2,16,2048]{2,1,0:T(8,128)(2,1)S(1)}, bf16[2,16,2048]{2,1,0:T(8,128)(2,1)S(1)}, u32[]{:S(2)}, u32[]{:S(2)}) collective-permute-start(bf16[2,16,2048]{2,1,0:T(8,128)(2,1)S(1)} %get-tuple-element.40), channel_id=1, source_target_pairs={{0,1},{1,0},{2,3},{3,2},{4,5},{5,4},{6,7},{7,6},{8,9},{9,8},{10,11... | collective-permute-start | bytes 393224 | tf_op jit(solution)/shard_map/ppermute | solution.py:310
  41.4 3.4 %down_grad.1 = (bf16[112,128,128]{2,1,0:T(8,128)(2,1)}, f32[8,128]{1,0:T(8,128)S(1)}) custom-call(s32[112]{0:T(128)S(1)} %bitcast.12, bf16[28,64,128]{2,1,0:T(8,128)(2,1)S(1)} %get-tuple-element.41.left_ref, bf16[16,64,128]{2,1,0:T(8,128)(2,1)S(1)} %get-tuple-element.31.cot_ref.right_ref), custom_call_target="tpu_custom_call" | custom-call | flops 234881024 | bytes 3670016 | tf_op jit(solution)/shard_map/down_grad/pallas_call | solution.py:313
  44.9 0.7 %collective-permute-done.14.refs_0_ = bf16[2,16,2048]{2,1,0:T(8,128)(2,1)S(1)} collective-permute-done((bf16[2,16,2048]{2,1,0:T(8,128)(2,1)S(1)}, bf16[2,16,2048]{2,1,0:T(8,128)(2,1)S(1)}, u32[]{:S(2)}, u32[]{:S(2)}) %collective-permute-start.14) | collective-permute-done | bytes 131104 | tf_op jit(solution)/shard_map/ppermute | solution.py:310
  45.6 2.7 %collective-permute-start.15 = (bf16[16,2048]{1,0:T(8,128)(2,1)S(1)}, bf16[16,2048]{1,0:T(8,128)(2,1)S(1)}, u32[]{:S(2)}, u32[]{:S(2)}) collective-permute-start(bf16[16,2048]{1,0:T(8,128)(2,1)S(1)} %get-tuple-element.49), channel_id=1, source_target_pairs={{0,6},{1,7},{2,4},{3,5},{4,2},{5,3},{6,0},{7,1},{8,14},{9,15},{10,... | collective-permute-start | bytes 196616 | tf_op jit(solution)/shard_map/ppermute | solution.py:310
  48.5 2.6 %collective-permute-start.17 = (bf16[16,2048]{1,0:T(8,128)(2,1)S(1)}, bf16[16,2048]{1,0:T(8,128)(2,1)S(1)}, u32[]{:S(2)}, u32[]{:S(2)}) collective-permute-start(bf16[16,2048]{1,0:T(8,128)(2,1)S(1)} %get-tuple-element.51), channel_id=1, source_target_pairs={{0,3},{1,2},{2,1},{3,0},{4,7},{5,6},{6,5},{7,4},{8,11},{9,10},{10,... | collective-permute-start | bytes 196616 | tf_op jit(solution)/shard_map/ppermute | solution.py:310
  51.1 0.5 collective-permute-start.19
  51.6 3.9 %up_grad.1 = (bf16[112,128,128]{2,1,0:T(8,128)(2,1)}, f32[8,128]{1,0:T(8,128)}) custom-call(s32[112]{0:T(128)S(1)} %bitcast.15, bf16[16,64,128]{2,1,0:T(8,128)(2,1)S(1)} %get-tuple-element.54.left_ref, bf16[28,64,128]{2,1,0:T(8,128)(2,1)S(1)} %get-tuple-element.55.right_ref), custom_call_target="tpu_custom_call" | custom-call | flops 234881024 | bytes 3670016 | tf_op jit(solution)/shard_map/up_grad/pallas_call | solution.py:313
  55.6 0.6 %fusion = (bf16[8,2048]{1,0:T(8,128)(2,1)}, bf16[8,2048]{1,0:T(8,128)(2,1)}) fusion(bf16[16,2048]{1,0:T(8,128)(2,1)S(1)} %add_convert_fusion), kind=kLoop, calls=%fused_computation.1 | loop fusion | bytes 131072 | tf_op jit(solution)/shard_map/slice | solution.py:471
  (30 shorter events, 1.0 us)
Async XLA Ops:
  0.6 19.0 %copy-start.2 = (s32[1,1,112]{2,1,0:T(1,128)S(1)}, s32[1,1,112]{2,1,0:T(1,128)}, u32[]{:S(2)}) copy-start(s32[1,1,112]{2,1,0:T(1,128)} %param.10) | copy-start | bytes 1348
  0.6 19.0 %copy-start = (bf16[1,1,112,128,128]{4,3,2,1,0:T(8,128)(2,1)S(1)}, bf16[1,1,112,128,128]{4,3,2,1,0:T(8,128)(2,1)}, u32[]{:S(2)}) copy-start(bf16[1,1,112,128,128]{4,3,2,1,0:T(8,128)(2,1)} %param.9) | copy-start | bytes 11010052
  1.6 8.6 %collective-permute-start.5 = (bf16[16,2048]{1,0:T(8,128)(2,1)S(1)}, bf16[16,2048]{1,0:T(8,128)(2,1)S(1)}, u32[]{:S(2)}, u32[]{:S(2)}) collective-permute-start(bf16[16,2048]{1,0:T(8,128)(2,1)S(1)} %pack.1.refs_0_), channel_id=1, source_target_pairs={{0,6},{1,7},{2,4},{3,5},{4,2},{5,3},{6,0},{7,1},{8,14},{9,15},{10,... | collective-permute-start | bytes 196616 | tf_op jit(solution)/shard_map/ppermute | solution.py:310
  6.7 5.7 %collective-permute-start.3 = (bf16[16,2048]{1,0:T(8,128)(2,1)S(1)}, bf16[16,2048]{1,0:T(8,128)(2,1)S(1)}, u32[]{:S(2)}, u32[]{:S(2)}) collective-permute-start(bf16[16,2048]{1,0:T(8,128)(2,1)S(1)} %pack.1.refs_0_), channel_id=1, source_target_pairs={{0,4},{1,5},{2,6},{3,7},{4,0},{5,1},{6,2},{7,3},{8,12},{9,13},{10,... | collective-permute-start | bytes 196616 | tf_op jit(solution)/shard_map/ppermute | solution.py:310
  6.7 7.2 %collective-permute-start.2 = (bf16[16,2048]{1,0:T(8,128)(2,1)S(1)}, bf16[16,2048]{1,0:T(8,128)(2,1)S(1)}, u32[]{:S(2)}, u32[]{:S(2)}) collective-permute-start(bf16[16,2048]{1,0:T(8,128)(2,1)S(1)} %pack.1.refs_0_), channel_id=1, source_target_pairs={{0,3},{1,2},{2,1},{3,0},{4,7},{5,6},{6,5},{7,4},{8,11},{9,10},{10,... | collective-permute-start | bytes 196616 | tf_op jit(solution)/shard_map/ppermute | solution.py:310
  8.4 5.6 %collective-permute-start.1 = (bf16[16,2048]{1,0:T(8,128)(2,1)S(1)}, bf16[16,2048]{1,0:T(8,128)(2,1)S(1)}, u32[]{:S(2)}, u32[]{:S(2)}) collective-permute-start(bf16[16,2048]{1,0:T(8,128)(2,1)S(1)} %pack.1.refs_0_), channel_id=1, source_target_pairs={{0,2},{1,3},{2,0},{3,1},{4,6},{5,7},{6,4},{7,5},{8,10},{9,11},{10,... | collective-permute-start | bytes 196616 | tf_op jit(solution)/shard_map/ppermute | solution.py:310
  9.7 4.6 %collective-permute-start = (bf16[16,2048]{1,0:T(8,128)(2,1)S(1)}, bf16[16,2048]{1,0:T(8,128)(2,1)S(1)}, u32[]{:S(2)}, u32[]{:S(2)}) collective-permute-start(bf16[16,2048]{1,0:T(8,128)(2,1)S(1)} %pack.1.refs_0_), channel_id=1, source_target_pairs={{0,1},{1,0},{2,3},{3,2},{4,5},{5,4},{6,7},{7,6},{8,9},{9,8},{10,11... | collective-permute-start | bytes 196616 | tf_op jit(solution)/shard_map/ppermute | solution.py:310
  10.2 5.0 %collective-permute-start.6 = (bf16[16,2048]{1,0:T(8,128)(2,1)S(1)}, bf16[16,2048]{1,0:T(8,128)(2,1)S(1)}, u32[]{:S(2)}, u32[]{:S(2)}) collective-permute-start(bf16[16,2048]{1,0:T(8,128)(2,1)S(1)} %collective-permute-done.5.refs_6_), channel_id=1, source_target_pairs={{0,1},{1,0},{2,3},{3,2},{4,5},{5,4},{6,7},{7,6},{8,9},{9,8},{10,11... | collective-permute-start | bytes 196616 | tf_op jit(solution)/shard_map/ppermute | solution.py:310
  12.4 4.3 %collective-permute-start.4 = (bf16[16,2048]{1,0:T(8,128)(2,1)S(1)}, bf16[16,2048]{1,0:T(8,128)(2,1)S(1)}, u32[]{:S(2)}, u32[]{:S(2)}) collective-permute-start(bf16[16,2048]{1,0:T(8,128)(2,1)S(1)} %collective-permute-done.3.refs_4_), channel_id=1, source_target_pairs={{0,1},{1,0},{2,3},{3,2},{4,5},{5,4},{6,7},{7,6},{8,9},{9,8},{10,11... | collective-permute-start | bytes 196616 | tf_op jit(solution)/shard_map/ppermute | solution.py:310
  19.6 3.3 %collective-permute-start.9 = (bf16[28,32,128]{2,1,0:T(8,128)(2,1)S(1)}, bf16[28,32,128]{2,1,0:T(8,128)(2,1)S(1)}, u32[]{:S(2)}, u32[]{:S(2)}) collective-permute-start(bf16[28,32,128]{2,1,0:T(8,128)(2,1)S(1)} %get-tuple-element.35), channel_id=1, source_target_pairs={{0,8},{8,0},{16,24},{24,16},{1,9},{9,1},{17,25},{25,17},{2,10},{10... | collective-permute-start | bytes 688136 | tf_op jit(solution)/shard_map/ppermute | solution.py:310
  22.4 2.2 %collective-permute-start.7 = (bf16[28,32,128]{2,1,0:T(8,128)(2,1)S(1)}, bf16[28,32,128]{2,1,0:T(8,128)(2,1)S(1)}, u32[]{:S(2)}, u32[]{:S(2)}) collective-permute-start(bf16[28,32,128]{2,1,0:T(8,128)(2,1)S(1)} %get-tuple-element.33), channel_id=1, source_target_pairs={{0,8},{8,0},{16,24},{24,16},{1,9},{9,1},{17,25},{25,17},{2,10},{10... | collective-permute-start | bytes 688136 | tf_op jit(solution)/shard_map/ppermute | solution.py:310
  23.0 14.2 %copy-start.1 = (bf16[1,1,112,128,128]{4,3,2,1,0:T(8,128)(2,1)S(1)}, bf16[1,1,112,128,128]{4,3,2,1,0:T(8,128)(2,1)}, u32[]{:S(2)}) copy-start(bf16[1,1,112,128,128]{4,3,2,1,0:T(8,128)(2,1)} %param.7) | copy-start | bytes 11010052
  23.0 14.2 %copy-start.3 = (s32[1,1,112]{2,1,0:T(1,128)S(1)}, s32[1,1,112]{2,1,0:T(1,128)}, u32[]{:S(2)}) copy-start(s32[1,1,112]{2,1,0:T(1,128)} %param.8) | copy-start | bytes 1348
  23.0 8.5 %collective-permute-start.10 = (bf16[28,32,128]{2,1,0:T(8,128)(2,1)S(1)}, bf16[28,32,128]{2,1,0:T(8,128)(2,1)S(1)}, u32[]{:S(2)}, u32[]{:S(2)}) collective-permute-start(bf16[28,32,128]{2,1,0:T(8,128)(2,1)S(1)} %add.28.own_ref), channel_id=1, source_target_pairs={{0,16},{8,24},{16,0},{24,8},{1,17},{9,25},{17,1},{25,9},{2,18},{10... | collective-permute-start | bytes 688136 | tf_op jit(solution)/shard_map/ppermute | solution.py:310
  24.7 10.8 %collective-permute-start.8 = (bf16[28,32,128]{2,1,0:T(8,128)(2,1)S(1)}, bf16[28,32,128]{2,1,0:T(8,128)(2,1)S(1)}, u32[]{:S(2)}, u32[]{:S(2)}) collective-permute-start(bf16[28,32,128]{2,1,0:T(8,128)(2,1)S(1)} %add.27.after_ref.own_ref), channel_id=1, source_target_pairs={{0,16},{8,24},{16,0},{24,8},{1,17},{9,25},{17,1},{25,9},{2,18},{10... | collective-permute-start | bytes 688136 | tf_op jit(solution)/shard_map/ppermute | solution.py:310
  31.9 1.4 %collective-permute-start.11 = (bf16[14,32,128]{2,1,0:T(8,128)(2,1)S(1)}, bf16[14,32,128]{2,1,0:T(8,128)(2,1)S(1)}, u32[]{:S(2)}, u32[]{:S(2)}) collective-permute-start(bf16[14,32,128]{2,1,0:T(8,128)(2,1)S(1)} %get-tuple-element.37.refs_0_), channel_id=1, source_target_pairs={{0,8},{8,0},{16,24},{24,16},{1,9},{9,1},{17,25},{25,17},{2,10},{10... | collective-permute-start | bytes 344072 | tf_op jit(solution)/shard_map/ppermute | solution.py:310
  31.9 1.5 %collective-permute-start.12 = (bf16[14,32,128]{2,1,0:T(8,128)(2,1)S(1)}, bf16[14,32,128]{2,1,0:T(8,128)(2,1)S(1)}, u32[]{:S(2)}, u32[]{:S(2)}) collective-permute-start(bf16[14,32,128]{2,1,0:T(8,128)(2,1)S(1)} %get-tuple-element.38.refs_2_), channel_id=1, source_target_pairs={{0,8},{8,0},{16,24},{24,16},{1,9},{9,1},{17,25},{25,17},{2,10},{10... | collective-permute-start | bytes 344072 | tf_op jit(solution)/shard_map/ppermute | solution.py:310
  35.6 1.6 %collective-permute-start.13 = (bf16[28,32,128]{2,1,0:T(8,128)(2,1)S(1)}, bf16[28,32,128]{2,1,0:T(8,128)(2,1)S(1)}, u32[]{:S(2)}, u32[]{:S(2)}) collective-permute-start(bf16[28,32,128]{2,1,0:T(8,128)(2,1)S(1)} %slope.1.own_ref), channel_id=1, source_target_pairs={{0,8},{8,0},{16,24},{24,16},{1,9},{9,1},{17,25},{25,17},{2,10},{10... | collective-permute-start | bytes 688136 | tf_op jit(solution)/shard_map/ppermute | solution.py:310
  39.8 5.8 %collective-permute-start.14 = (bf16[2,16,2048]{2,1,0:T(8,128)(2,1)S(1)}, bf16[2,16,2048]{2,1,0:T(8,128)(2,1)S(1)}, u32[]{:S(2)}, u32[]{:S(2)}) collective-permute-start(bf16[2,16,2048]{2,1,0:T(8,128)(2,1)S(1)} %get-tuple-element.40), channel_id=1, source_target_pairs={{0,1},{1,0},{2,3},{3,2},{4,5},{5,4},{6,7},{7,6},{8,9},{9,8},{10,11... | collective-permute-start | bytes 393224 | tf_op jit(solution)/shard_map/ppermute | solution.py:310
  44.8 10.7 %collective-permute-start.18 = (bf16[16,2048]{1,0:T(8,128)(2,1)S(1)}, bf16[16,2048]{1,0:T(8,128)(2,1)S(1)}, u32[]{:S(2)}, u32[]{:S(2)}) collective-permute-start(bf16[16,2048]{1,0:T(8,128)(2,1)S(1)} %get-tuple-element.52), channel_id=1, source_target_pairs={{0,2},{1,3},{2,0},{3,1},{4,6},{5,7},{6,4},{7,5},{8,10},{9,11},{10,... | collective-permute-start | bytes 196616 | tf_op jit(solution)/shard_map/ppermute | solution.py:310
  45.6 9.8 %collective-permute-start.15 = (bf16[16,2048]{1,0:T(8,128)(2,1)S(1)}, bf16[16,2048]{1,0:T(8,128)(2,1)S(1)}, u32[]{:S(2)}, u32[]{:S(2)}) collective-permute-start(bf16[16,2048]{1,0:T(8,128)(2,1)S(1)} %get-tuple-element.49), channel_id=1, source_target_pairs={{0,6},{1,7},{2,4},{3,5},{4,2},{5,3},{6,0},{7,1},{8,14},{9,15},{10,... | collective-permute-start | bytes 196616 | tf_op jit(solution)/shard_map/ppermute | solution.py:310
  48.4 7.1 %collective-permute-start.16 = (bf16[16,2048]{1,0:T(8,128)(2,1)S(1)}, bf16[16,2048]{1,0:T(8,128)(2,1)S(1)}, u32[]{:S(2)}, u32[]{:S(2)}) collective-permute-start(bf16[16,2048]{1,0:T(8,128)(2,1)S(1)} %get-tuple-element.50), channel_id=1, source_target_pairs={{0,4},{1,5},{2,6},{3,7},{4,0},{5,1},{6,2},{7,3},{8,12},{9,13},{10,... | collective-permute-start | bytes 196616 | tf_op jit(solution)/shard_map/ppermute | solution.py:310
  48.5 7.0 %collective-permute-start.17 = (bf16[16,2048]{1,0:T(8,128)(2,1)S(1)}, bf16[16,2048]{1,0:T(8,128)(2,1)S(1)}, u32[]{:S(2)}, u32[]{:S(2)}) collective-permute-start(bf16[16,2048]{1,0:T(8,128)(2,1)S(1)} %get-tuple-element.51), channel_id=1, source_target_pairs={{0,3},{1,2},{2,1},{3,0},{4,7},{5,6},{6,5},{7,4},{8,11},{9,10},{10,... | collective-permute-start | bytes 196616 | tf_op jit(solution)/shard_map/ppermute | solution.py:310
  51.1 4.4 %collective-permute-start.19 = (bf16[16,2048]{1,0:T(8,128)(2,1)S(1)}, bf16[16,2048]{1,0:T(8,128)(2,1)S(1)}, u32[]{:S(2)}, u32[]{:S(2)}) collective-permute-start(bf16[16,2048]{1,0:T(8,128)(2,1)S(1)} %get-tuple-element.53), channel_id=1, source_target_pairs={{0,1},{1,0},{2,3},{3,2},{4,5},{5,4},{6,7},{7,6},{8,9},{9,8},{10,11... | collective-permute-start | bytes 196616 | tf_op jit(solution)/shard_map/ppermute | solution.py:310

commit v5 on v4

--- a/solution.py
+++ b/solution.py
@@ -126,12 +126,13 @@
     lax.fori_loop(0, source.blocks.shape[0] // source.step, group, 0)
 
 
-def split_halves(core, read, targets, keep_ref, give_ref):
+def split_halves(core, read, targets, keep_ref, gives):
     half = keep_ref.shape[1]
-    for at in range(targets):
+    places = [(give_ref, at) for give_ref in gives for at in range(give_ref.shape[0])]
+    for at, (give_ref, place) in zip(range(targets), places):
         low, high = read(at, 0), read(at, half)
         keep_ref[at] = jnp.where(core == 0, low, high).astype(BF16)
-        give_ref[at] = jnp.where(core == 0, high, low).astype(BF16)
+        give_ref[place] = jnp.where(core == 0, high, low).astype(BF16)
 
 
 def position(axis):
@@ -154,10 +155,21 @@
     mine_ref[...] = jnp.concatenate([held[0].astype(F32), held[1].astype(F32)]).astype(BF16)
 
 
-def up_kernel(leading, trailing, index_hbm, blocks_hbm, *refs):
-    parts = refs[:-9]
-    tokens_ref, cot_ref, keep_ref, give_ref, acc = refs[-9:-4]
-    source = Stream(index_hbm, blocks_hbm, *refs[-4:])
+def fetch_kernel(index_hbm, blocks_hbm, after_ref, index_ref, blocks_ref, sems):
+    copies = [
+        pltpu.make_async_copy(source, target, sems.at[at])
+        for at, (source, target) in enumerate(((index_hbm, index_ref), (blocks_hbm, blocks_ref)))
+    ]
+    for copy in copies:
+        copy.start()
+    for copy in copies:
+        copy.wait()
+
+
+def up_kernel(leading, trailing, index_ref, blocks_ref, *refs):
+    parts = refs[:-5]
+    tokens_ref, cot_ref, keep_ref, give_ref, acc = refs[-5:]
+    source = Held(index_ref, blocks_ref, 56)
     rows = parts[0].shape[0] // 2
     for pair in range(len(parts) // 2):
         here = pl.ds(pair * 2 * rows, 2 * rows)
@@ -169,19 +181,20 @@
             cot_ref[at, here, :] = jnp.concatenate([first[rows:], second[rows:]]).astype(BF16)
     accumulate(source, leading, trailing, tokens_ref, acc)
     half = keep_ref.shape[1]
-    split_halves(core(), lambda at, low: acc[at, low : low + half, :], trailing, keep_ref, give_ref)
+    split_halves(core(), lambda at, low: acc[at, low : low + half, :], trailing, keep_ref, [give_ref])
 
 
 def act_kernel(
-    leading, trailing, index_ref, blocks_ref, cot_ref, keep_ref, give_ref, turned, acc
+    leading, trailing, index_ref, blocks_ref, cot_ref, keep_ref, *refs
 ):
+    gives, (turned, acc) = refs[:-2], refs[-2:]
     accumulate_turned(Held(index_ref, blocks_ref, 56), leading, trailing, cot_ref, turned, acc)
     half = keep_ref.shape[1]
 
     def read(at, low):
         return acc[at].T[low : low + half]
 
-    split_halves(core(), read, leading, keep_ref, give_ref)
+    split_halves(core(), read, leading, keep_ref, gives)
 
 
 def join_halves(core, pieces, whole_ref):
@@ -195,9 +208,13 @@
         base += own_ref.shape[0]
 
 
-def add_kernel(keep_ref, other_ref, after_ref, out_ref):
-    for at in range(keep_ref.shape[0]):
-        out_ref[at] = (keep_ref[at].astype(F32) + other_ref[at].astype(F32)).astype(BF16)
+def add_kernel(keep_ref, after_ref, *refs):
+    others, out_ref = refs[:-1], refs[-1]
+    base = 0
+    for other_ref in others:
+        for at in range(other_ref.shape[0]):
+            out_ref[base + at] = (keep_ref[base + at].astype(F32) + other_ref[at].astype(F32)).astype(BF16)
+        base += other_ref.shape[0]
 
 
 def gelu_kernel(own_ref, other_ref, after_ref, slope_ref, *pieces):
@@ -245,38 +262,36 @@
             target[:, pl.ds(at * BS, BS)] = jnp.concatenate([outs[mine], grads[mine]]).astype(BF16)
 
 
-def block_grads(leading, trailing, index_ref, left_ref, right_ref, out_ref, turned, held, sems):
+def turn_kernel(*refs):
+    count = len(refs) // 2
+    for source, target in zip(refs[:count], refs[count:]):
+        for at in range(source.shape[0]):
+            target[at] = source[at].T
+
+
+def grad_kernel(index_ref, turned_ref, right_ref, out_ref, mark_ref, held, sems):
+    leading, trailing = turned_ref.shape[0], right_ref.shape[0]
     slots = index_ref.shape[0]
     step = divisor(slots, 56)
 
     def out_copy(at):
         here = pl.ds(at * step, step)
         return pltpu.make_async_copy(held.at[here], out_ref.at[here], sems.at[at])
-
-    for at in range(leading):
-        turned[at] = left_ref[at].T
 
     def group(at, carry):
         for inner in range(step):
             slot = at * step + inner
             place = index_ref[slot]
             lead = jnp.minimum(place // trailing, leading - 1)
-            product = jnp.dot(turned[lead], right_ref[place % trailing], preferred_element_type=F32)
+            product = jnp.dot(turned_ref[lead], right_ref[place % trailing], preferred_element_type=F32)
             held[slot] = jnp.where(place < leading * trailing, product, 0.0).astype(BF16)
         out_copy(at).start()
         return carry
 
     lax.fori_loop(0, slots // step, group, 0)
-    return [out_copy(at) for at in range(slots // step)]
-
-
-def grad_kernel(index_ref, left_ref, right_ref, out_ref, mark_ref, turned, held, sems):
-    copies = block_grads(
-        left_ref.shape[0], right_ref.shape[0], index_ref, left_ref, right_ref, out_ref, turned, held, sems
-    )
     mark_ref[...] = jnp.zeros_like(mark_ref)
-    for copy in copies:
-        copy.wait()
+    for at in range(slots // step):
+        out_copy(at).wait()
 
 
 def merge_kernel(count, *refs):
@@ -352,9 +367,10 @@
     cols_turned = pltpu.VMEM((col_blocks, BS, tok_count), BF16)
     ANY = pl.BlockSpec(memory_space=pl.ANY)
 
-    def pair_sum(keep, give, after):
+    def pair_sum(keep, gives, after):
+        others = [swap(give, "row", 1) for give in gives]
         total = call(
-            add_kernel, "add", half_cols, [VMEM, VMEM, ANY], [], keep, swap(give, "row", 1), after
+            add_kernel, "add", half_cols, [VMEM, ANY] + [VMEM] * len(others), [], keep, after, *others
         )
         bit = 2
         while 2 * bit < row_devices:
@@ -363,21 +379,35 @@
         return total
 
     last = row_devices // 2
+    up_place, up_weight = call(
+        fetch_kernel,
+        "fetch",
+        (shape(slots, dtype=jnp.int32), shape(slots, BS, BS)),
+        [HBM, HBM, VMEM],
+        [pltpu.SemaphoreType.DMA((2,))],
+        up_place,
+        up_weight,
+        parts[4 if col_devices > 4 else -1],
+        out_specs=(SMEM, VMEM),
+        cost_estimate=cost,
+    )
     features, cotangents, pre_keep, pre_give = call(
         functools.partial(up_kernel, row_blocks, col_blocks),
         "up",
         (tile_rows, tile_rows, half_cols, half_cols),
-        [HBM, HBM] + [VMEM] * len(parts),
-        [acc_cols] + Stream.scratch(slots, 28),
+        [SMEM] + [VMEM] * (1 + len(parts)),
+        [acc_cols],
         up_place,
         up_weight,
         *parts,
         cost_estimate=cost,
     )
-    act_keep, act_give = call(
+    pieces = 2
+    bounds = [col_blocks * at // pieces for at in range(pieces + 1)]
+    act_keep, *act_gives = call(
         functools.partial(act_kernel, col_blocks, row_blocks),
         "act",
-        (half_cols, half_cols),
+        (half_cols,) + tuple(shape(b - a, half, BS) for a, b in zip(bounds, bounds[1:])),
         [SMEM, VMEM, VMEM],
         [rows_turned, acc_cols_turned],
         down_place,
@@ -385,9 +415,9 @@
         cotangents,
         cost_estimate=cost,
     )
-    pre_own = pair_sum(pre_keep, pre_give, act_keep)
+    pre_own = pair_sum(pre_keep, [pre_give], pre_keep)
     pre_other = swap(pre_own, "row", last)
-    act_own = pair_sum(act_keep, act_give, act_keep)
+    act_own = pair_sum(act_keep, act_gives, act_keep)
     act_other = swap(act_own, "row", last)
 
     cut = (col_blocks + 1) // 2
@@ -414,27 +444,35 @@
         cost_estimate=cost,
     )
 
-    def grads(name, index, left, right):
+    def grads(name, index, turned, right):
         return call(
             grad_kernel,
             name,
             (shape(slots, BS, BS), shape(8, BS, dtype=F32)),
             [SMEM, VMEM, VMEM],
             [
-                pltpu.VMEM((left.shape[0], BS, tok_count), BF16),
                 pltpu.VMEM((slots, BS, BS), BF16),
                 pltpu.SemaphoreType.DMA((slots // divisor(slots, 56),)),
             ],
             index,
-            left,
+            turned,
             right,
             out_specs=(HBM, VMEM),
             cost_estimate=cost,
         )
 
-    down_grad, down_mark = grads("down_grad", down_place, hidden, cotangents)
+    turned_hidden, turned_features = call(
+        turn_kernel,
+        "turn",
+        (shape(col_blocks, BS, tok_count), shape(row_blocks, BS, tok_count)),
+        [VMEM] * 2,
+        [],
+        hidden,
+        features,
+    )
+    down_grad, down_mark = grads("down_grad", down_place, turned_hidden, cotangents)
     grad_own = call(
-        slope_kernel, "slope", half_cols, [VMEM] * 3 + [ANY], [], act_own, act_other, slope, out_terms
+        slope_kernel, "slope", half_cols, [VMEM] * 3 + [ANY], [], act_own, act_other, slope, turned_features
     )
     by_way = [bit for bit in range(col_devices) if relayed(bit)]
     direct = [bit for bit in range(col_devices) if not relayed(bit)]
@@ -444,14 +482,14 @@
         (tile_cols, shape(len(by_way), 2 * rows, width)) + (chunk,) * len(direct),
         [SMEM, VMEM, VMEM, VMEM, VMEM],
         [cols_turned, acc_rows_turned],
-        up_index[0, 0],
-        up_blocks[0, 0],
+        up_place,
+        up_weight,
         grad_own,
         swap(grad_own, "row", 1),
         out_terms,
         cost_estimate=cost,
     )
-    up_grad, up_mark = grads("up_grad", up_index[0, 0], features, pre_grad)
+    up_grad, up_mark = grads("up_grad", up_place, turned_features, pre_grad)
     later = [bit for bit in direct if bit not in (2,)]
     merged = call(
         functools.partial(merge_kernel, len(later)),

time: 56.4 us -> 54.7 us (0.970)
  waiting for transfers between devices: 12.2 us -> 9.66 us
  Pallas kernels: 19 us -> 20.9 us
  starting transfers between devices: 23.4 us -> 22.5 us
    ppermute x20 -> x21, waiting for transfers between devices: 12.2 us -> 9.66 us  [swap(): return lax.ppermute(values, axis, [(at, at ^ bit) for at in range(count)])]
    pallas_call x12 -> x14, Pallas kernels: 19 us -> 20.9 us  [call(): pl.pallas_call(body, out_shape=outs, in_specs=ins, out_specs=out_specs or...]
    ppermute x20 -> x21, starting transfers between devices: 23.4 us -> 22.5 us  [swap(): return lax.ppermute(values, axis, [(at, at ^ bit) for at in range(count)])]
  transfers between devices with their start and end apart: 20 -> 21, of which waited for: 11 -> 10; matrix products, arithmetic and copies ran while one was open for 0% -> 0% of each run, Pallas kernels for 22% -> 28%
where the time goes in v5:
time: 54.7 us; the launch traced here: 54.6 us
  starting transfers between devices  22.5 us (41%)
  Pallas kernels  20.9 us (38%)
  waiting for transfers between devices  9.66 us (18%)
  between operations  0.85 us (2%)
  local copies, waits for them, and re-layouts  0.64 us (1%)
    ppermute x21, starting transfers between devices, swap(): return lax.ppermute(values, axis, [(at, at ^ bit) for at in range(count)])  22.5 us
    pallas_call x14, Pallas kernels, call(): pl.pallas_call(body, out_shape=outs, in_specs=ins, out_specs=out_specs or...  20.9 us
    ppermute x21, waiting for transfers between devices, swap(): return lax.ppermute(values, axis, [(at, at ^ bit) for at in range(count)])  9.66 us
  transfers between devices with their start and end apart: 21, of which 10 were waited for; matrix products, arithmetic and copies ran while one was open for 0% of the time, Pallas kernels for 28%

profile of v5, /device:TPU:0, one launch (start us, length us, event | category | flops | bytes accessed | tf_op | source)
XLA Modules:
  0.0 54.6 jit_solution(11245791351609207322)
XLA Ops:
  0.6 0.8 %pack.1.refs_0_ = bf16[16,2048]{1,0:T(8,128)(2,1)S(1)} custom-call(bf16[8,2048]{1,0:T(8,128)(2,1)} %tokens_ref.1, bf16[8,2048]{1,0:T(8,128)(2,1)} %cot_ref.1), custom_call_target="tpu_custom_call" | custom-call | bytes 33554432 | tf_op jit(solution)/shard_map/pack/pallas_call | solution.py:328
  1.4 5.1 %collective-permute-start.5 = (bf16[16,2048]{1,0:T(8,128)(2,1)S(1)}, bf16[16,2048]{1,0:T(8,128)(2,1)S(1)}, u32[]{:S(2)}, u32[]{:S(2)}) collective-permute-start(bf16[16,2048]{1,0:T(8,128)(2,1)S(1)} %pack.1.refs_0_), channel_id=1, source_target_pairs={{0,6},{1,7},{2,4},{3,5},{4,2},{5,3},{6,0},{7,1},{8,14},{9,15},{10,... | collective-permute-start | bytes 196616 | tf_op jit(solution)/shard_map/ppermute | solution.py:325
  6.6 1.7 %collective-permute-start.3 = (bf16[16,2048]{1,0:T(8,128)(2,1)S(1)}, bf16[16,2048]{1,0:T(8,128)(2,1)S(1)}, u32[]{:S(2)}, u32[]{:S(2)}) collective-permute-start(bf16[16,2048]{1,0:T(8,128)(2,1)S(1)} %pack.1.refs_0_), channel_id=1, source_target_pairs={{0,3},{1,2},{2,1},{3,0},{4,7},{5,6},{6,5},{7,4},{8,11},{9,10},{10,... | collective-permute-start | bytes 196616 | tf_op jit(solution)/shard_map/ppermute | solution.py:325
  8.3 1.2 %collective-permute-start.2 = (bf16[16,2048]{1,0:T(8,128)(2,1)S(1)}, bf16[16,2048]{1,0:T(8,128)(2,1)S(1)}, u32[]{:S(2)}, u32[]{:S(2)}) collective-permute-start(bf16[16,2048]{1,0:T(8,128)(2,1)S(1)} %pack.1.refs_0_), channel_id=1, source_target_pairs={{0,2},{1,3},{2,0},{3,1},{4,6},{5,7},{6,4},{7,5},{8,10},{9,11},{10,... | collective-permute-start | bytes 196616 | tf_op jit(solution)/shard_map/ppermute | solution.py:325
  9.5 0.5 collective-permute-start.1
  10.0 1.5 %collective-permute-start.6 = (bf16[16,2048]{1,0:T(8,128)(2,1)S(1)}, bf16[16,2048]{1,0:T(8,128)(2,1)S(1)}, u32[]{:S(2)}, u32[]{:S(2)}) collective-permute-start(bf16[16,2048]{1,0:T(8,128)(2,1)S(1)} %collective-permute-done.5.refs_6_), channel_id=1, source_target_pairs={{0,1},{1,0},{2,3},{3,2},{4,5},{5,4},{6,7},{7,6},{8,9},{9,8},{10,11... | collective-permute-start | bytes 196616 | tf_op jit(solution)/shard_map/ppermute | solution.py:325
  11.5 0.7 %collective-permute-done.after_ref.refs_4_ = bf16[16,2048]{1,0:T(8,128)(2,1)S(1)} collective-permute-done((bf16[16,2048]{1,0:T(8,128)(2,1)S(1)}, bf16[16,2048]{1,0:T(8,128)(2,1)S(1)}, u32[]{:S(2)}, u32[]{:S(2)}) %collective-permute-start) | collective-permute-done | bytes 65568 | tf_op jit(solution)/shard_map/ppermute | solution.py:325
  12.3 1.5 %collective-permute-start.4 = (bf16[16,2048]{1,0:T(8,128)(2,1)S(1)}, bf16[16,2048]{1,0:T(8,128)(2,1)S(1)}, u32[]{:S(2)}, u32[]{:S(2)}) collective-permute-start(bf16[16,2048]{1,0:T(8,128)(2,1)S(1)} %collective-permute-done.after_ref.refs_4_), channel_id=1, source_target_pairs={{0,1},{1,0},{2,3},{3,2},{4,5},{5,4},{6,7},{7,6},{8,9},{9,8},{10,11... | collective-permute-start | bytes 196616 | tf_op jit(solution)/shard_map/ppermute | solution.py:325
  13.8 2.8 %fetch.1 = (s32[112]{0:T(128)S(1)}, bf16[112,128,128]{2,1,0:T(8,128)(2,1)S(1)}) custom-call(s32[112]{0:T(128)} %bitcast.12, bf16[112,128,128]{2,1,0:T(8,128)(2,1)} %bitcast.11, bf16[16,2048]{1,0:T(8,128)(2,1)S(1)} %collective-permute-done.after_ref.refs_4_), custom_call_target="tpu_custom_call" | custom-call | flops 234881024 | bytes 3670016 | tf_op jit(solution)/shard_map/fetch/pallas_call | solution.py:328
  16.6 2.1 %up.1 = (bf16[16,64,128]{2,1,0:T(8,128)(2,1)S(1)}, bf16[16,64,128]{2,1,0:T(8,128)(2,1)S(1)}, bf16[28,32,128]{2,1,0:T(8,128)(2,1)S(1)}, bf16[28,32,128]{2,1,0:T(8,128)(2,1)S(1)}) custom-call(s32[112]{0:T(128)S(1)} %get-tuple-element.36.index_ref, bf16[112,128,128]{2,1,0:T(8,128)(2,1)S(1)} %get-tuple-element.37.blocks_ref, bf16[16,2048]{1,0:T(8,128)(2,1)S(1)} %pack.1.refs_0_, ...), custom_call_target="tpu_custom_call" | custom-call | flops 234881024 | bytes 3670016 | tf_op jit(solution)/shard_map/up/pallas_call | solution.py:328
  18.8 1.5 %collective-permute-done.10.refs_0_ = bf16[28,32,128]{2,1,0:T(8,128)(2,1)S(1)} collective-permute-done((bf16[28,32,128]{2,1,0:T(8,128)(2,1)S(1)}, bf16[28,32,128]{2,1,0:T(8,128)(2,1)S(1)}, u32[]{:S(2)}, u32[]{:S(2)}) %collective-permute-start.10) | collective-permute-done | bytes 229408 | tf_op jit(solution)/shard_map/ppermute | solution.py:325
  20.4 1.6 %collective-permute-start.11 = (bf16[28,32,128]{2,1,0:T(8,128)(2,1)S(1)}, bf16[28,32,128]{2,1,0:T(8,128)(2,1)S(1)}, u32[]{:S(2)}, u32[]{:S(2)}) collective-permute-start(bf16[28,32,128]{2,1,0:T(8,128)(2,1)S(1)} %add.28.own_ref), channel_id=1, source_target_pairs={{0,16},{8,24},{16,0},{24,8},{1,17},{9,25},{17,1},{25,9},{2,18},{10... | collective-permute-start | bytes 688136 | tf_op jit(solution)/shard_map/ppermute | solution.py:325
  22.0 2.7 %act.1 = (bf16[28,32,128]{2,1,0:T(8,128)(2,1)S(1)}, bf16[14,32,128]{2,1,0:T(8,128)(2,1)S(1)}, bf16[14,32,128]{2,1,0:T(8,128)(2,1)S(1)}) custom-call(s32[112]{0:T(128)S(1)} %bitcast.8, bf16[112,128,128]{2,1,0:T(8,128)(2,1)S(1)} %bitcast.6, bf16[16,64,128]{2,1,0:T(8,128)(2,1)S(1)} %get-tuple-element.38.cot_ref.right_ref), custom_call_target="tpu_custom_call" | custom-call | flops 234881024 | bytes 3670016 | tf_op jit(solution)/shard_map/act/pallas_call | solution.py:328
  24.8 0.5 collective-permute-start.8
  25.2 0.8 %collective-permute-done.7.refs_0_ = bf16[14,32,128]{2,1,0:T(8,128)(2,1)S(1)} collective-permute-done((bf16[14,32,128]{2,1,0:T(8,128)(2,1)S(1)}, bf16[14,32,128]{2,1,0:T(8,128)(2,1)S(1)}, u32[]{:S(2)}, u32[]{:S(2)}) %collective-permute-start.7) | collective-permute-done | bytes 114720 | tf_op jit(solution)/shard_map/ppermute | solution.py:325
  26.3 0.5 collective-permute-start.9
  26.8 1.2 %collective-permute-done.11.other_ref = bf16[28,32,128]{2,1,0:T(8,128)(2,1)S(1)} collective-permute-done((bf16[28,32,128]{2,1,0:T(8,128)(2,1)S(1)}, bf16[28,32,128]{2,1,0:T(8,128)(2,1)S(1)}, u32[]{:S(2)}, u32[]{:S(2)}) %collective-permute-start.11) | collective-permute-done | bytes 229408 | tf_op jit(solution)/shard_map/ppermute | solution.py:325
  28.5 0.5 collective-permute-start.13
  29.0 0.8 %collective-permute-done.12.refs_1_ = bf16[14,32,128]{2,1,0:T(8,128)(2,1)S(1)} collective-permute-done((bf16[14,32,128]{2,1,0:T(8,128)(2,1)S(1)}, bf16[14,32,128]{2,1,0:T(8,128)(2,1)S(1)}, u32[]{:S(2)}, u32[]{:S(2)}) %collective-permute-start.12) | collective-permute-done | bytes 114720 | tf_op jit(solution)/shard_map/ppermute | solution.py:325
  30.0 2.0 %down.1 = (bf16[28,64,128]{2,1,0:T(8,128)(2,1)S(1)}, bf16[16,64,128]{2,1,0:T(8,128)(2,1)S(1)}) custom-call(s32[112]{0:T(128)S(1)} %bitcast.9, bf16[112,128,128]{2,1,0:T(8,128)(2,1)S(1)} %bitcast.7, bf16[14,32,128]{2,1,0:T(8,128)(2,1)S(1)} %get-tuple-element.45.refs_0_, bf16[14,32,128]{2,1,0:T(8,128)(2,1)S(1)} %collective-permute-done.12.refs_1_, ...), custom_call_target="tpu_custom_call" | custom-call | flops 234881024 | bytes 3670016 | tf_op jit(solution)/shard_map/down/pallas_call | solution.py:328
  32.0 0.5 turn.1
  32.4 1.8 %collective-permute-done.9.other_ref = bf16[28,32,128]{2,1,0:T(8,128)(2,1)S(1)} collective-permute-done((bf16[28,32,128]{2,1,0:T(8,128)(2,1)S(1)}, bf16[28,32,128]{2,1,0:T(8,128)(2,1)S(1)}, u32[]{:S(2)}, u32[]{:S(2)}) %collective-permute-start.9) | collective-permute-done | bytes 229408 | tf_op jit(solution)/shard_map/ppermute | solution.py:325
  34.4 1.5 %collective-permute-done.14.other_ref = bf16[28,32,128]{2,1,0:T(8,128)(2,1)S(1)} collective-permute-done((bf16[28,32,128]{2,1,0:T(8,128)(2,1)S(1)}, bf16[28,32,128]{2,1,0:T(8,128)(2,1)S(1)}, u32[]{:S(2)}, u32[]{:S(2)}) %collective-permute-start.14) | collective-permute-done | bytes 229408 | tf_op jit(solution)/shard_map/ppermute | solution.py:325
  35.8 2.7 %input.1 = (bf16[28,64,128]{2,1,0:T(8,128)(2,1)S(1)}, bf16[2,16,2048]{2,1,0:T(8,128)(2,1)S(1)}, bf16[16,2048]{1,0:T(8,128)(2,1)S(1)}, bf16[16,2048]{1,0:T(8,128)...) custom-call(s32[112]{0:T(128)S(1)} %get-tuple-element.36.index_ref, ...), custom_call_target="tpu_custom_call" | custom-call | flops 234881024 | bytes 3670016 | tf_op jit(solution)/shard_map/input/pallas_call | solution.py:328
  38.5 1.4 %collective-permute-start.15 = (bf16[2,16,2048]{2,1,0:T(8,128)(2,1)S(1)}, bf16[2,16,2048]{2,1,0:T(8,128)(2,1)S(1)}, u32[]{:S(2)}, u32[]{:S(2)}) collective-permute-start(bf16[2,16,2048]{2,1,0:T(8,128)(2,1)S(1)} %get-tuple-element.51), channel_id=1, source_target_pairs={{0,1},{1,0},{2,3},{3,2},{4,5},{5,4},{6,7},{7,6},{8,9},{9,8},{10,11... | collective-permute-start | bytes 393224 | tf_op jit(solution)/shard_map/ppermute | solution.py:325
  40.0 3.1 %down_grad.1 = (bf16[112,128,128]{2,1,0:T(8,128)(2,1)}, f32[8,128]{1,0:T(8,128)S(1)}) custom-call(s32[112]{0:T(128)S(1)} %bitcast.10, bf16[28,128,64]{2,1,0:T(8,128)(2,1)S(1)} %get-tuple-element.52.turned_ref, bf16[16,64,128]{2,1,0:T(8,128)(2,1)S(1)} %get-tuple-element.38.cot_ref.right_ref), custom_call_target="tpu_custom_call" | custom-call | flops 234881024 | bytes 3670016 | tf_op jit(solution)/shard_map/down_grad/pallas_call | solution.py:328
  43.1 1.0 %collective-permute-done.15.refs_0_ = bf16[2,16,2048]{2,1,0:T(8,128)(2,1)S(1)} collective-permute-done((bf16[2,16,2048]{2,1,0:T(8,128)(2,1)S(1)}, bf16[2,16,2048]{2,1,0:T(8,128)(2,1)S(1)}, u32[]{:S(2)}, u32[]{:S(2)}) %collective-permute-start.15) | collective-permute-done | bytes 131104 | tf_op jit(solution)/shard_map/ppermute | solution.py:325
  44.2 2.7 %collective-permute-start.16 = (bf16[16,2048]{1,0:T(8,128)(2,1)S(1)}, bf16[16,2048]{1,0:T(8,128)(2,1)S(1)}, u32[]{:S(2)}, u32[]{:S(2)}) collective-permute-start(bf16[16,2048]{1,0:T(8,128)(2,1)S(1)} %get-tuple-element.60), channel_id=1, source_target_pairs={{0,6},{1,7},{2,4},{3,5},{4,2},{5,3},{6,0},{7,1},{8,14},{9,15},{10,... | collective-permute-start | bytes 196616 | tf_op jit(solution)/shard_map/ppermute | solution.py:325
  46.9 2.6 %collective-permute-start.18 = (bf16[16,2048]{1,0:T(8,128)(2,1)S(1)}, bf16[16,2048]{1,0:T(8,128)(2,1)S(1)}, u32[]{:S(2)}, u32[]{:S(2)}) collective-permute-start(bf16[16,2048]{1,0:T(8,128)(2,1)S(1)} %get-tuple-element.62), channel_id=1, source_target_pairs={{0,3},{1,2},{2,1},{3,0},{4,7},{5,6},{6,5},{7,4},{8,11},{9,10},{10,... | collective-permute-start | bytes 196616 | tf_op jit(solution)/shard_map/ppermute | solution.py:325
  49.4 0.7 %collective-permute-start.20 = (bf16[16,2048]{1,0:T(8,128)(2,1)S(1)}, bf16[16,2048]{1,0:T(8,128)(2,1)S(1)}, u32[]{:S(2)}, u32[]{:S(2)}) collective-permute-start(bf16[16,2048]{1,0:T(8,128)(2,1)S(1)} %get-tuple-element.64), channel_id=1, source_target_pairs={{0,1},{1,0},{2,3},{3,2},{4,5},{5,4},{6,7},{7,6},{8,9},{9,8},{10,11... | collective-permute-start | bytes 196616 | tf_op jit(solution)/shard_map/ppermute | solution.py:325
  50.1 3.7 %up_grad.1 = (bf16[112,128,128]{2,1,0:T(8,128)(2,1)}, f32[8,128]{1,0:T(8,128)}) custom-call(s32[112]{0:T(128)S(1)} %get-tuple-element.36.index_ref, bf16[16,128,64]{2,1,0:T(8,128)(2,1)S(1)} %get-tuple-element.49.after_ref.turned_ref, bf16[28,64,128]{2,1,0:T(8,128)(2,1)S(1)} %get-tuple-element.65.right_ref), custom_call_target="tpu_custom_call" | custom-call | flops 234881024 | bytes 3670016 | tf_op jit(solution)/shard_map/up_grad/pallas_call | solution.py:328
  53.9 0.6 %fusion = (bf16[8,2048]{1,0:T(8,128)(2,1)}, bf16[8,2048]{1,0:T(8,128)(2,1)}) fusion(bf16[16,2048]{1,0:T(8,128)(2,1)S(1)} %add_convert_fusion), kind=kLoop, calls=%fused_computation.1 | loop fusion | bytes 131072 | tf_op jit(solution)/shard_map/slice | solution.py:509
  (30 shorter events, 1.4 us)
Async XLA Ops:
  1.4 8.6 %collective-permute-start.5 = (bf16[16,2048]{1,0:T(8,128)(2,1)S(1)}, bf16[16,2048]{1,0:T(8,128)(2,1)S(1)}, u32[]{:S(2)}, u32[]{:S(2)}) collective-permute-start(bf16[16,2048]{1,0:T(8,128)(2,1)S(1)} %pack.1.refs_0_), channel_id=1, source_target_pairs={{0,6},{1,7},{2,4},{3,5},{4,2},{5,3},{6,0},{7,1},{8,14},{9,15},{10,... | collective-permute-start | bytes 196616 | tf_op jit(solution)/shard_map/ppermute | solution.py:325
  6.5 5.7 %collective-permute-start = (bf16[16,2048]{1,0:T(8,128)(2,1)S(1)}, bf16[16,2048]{1,0:T(8,128)(2,1)S(1)}, u32[]{:S(2)}, u32[]{:S(2)}) collective-permute-start(bf16[16,2048]{1,0:T(8,128)(2,1)S(1)} %pack.1.refs_0_), channel_id=1, source_target_pairs={{0,4},{1,5},{2,6},{3,7},{4,0},{5,1},{6,2},{7,3},{8,12},{9,13},{10,... | collective-permute-start | bytes 196616 | tf_op jit(solution)/shard_map/ppermute | solution.py:325
  6.6 10.0 %collective-permute-start.3 = (bf16[16,2048]{1,0:T(8,128)(2,1)S(1)}, bf16[16,2048]{1,0:T(8,128)(2,1)S(1)}, u32[]{:S(2)}, u32[]{:S(2)}) collective-permute-start(bf16[16,2048]{1,0:T(8,128)(2,1)S(1)} %pack.1.refs_0_), channel_id=1, source_target_pairs={{0,3},{1,2},{2,1},{3,0},{4,7},{5,6},{6,5},{7,4},{8,11},{9,10},{10,... | collective-permute-start | bytes 196616 | tf_op jit(solution)/shard_map/ppermute | solution.py:325
  8.3 8.3 %collective-permute-start.2 = (bf16[16,2048]{1,0:T(8,128)(2,1)S(1)}, bf16[16,2048]{1,0:T(8,128)(2,1)S(1)}, u32[]{:S(2)}, u32[]{:S(2)}) collective-permute-start(bf16[16,2048]{1,0:T(8,128)(2,1)S(1)} %pack.1.refs_0_), channel_id=1, source_target_pairs={{0,2},{1,3},{2,0},{3,1},{4,6},{5,7},{6,4},{7,5},{8,10},{9,11},{10,... | collective-permute-start | bytes 196616 | tf_op jit(solution)/shard_map/ppermute | solution.py:325
  9.5 7.1 %collective-permute-start.1 = (bf16[16,2048]{1,0:T(8,128)(2,1)S(1)}, bf16[16,2048]{1,0:T(8,128)(2,1)S(1)}, u32[]{:S(2)}, u32[]{:S(2)}) collective-permute-start(bf16[16,2048]{1,0:T(8,128)(2,1)S(1)} %pack.1.refs_0_), channel_id=1, source_target_pairs={{0,1},{1,0},{2,3},{3,2},{4,5},{5,4},{6,7},{7,6},{8,9},{9,8},{10,11... | collective-permute-start | bytes 196616 | tf_op jit(solution)/shard_map/ppermute | solution.py:325
  10.0 6.5 %collective-permute-start.6 = (bf16[16,2048]{1,0:T(8,128)(2,1)S(1)}, bf16[16,2048]{1,0:T(8,128)(2,1)S(1)}, u32[]{:S(2)}, u32[]{:S(2)}) collective-permute-start(bf16[16,2048]{1,0:T(8,128)(2,1)S(1)} %collective-permute-done.5.refs_6_), channel_id=1, source_target_pairs={{0,1},{1,0},{2,3},{3,2},{4,5},{5,4},{6,7},{7,6},{8,9},{9,8},{10,11... | collective-permute-start | bytes 196616 | tf_op jit(solution)/shard_map/ppermute | solution.py:325
  12.3 4.3 %collective-permute-start.4 = (bf16[16,2048]{1,0:T(8,128)(2,1)S(1)}, bf16[16,2048]{1,0:T(8,128)(2,1)S(1)}, u32[]{:S(2)}, u32[]{:S(2)}) collective-permute-start(bf16[16,2048]{1,0:T(8,128)(2,1)S(1)} %collective-permute-done.after_ref.refs_4_), channel_id=1, source_target_pairs={{0,1},{1,0},{2,3},{3,2},{4,5},{5,4},{6,7},{7,6},{8,9},{9,8},{10,11... | collective-permute-start | bytes 196616 | tf_op jit(solution)/shard_map/ppermute | solution.py:325
  13.7 8.2 %copy-start = (bf16[1,1,112,128,128]{4,3,2,1,0:T(8,128)(2,1)S(1)}, bf16[1,1,112,128,128]{4,3,2,1,0:T(8,128)(2,1)}, u32[]{:S(2)}) copy-start(bf16[1,1,112,128,128]{4,3,2,1,0:T(8,128)(2,1)} %param.9) | copy-start | bytes 11010052
  13.7 8.2 %copy-start.1 = (s32[1,1,112]{2,1,0:T(1,128)S(1)}, s32[1,1,112]{2,1,0:T(1,128)}, u32[]{:S(2)}) copy-start(s32[1,1,112]{2,1,0:T(1,128)} %param.10) | copy-start | bytes 1348
  18.7 1.6 %collective-permute-start.10 = (bf16[28,32,128]{2,1,0:T(8,128)(2,1)S(1)}, bf16[28,32,128]{2,1,0:T(8,128)(2,1)S(1)}, u32[]{:S(2)}, u32[]{:S(2)}) collective-permute-start(bf16[28,32,128]{2,1,0:T(8,128)(2,1)S(1)} %get-tuple-element.43), channel_id=1, source_target_pairs={{0,8},{8,0},{16,24},{24,16},{1,9},{9,1},{17,25},{25,17},{2,10},{10... | collective-permute-start | bytes 688136 | tf_op jit(solution)/shard_map/ppermute | solution.py:325
  20.4 7.7 %collective-permute-start.11 = (bf16[28,32,128]{2,1,0:T(8,128)(2,1)S(1)}, bf16[28,32,128]{2,1,0:T(8,128)(2,1)S(1)}, u32[]{:S(2)}, u32[]{:S(2)}) collective-permute-start(bf16[28,32,128]{2,1,0:T(8,128)(2,1)S(1)} %add.28.own_ref), channel_id=1, source_target_pairs={{0,16},{8,24},{16,0},{24,8},{1,17},{9,25},{17,1},{25,9},{2,18},{10... | collective-permute-start | bytes 688136 | tf_op jit(solution)/shard_map/ppermute | solution.py:325
  24.7 1.4 %collective-permute-start.7 = (bf16[14,32,128]{2,1,0:T(8,128)(2,1)S(1)}, bf16[14,32,128]{2,1,0:T(8,128)(2,1)S(1)}, u32[]{:S(2)}, u32[]{:S(2)}) collective-permute-start(bf16[14,32,128]{2,1,0:T(8,128)(2,1)S(1)} %get-tuple-element.40), channel_id=1, source_target_pairs={{0,8},{8,0},{16,24},{24,16},{1,9},{9,1},{17,25},{25,17},{2,10},{10... | collective-permute-start | bytes 344072 | tf_op jit(solution)/shard_map/ppermute | solution.py:325
  24.8 1.5 %collective-permute-start.8 = (bf16[14,32,128]{2,1,0:T(8,128)(2,1)S(1)}, bf16[14,32,128]{2,1,0:T(8,128)(2,1)S(1)}, u32[]{:S(2)}, u32[]{:S(2)}) collective-permute-start(bf16[14,32,128]{2,1,0:T(8,128)(2,1)S(1)} %get-tuple-element.41), channel_id=1, source_target_pairs={{0,8},{8,0},{16,24},{24,16},{1,9},{9,1},{17,25},{25,17},{2,10},{10... | collective-permute-start | bytes 344072 | tf_op jit(solution)/shard_map/ppermute | solution.py:325
  26.3 7.9 %collective-permute-start.9 = (bf16[28,32,128]{2,1,0:T(8,128)(2,1)S(1)}, bf16[28,32,128]{2,1,0:T(8,128)(2,1)S(1)}, u32[]{:S(2)}, u32[]{:S(2)}) collective-permute-start(bf16[28,32,128]{2,1,0:T(8,128)(2,1)S(1)} %add.27.after_ref.own_ref), channel_id=1, source_target_pairs={{0,16},{8,24},{16,0},{24,8},{1,17},{9,25},{17,1},{25,9},{2,18},{10... | collective-permute-start | bytes 688136 | tf_op jit(solution)/shard_map/ppermute | solution.py:325
  28.4 1.4 %collective-permute-start.12 = (bf16[14,32,128]{2,1,0:T(8,128)(2,1)S(1)}, bf16[14,32,128]{2,1,0:T(8,128)(2,1)S(1)}, u32[]{:S(2)}, u32[]{:S(2)}) collective-permute-start(bf16[14,32,128]{2,1,0:T(8,128)(2,1)S(1)} %get-tuple-element.45.refs_0_), channel_id=1, source_target_pairs={{0,8},{8,0},{16,24},{24,16},{1,9},{9,1},{17,25},{25,17},{2,10},{10... | collective-permute-start | bytes 344072 | tf_op jit(solution)/shard_map/ppermute | solution.py:325
  28.5 1.5 %collective-permute-start.13 = (bf16[14,32,128]{2,1,0:T(8,128)(2,1)S(1)}, bf16[14,32,128]{2,1,0:T(8,128)(2,1)S(1)}, u32[]{:S(2)}, u32[]{:S(2)}) collective-permute-start(bf16[14,32,128]{2,1,0:T(8,128)(2,1)S(1)} %get-tuple-element.46.refs_2_), channel_id=1, source_target_pairs={{0,8},{8,0},{16,24},{24,16},{1,9},{9,1},{17,25},{25,17},{2,10},{10... | collective-permute-start | bytes 344072 | tf_op jit(solution)/shard_map/ppermute | solution.py:325
  34.3 1.6 %collective-permute-start.14 = (bf16[28,32,128]{2,1,0:T(8,128)(2,1)S(1)}, bf16[28,32,128]{2,1,0:T(8,128)(2,1)S(1)}, u32[]{:S(2)}, u32[]{:S(2)}) collective-permute-start(bf16[28,32,128]{2,1,0:T(8,128)(2,1)S(1)} %slope.1.own_ref), channel_id=1, source_target_pairs={{0,8},{8,0},{16,24},{24,16},{1,9},{9,1},{17,25},{25,17},{2,10},{10... | collective-permute-start | bytes 688136 | tf_op jit(solution)/shard_map/ppermute | solution.py:325
  38.5 5.6 %collective-permute-start.15 = (bf16[2,16,2048]{2,1,0:T(8,128)(2,1)S(1)}, bf16[2,16,2048]{2,1,0:T(8,128)(2,1)S(1)}, u32[]{:S(2)}, u32[]{:S(2)}) collective-permute-start(bf16[2,16,2048]{2,1,0:T(8,128)(2,1)S(1)} %get-tuple-element.51), channel_id=1, source_target_pairs={{0,1},{1,0},{2,3},{3,2},{4,5},{5,4},{6,7},{7,6},{8,9},{9,8},{10,11... | collective-permute-start | bytes 393224 | tf_op jit(solution)/shard_map/ppermute | solution.py:325
  43.0 10.8 %collective-permute-start.19 = (bf16[16,2048]{1,0:T(8,128)(2,1)S(1)}, bf16[16,2048]{1,0:T(8,128)(2,1)S(1)}, u32[]{:S(2)}, u32[]{:S(2)}) collective-permute-start(bf16[16,2048]{1,0:T(8,128)(2,1)S(1)} %get-tuple-element.63), channel_id=1, source_target_pairs={{0,2},{1,3},{2,0},{3,1},{4,6},{5,7},{6,4},{7,5},{8,10},{9,11},{10,... | collective-permute-start | bytes 196616 | tf_op jit(solution)/shard_map/ppermute | solution.py:325
  44.2 9.7 %collective-permute-start.16 = (bf16[16,2048]{1,0:T(8,128)(2,1)S(1)}, bf16[16,2048]{1,0:T(8,128)(2,1)S(1)}, u32[]{:S(2)}, u32[]{:S(2)}) collective-permute-start(bf16[16,2048]{1,0:T(8,128)(2,1)S(1)} %get-tuple-element.60), channel_id=1, source_target_pairs={{0,6},{1,7},{2,4},{3,5},{4,2},{5,3},{6,0},{7,1},{8,14},{9,15},{10,... | collective-permute-start | bytes 196616 | tf_op jit(solution)/shard_map/ppermute | solution.py:325
  46.9 7.0 %collective-permute-start.17 = (bf16[16,2048]{1,0:T(8,128)(2,1)S(1)}, bf16[16,2048]{1,0:T(8,128)(2,1)S(1)}, u32[]{:S(2)}, u32[]{:S(2)}) collective-permute-start(bf16[16,2048]{1,0:T(8,128)(2,1)S(1)} %get-tuple-element.61), channel_id=1, source_target_pairs={{0,4},{1,5},{2,6},{3,7},{4,0},{5,1},{6,2},{7,3},{8,12},{9,13},{10,... | collective-permute-start | bytes 196616 | tf_op jit(solution)/shard_map/ppermute | solution.py:325
  46.9 7.0 %collective-permute-start.18 = (bf16[16,2048]{1,0:T(8,128)(2,1)S(1)}, bf16[16,2048]{1,0:T(8,128)(2,1)S(1)}, u32[]{:S(2)}, u32[]{:S(2)}) collective-permute-start(bf16[16,2048]{1,0:T(8,128)(2,1)S(1)} %get-tuple-element.62), channel_id=1, source_target_pairs={{0,3},{1,2},{2,1},{3,0},{4,7},{5,6},{6,5},{7,4},{8,11},{9,10},{10,... | collective-permute-start | bytes 196616 | tf_op jit(solution)/shard_map/ppermute | solution.py:325
  49.4 4.4 %collective-permute-start.20 = (bf16[16,2048]{1,0:T(8,128)(2,1)S(1)}, bf16[16,2048]{1,0:T(8,128)(2,1)S(1)}, u32[]{:S(2)}, u32[]{:S(2)}) collective-permute-start(bf16[16,2048]{1,0:T(8,128)(2,1)S(1)} %get-tuple-element.64), channel_id=1, source_target_pairs={{0,1},{1,0},{2,3},{3,2},{4,5},{5,4},{6,7},{7,6},{8,9},{9,8},{10,11... | collective-permute-start | bytes 196616 | tf_op jit(solution)/shard_map/ppermute | solution.py:325

commit v6 on v5

--- a/solution.py
+++ b/solution.py
@@ -169,7 +169,7 @@
 def up_kernel(leading, trailing, index_ref, blocks_ref, *refs):
     parts = refs[:-5]
     tokens_ref, cot_ref, keep_ref, give_ref, acc = refs[-5:]
-    source = Held(index_ref, blocks_ref, 56)
+    source = Held(index_ref, blocks_ref, 112)
     rows = parts[0].shape[0] // 2
     for pair in range(len(parts) // 2):
         here = pl.ds(pair * 2 * rows, 2 * rows)
@@ -188,7 +188,7 @@
     leading, trailing, index_ref, blocks_ref, cot_ref, keep_ref, *refs
 ):
     gives, (turned, acc) = refs[:-2], refs[-2:]
-    accumulate_turned(Held(index_ref, blocks_ref, 56), leading, trailing, cot_ref, turned, acc)
+    accumulate_turned(Held(index_ref, blocks_ref, 112), leading, trailing, cot_ref, turned, acc)
     half = keep_ref.shape[1]
 
     def read(at, low):
@@ -236,7 +236,7 @@
 def down_kernel(leading, trailing, index_ref, blocks_ref, *refs):
     pieces, (hidden_ref, terms_ref, acc) = refs[:-3], refs[-3:]
     join_halves(core(), list(zip(pieces[::2], pieces[1::2])), hidden_ref)
-    accumulate(Held(index_ref, blocks_ref, 56), leading, trailing, hidden_ref, acc)
+    accumulate(Held(index_ref, blocks_ref, 112), leading, trailing, hidden_ref, acc)
     for at in range(trailing):
         terms_ref[at] = acc[at].astype(BF16)
 
@@ -250,7 +250,7 @@
 ):
     chunks, turned, acc = refs[:-2], refs[-2], refs[-1]
     join_halves(core(), [(own_ref, other_ref)], grad_ref)
-    accumulate_turned(Held(index_ref, blocks_ref, 56), leading, trailing, grad_ref, turned, acc)
+    accumulate_turned(Held(index_ref, blocks_ref, 112), leading, trailing, grad_ref, turned, acc)
     devices = relay_ref.shape[0] + len(chunks)
     rows = grad_ref.shape[1] // devices
     for at in range(leading):

time: 54.7 us -> 54 us (0.987)
  Pallas kernels: 20.9 us -> 20 us
    pallas_call x14, Pallas kernels: 20.9 us -> 20 us  [call(): pl.pallas_call(body, out_shape=outs, in_specs=ins, out_specs=out_specs or...]
where the time goes in v6:
time: 54 us; the launch traced here: 53.8 us
  starting transfers between devices  22.5 us (42%)
  Pallas kernels  20 us (37%)
  waiting for transfers between devices  9.77 us (18%)
  between operations  0.86 us (2%)
  local copies, waits for them, and re-layouts  0.64 us (1%)
    ppermute x21, starting transfers between devices, swap(): return lax.ppermute(values, axis, [(at, at ^ bit) for at in range(count)])  22.5 us
    pallas_call x14, Pallas kernels, call(): pl.pallas_call(body, out_shape=outs, in_specs=ins, out_specs=out_specs or...  20 us
    ppermute x21, waiting for transfers between devices, swap(): return lax.ppermute(values, axis, [(at, at ^ bit) for at in range(count)])  9.77 us
  transfers between devices with their start and end apart: 21, of which 10 were waited for; matrix products, arithmetic and copies ran while one was open for 0% of the time, Pallas kernels for 28%

profile of v6, /device:TPU:0, one launch (start us, length us, event | category | flops | bytes accessed | tf_op | source)
XLA Modules:
  0.0 53.8 jit_solution(11018989658722163058)
XLA Ops:
  0.6 0.8 %pack.1.refs_0_ = bf16[16,2048]{1,0:T(8,128)(2,1)S(1)} custom-call(bf16[8,2048]{1,0:T(8,128)(2,1)} %tokens_ref.1, bf16[8,2048]{1,0:T(8,128)(2,1)} %cot_ref.1), custom_call_target="tpu_custom_call" | custom-call | bytes 33554432 | tf_op jit(solution)/shard_map/pack/pallas_call | solution.py:328
  1.4 5.1 %collective-permute-start.5 = (bf16[16,2048]{1,0:T(8,128)(2,1)S(1)}, bf16[16,2048]{1,0:T(8,128)(2,1)S(1)}, u32[]{:S(2)}, u32[]{:S(2)}) collective-permute-start(bf16[16,2048]{1,0:T(8,128)(2,1)S(1)} %pack.1.refs_0_), channel_id=1, source_target_pairs={{0,6},{1,7},{2,4},{3,5},{4,2},{5,3},{6,0},{7,1},{8,14},{9,15},{10,... | collective-permute-start | bytes 196616 | tf_op jit(solution)/shard_map/ppermute | solution.py:325
  6.6 1.7 %collective-permute-start.3 = (bf16[16,2048]{1,0:T(8,128)(2,1)S(1)}, bf16[16,2048]{1,0:T(8,128)(2,1)S(1)}, u32[]{:S(2)}, u32[]{:S(2)}) collective-permute-start(bf16[16,2048]{1,0:T(8,128)(2,1)S(1)} %pack.1.refs_0_), channel_id=1, source_target_pairs={{0,3},{1,2},{2,1},{3,0},{4,7},{5,6},{6,5},{7,4},{8,11},{9,10},{10,... | collective-permute-start | bytes 196616 | tf_op jit(solution)/shard_map/ppermute | solution.py:325
  8.3 1.2 %collective-permute-start.2 = (bf16[16,2048]{1,0:T(8,128)(2,1)S(1)}, bf16[16,2048]{1,0:T(8,128)(2,1)S(1)}, u32[]{:S(2)}, u32[]{:S(2)}) collective-permute-start(bf16[16,2048]{1,0:T(8,128)(2,1)S(1)} %pack.1.refs_0_), channel_id=1, source_target_pairs={{0,2},{1,3},{2,0},{3,1},{4,6},{5,7},{6,4},{7,5},{8,10},{9,11},{10,... | collective-permute-start | bytes 196616 | tf_op jit(solution)/shard_map/ppermute | solution.py:325
  9.5 0.5 collective-permute-start.1
  10.0 1.5 %collective-permute-start.6 = (bf16[16,2048]{1,0:T(8,128)(2,1)S(1)}, bf16[16,2048]{1,0:T(8,128)(2,1)S(1)}, u32[]{:S(2)}, u32[]{:S(2)}) collective-permute-start(bf16[16,2048]{1,0:T(8,128)(2,1)S(1)} %collective-permute-done.5.refs_6_), channel_id=1, source_target_pairs={{0,1},{1,0},{2,3},{3,2},{4,5},{5,4},{6,7},{7,6},{8,9},{9,8},{10,11... | collective-permute-start | bytes 196616 | tf_op jit(solution)/shard_map/ppermute | solution.py:325
  11.5 0.7 %collective-permute-done.after_ref.refs_4_ = bf16[16,2048]{1,0:T(8,128)(2,1)S(1)} collective-permute-done((bf16[16,2048]{1,0:T(8,128)(2,1)S(1)}, bf16[16,2048]{1,0:T(8,128)(2,1)S(1)}, u32[]{:S(2)}, u32[]{:S(2)}) %collective-permute-start) | collective-permute-done | bytes 65568 | tf_op jit(solution)/shard_map/ppermute | solution.py:325
  12.3 1.5 %collective-permute-start.4 = (bf16[16,2048]{1,0:T(8,128)(2,1)S(1)}, bf16[16,2048]{1,0:T(8,128)(2,1)S(1)}, u32[]{:S(2)}, u32[]{:S(2)}) collective-permute-start(bf16[16,2048]{1,0:T(8,128)(2,1)S(1)} %collective-permute-done.after_ref.refs_4_), channel_id=1, source_target_pairs={{0,1},{1,0},{2,3},{3,2},{4,5},{5,4},{6,7},{7,6},{8,9},{9,8},{10,11... | collective-permute-start | bytes 196616 | tf_op jit(solution)/shard_map/ppermute | solution.py:325
  13.8 2.8 %fetch.1 = (s32[112]{0:T(128)S(1)}, bf16[112,128,128]{2,1,0:T(8,128)(2,1)S(1)}) custom-call(s32[112]{0:T(128)} %bitcast.12, bf16[112,128,128]{2,1,0:T(8,128)(2,1)} %bitcast.11, bf16[16,2048]{1,0:T(8,128)(2,1)S(1)} %collective-permute-done.after_ref.refs_4_), custom_call_target="tpu_custom_call" | custom-call | flops 234881024 | bytes 3670016 | tf_op jit(solution)/shard_map/fetch/pallas_call | solution.py:328
  16.6 1.9 %up.1 = (bf16[16,64,128]{2,1,0:T(8,128)(2,1)S(1)}, bf16[16,64,128]{2,1,0:T(8,128)(2,1)S(1)}, bf16[28,32,128]{2,1,0:T(8,128)(2,1)S(1)}, bf16[28,32,128]{2,1,0:T(8,128)(2,1)S(1)}) custom-call(s32[112]{0:T(128)S(1)} %get-tuple-element.36.index_ref, bf16[112,128,128]{2,1,0:T(8,128)(2,1)S(1)} %get-tuple-element.37.blocks_ref, bf16[16,2048]{1,0:T(8,128)(2,1)S(1)} %pack.1.refs_0_, ...), custom_call_target="tpu_custom_call" | custom-call | flops 234881024 | bytes 3670016 | tf_op jit(solution)/shard_map/up/pallas_call | solution.py:328
  18.6 1.5 %collective-permute-done.10.refs_0_ = bf16[28,32,128]{2,1,0:T(8,128)(2,1)S(1)} collective-permute-done((bf16[28,32,128]{2,1,0:T(8,128)(2,1)S(1)}, bf16[28,32,128]{2,1,0:T(8,128)(2,1)S(1)}, u32[]{:S(2)}, u32[]{:S(2)}) %collective-permute-start.10) | collective-permute-done | bytes 229408 | tf_op jit(solution)/shard_map/ppermute | solution.py:325
  20.1 1.6 %collective-permute-start.11 = (bf16[28,32,128]{2,1,0:T(8,128)(2,1)S(1)}, bf16[28,32,128]{2,1,0:T(8,128)(2,1)S(1)}, u32[]{:S(2)}, u32[]{:S(2)}) collective-permute-start(bf16[28,32,128]{2,1,0:T(8,128)(2,1)S(1)} %add.28.own_ref), channel_id=1, source_target_pairs={{0,16},{8,24},{16,0},{24,8},{1,17},{9,25},{17,1},{25,9},{2,18},{10... | collective-permute-start | bytes 688136 | tf_op jit(solution)/shard_map/ppermute | solution.py:325
  21.7 2.5 %act.1 = (bf16[28,32,128]{2,1,0:T(8,128)(2,1)S(1)}, bf16[14,32,128]{2,1,0:T(8,128)(2,1)S(1)}, bf16[14,32,128]{2,1,0:T(8,128)(2,1)S(1)}) custom-call(s32[112]{0:T(128)S(1)} %bitcast.8, bf16[112,128,128]{2,1,0:T(8,128)(2,1)S(1)} %bitcast.6, bf16[16,64,128]{2,1,0:T(8,128)(2,1)S(1)} %get-tuple-element.38.cot_ref.right_ref), custom_call_target="tpu_custom_call" | custom-call | flops 234881024 | bytes 3670016 | tf_op jit(solution)/shard_map/act/pallas_call | solution.py:328
  24.3 0.5 collective-permute-start.8
  24.8 0.8 %collective-permute-done.7.refs_0_ = bf16[14,32,128]{2,1,0:T(8,128)(2,1)S(1)} collective-permute-done((bf16[14,32,128]{2,1,0:T(8,128)(2,1)S(1)}, bf16[14,32,128]{2,1,0:T(8,128)(2,1)S(1)}, u32[]{:S(2)}, u32[]{:S(2)}) %collective-permute-start.7) | collective-permute-done | bytes 114720 | tf_op jit(solution)/shard_map/ppermute | solution.py:325
  25.8 0.6 %collective-permute-start.9 = (bf16[28,32,128]{2,1,0:T(8,128)(2,1)S(1)}, bf16[28,32,128]{2,1,0:T(8,128)(2,1)S(1)}, u32[]{:S(2)}, u32[]{:S(2)}) collective-permute-start(bf16[28,32,128]{2,1,0:T(8,128)(2,1)S(1)} %add.27.after_ref.own_ref), channel_id=1, source_target_pairs={{0,16},{8,24},{16,0},{24,8},{1,17},{9,25},{17,1},{25,9},{2,18},{10... | collective-permute-start | bytes 688136 | tf_op jit(solution)/shard_map/ppermute | solution.py:325
  26.4 1.5 %collective-permute-done.11.other_ref = bf16[28,32,128]{2,1,0:T(8,128)(2,1)S(1)} collective-permute-done((bf16[28,32,128]{2,1,0:T(8,128)(2,1)S(1)}, bf16[28,32,128]{2,1,0:T(8,128)(2,1)S(1)}, u32[]{:S(2)}, u32[]{:S(2)}) %collective-permute-start.11) | collective-permute-done | bytes 229408 | tf_op jit(solution)/shard_map/ppermute | solution.py:325
  28.3 0.5 collective-permute-start.13
  28.7 0.8 %collective-permute-done.12.refs_1_ = bf16[14,32,128]{2,1,0:T(8,128)(2,1)S(1)} collective-permute-done((bf16[14,32,128]{2,1,0:T(8,128)(2,1)S(1)}, bf16[14,32,128]{2,1,0:T(8,128)(2,1)S(1)}, u32[]{:S(2)}, u32[]{:S(2)}) %collective-permute-start.12) | collective-permute-done | bytes 114720 | tf_op jit(solution)/shard_map/ppermute | solution.py:325
  29.7 1.8 %down.1 = (bf16[28,64,128]{2,1,0:T(8,128)(2,1)S(1)}, bf16[16,64,128]{2,1,0:T(8,128)(2,1)S(1)}) custom-call(s32[112]{0:T(128)S(1)} %bitcast.9, bf16[112,128,128]{2,1,0:T(8,128)(2,1)S(1)} %bitcast.7, bf16[14,32,128]{2,1,0:T(8,128)(2,1)S(1)} %get-tuple-element.45.refs_0_, bf16[14,32,128]{2,1,0:T(8,128)(2,1)S(1)} %collective-permute-done.12.refs_1_, ...), custom_call_target="tpu_custom_call" | custom-call | flops 234881024 | bytes 3670016 | tf_op jit(solution)/shard_map/down/pallas_call | solution.py:328
  31.6 0.5 turn.1
  32.0 1.7 %collective-permute-done.9.other_ref = bf16[28,32,128]{2,1,0:T(8,128)(2,1)S(1)} collective-permute-done((bf16[28,32,128]{2,1,0:T(8,128)(2,1)S(1)}, bf16[28,32,128]{2,1,0:T(8,128)(2,1)S(1)}, u32[]{:S(2)}, u32[]{:S(2)}) %collective-permute-start.9) | collective-permute-done | bytes 229408 | tf_op jit(solution)/shard_map/ppermute | solution.py:325
  33.9 1.5 %collective-permute-done.14.other_ref = bf16[28,32,128]{2,1,0:T(8,128)(2,1)S(1)} collective-permute-done((bf16[28,32,128]{2,1,0:T(8,128)(2,1)S(1)}, bf16[28,32,128]{2,1,0:T(8,128)(2,1)S(1)}, u32[]{:S(2)}, u32[]{:S(2)}) %collective-permute-start.14) | collective-permute-done | bytes 229408 | tf_op jit(solution)/shard_map/ppermute | solution.py:325
  35.4 2.4 %input.1 = (bf16[28,64,128]{2,1,0:T(8,128)(2,1)S(1)}, bf16[2,16,2048]{2,1,0:T(8,128)(2,1)S(1)}, bf16[16,2048]{1,0:T(8,128)(2,1)S(1)}, bf16[16,2048]{1,0:T(8,128)...) custom-call(s32[112]{0:T(128)S(1)} %get-tuple-element.36.index_ref, ...), custom_call_target="tpu_custom_call" | custom-call | flops 234881024 | bytes 3670016 | tf_op jit(solution)/shard_map/input/pallas_call | solution.py:328
  37.8 1.5 %collective-permute-start.15 = (bf16[2,16,2048]{2,1,0:T(8,128)(2,1)S(1)}, bf16[2,16,2048]{2,1,0:T(8,128)(2,1)S(1)}, u32[]{:S(2)}, u32[]{:S(2)}) collective-permute-start(bf16[2,16,2048]{2,1,0:T(8,128)(2,1)S(1)} %get-tuple-element.51), channel_id=1, source_target_pairs={{0,1},{1,0},{2,3},{3,2},{4,5},{5,4},{6,7},{7,6},{8,9},{9,8},{10,11... | collective-permute-start | bytes 393224 | tf_op jit(solution)/shard_map/ppermute | solution.py:325
  39.2 3.1 %down_grad.1 = (bf16[112,128,128]{2,1,0:T(8,128)(2,1)}, f32[8,128]{1,0:T(8,128)S(1)}) custom-call(s32[112]{0:T(128)S(1)} %bitcast.10, bf16[28,128,64]{2,1,0:T(8,128)(2,1)S(1)} %get-tuple-element.52.turned_ref, bf16[16,64,128]{2,1,0:T(8,128)(2,1)S(1)} %get-tuple-element.38.cot_ref.right_ref), custom_call_target="tpu_custom_call" | custom-call | flops 234881024 | bytes 3670016 | tf_op jit(solution)/shard_map/down_grad/pallas_call | solution.py:328
  42.4 1.0 %collective-permute-done.15.refs_0_ = bf16[2,16,2048]{2,1,0:T(8,128)(2,1)S(1)} collective-permute-done((bf16[2,16,2048]{2,1,0:T(8,128)(2,1)S(1)}, bf16[2,16,2048]{2,1,0:T(8,128)(2,1)S(1)}, u32[]{:S(2)}, u32[]{:S(2)}) %collective-permute-start.15) | collective-permute-done | bytes 131104 | tf_op jit(solution)/shard_map/ppermute | solution.py:325
  43.4 2.7 %collective-permute-start.16 = (bf16[16,2048]{1,0:T(8,128)(2,1)S(1)}, bf16[16,2048]{1,0:T(8,128)(2,1)S(1)}, u32[]{:S(2)}, u32[]{:S(2)}) collective-permute-start(bf16[16,2048]{1,0:T(8,128)(2,1)S(1)} %get-tuple-element.60), channel_id=1, source_target_pairs={{0,6},{1,7},{2,4},{3,5},{4,2},{5,3},{6,0},{7,1},{8,14},{9,15},{10,... | collective-permute-start | bytes 196616 | tf_op jit(solution)/shard_map/ppermute | solution.py:325
  46.1 2.6 %collective-permute-start.18 = (bf16[16,2048]{1,0:T(8,128)(2,1)S(1)}, bf16[16,2048]{1,0:T(8,128)(2,1)S(1)}, u32[]{:S(2)}, u32[]{:S(2)}) collective-permute-start(bf16[16,2048]{1,0:T(8,128)(2,1)S(1)} %get-tuple-element.62), channel_id=1, source_target_pairs={{0,3},{1,2},{2,1},{3,0},{4,7},{5,6},{6,5},{7,4},{8,11},{9,10},{10,... | collective-permute-start | bytes 196616 | tf_op jit(solution)/shard_map/ppermute | solution.py:325
  48.7 0.6 %collective-permute-start.20 = (bf16[16,2048]{1,0:T(8,128)(2,1)S(1)}, bf16[16,2048]{1,0:T(8,128)(2,1)S(1)}, u32[]{:S(2)}, u32[]{:S(2)}) collective-permute-start(bf16[16,2048]{1,0:T(8,128)(2,1)S(1)} %get-tuple-element.64), channel_id=1, source_target_pairs={{0,1},{1,0},{2,3},{3,2},{4,5},{5,4},{6,7},{7,6},{8,9},{9,8},{10,11... | collective-permute-start | bytes 196616 | tf_op jit(solution)/shard_map/ppermute | solution.py:325
  49.3 3.7 %up_grad.1 = (bf16[112,128,128]{2,1,0:T(8,128)(2,1)}, f32[8,128]{1,0:T(8,128)}) custom-call(s32[112]{0:T(128)S(1)} %get-tuple-element.36.index_ref, bf16[16,128,64]{2,1,0:T(8,128)(2,1)S(1)} %get-tuple-element.49.after_ref.turned_ref, bf16[28,64,128]{2,1,0:T(8,128)(2,1)S(1)} %get-tuple-element.65.right_ref), custom_call_target="tpu_custom_call" | custom-call | flops 234881024 | bytes 3670016 | tf_op jit(solution)/shard_map/up_grad/pallas_call | solution.py:328
  53.2 0.6 %fusion = (bf16[8,2048]{1,0:T(8,128)(2,1)}, bf16[8,2048]{1,0:T(8,128)(2,1)}) fusion(bf16[16,2048]{1,0:T(8,128)(2,1)S(1)} %add_convert_fusion), kind=kLoop, calls=%fused_computation.1 | loop fusion | bytes 131072 | tf_op jit(solution)/shard_map/slice | solution.py:509
  (30 shorter events, 1.4 us)
Async XLA Ops:
  1.4 8.6 %collective-permute-start.5 = (bf16[16,2048]{1,0:T(8,128)(2,1)S(1)}, bf16[16,2048]{1,0:T(8,128)(2,1)S(1)}, u32[]{:S(2)}, u32[]{:S(2)}) collective-permute-start(bf16[16,2048]{1,0:T(8,128)(2,1)S(1)} %pack.1.refs_0_), channel_id=1, source_target_pairs={{0,6},{1,7},{2,4},{3,5},{4,2},{5,3},{6,0},{7,1},{8,14},{9,15},{10,... | collective-permute-start | bytes 196616 | tf_op jit(solution)/shard_map/ppermute | solution.py:325
  6.5 5.7 %collective-permute-start = (bf16[16,2048]{1,0:T(8,128)(2,1)S(1)}, bf16[16,2048]{1,0:T(8,128)(2,1)S(1)}, u32[]{:S(2)}, u32[]{:S(2)}) collective-permute-start(bf16[16,2048]{1,0:T(8,128)(2,1)S(1)} %pack.1.refs_0_), channel_id=1, source_target_pairs={{0,4},{1,5},{2,6},{3,7},{4,0},{5,1},{6,2},{7,3},{8,12},{9,13},{10,... | collective-permute-start | bytes 196616 | tf_op jit(solution)/shard_map/ppermute | solution.py:325
  6.6 10.0 %collective-permute-start.3 = (bf16[16,2048]{1,0:T(8,128)(2,1)S(1)}, bf16[16,2048]{1,0:T(8,128)(2,1)S(1)}, u32[]{:S(2)}, u32[]{:S(2)}) collective-permute-start(bf16[16,2048]{1,0:T(8,128)(2,1)S(1)} %pack.1.refs_0_), channel_id=1, source_target_pairs={{0,3},{1,2},{2,1},{3,0},{4,7},{5,6},{6,5},{7,4},{8,11},{9,10},{10,... | collective-permute-start | bytes 196616 | tf_op jit(solution)/shard_map/ppermute | solution.py:325
  8.3 8.3 %collective-permute-start.2 = (bf16[16,2048]{1,0:T(8,128)(2,1)S(1)}, bf16[16,2048]{1,0:T(8,128)(2,1)S(1)}, u32[]{:S(2)}, u32[]{:S(2)}) collective-permute-start(bf16[16,2048]{1,0:T(8,128)(2,1)S(1)} %pack.1.refs_0_), channel_id=1, source_target_pairs={{0,2},{1,3},{2,0},{3,1},{4,6},{5,7},{6,4},{7,5},{8,10},{9,11},{10,... | collective-permute-start | bytes 196616 | tf_op jit(solution)/shard_map/ppermute | solution.py:325
  9.5 7.1 %collective-permute-start.1 = (bf16[16,2048]{1,0:T(8,128)(2,1)S(1)}, bf16[16,2048]{1,0:T(8,128)(2,1)S(1)}, u32[]{:S(2)}, u32[]{:S(2)}) collective-permute-start(bf16[16,2048]{1,0:T(8,128)(2,1)S(1)} %pack.1.refs_0_), channel_id=1, source_target_pairs={{0,1},{1,0},{2,3},{3,2},{4,5},{5,4},{6,7},{7,6},{8,9},{9,8},{10,11... | collective-permute-start | bytes 196616 | tf_op jit(solution)/shard_map/ppermute | solution.py:325
  10.0 6.5 %collective-permute-start.6 = (bf16[16,2048]{1,0:T(8,128)(2,1)S(1)}, bf16[16,2048]{1,0:T(8,128)(2,1)S(1)}, u32[]{:S(2)}, u32[]{:S(2)}) collective-permute-start(bf16[16,2048]{1,0:T(8,128)(2,1)S(1)} %collective-permute-done.5.refs_6_), channel_id=1, source_target_pairs={{0,1},{1,0},{2,3},{3,2},{4,5},{5,4},{6,7},{7,6},{8,9},{9,8},{10,11... | collective-permute-start | bytes 196616 | tf_op jit(solution)/shard_map/ppermute | solution.py:325
  12.3 4.3 %collective-permute-start.4 = (bf16[16,2048]{1,0:T(8,128)(2,1)S(1)}, bf16[16,2048]{1,0:T(8,128)(2,1)S(1)}, u32[]{:S(2)}, u32[]{:S(2)}) collective-permute-start(bf16[16,2048]{1,0:T(8,128)(2,1)S(1)} %collective-permute-done.after_ref.refs_4_), channel_id=1, source_target_pairs={{0,1},{1,0},{2,3},{3,2},{4,5},{5,4},{6,7},{7,6},{8,9},{9,8},{10,11... | collective-permute-start | bytes 196616 | tf_op jit(solution)/shard_map/ppermute | solution.py:325
  13.7 8.0 %copy-start = (bf16[1,1,112,128,128]{4,3,2,1,0:T(8,128)(2,1)S(1)}, bf16[1,1,112,128,128]{4,3,2,1,0:T(8,128)(2,1)}, u32[]{:S(2)}) copy-start(bf16[1,1,112,128,128]{4,3,2,1,0:T(8,128)(2,1)} %param.9) | copy-start | bytes 11010052
  13.7 8.0 %copy-start.1 = (s32[1,1,112]{2,1,0:T(1,128)S(1)}, s32[1,1,112]{2,1,0:T(1,128)}, u32[]{:S(2)}) copy-start(s32[1,1,112]{2,1,0:T(1,128)} %param.10) | copy-start | bytes 1348
  18.5 1.6 %collective-permute-start.10 = (bf16[28,32,128]{2,1,0:T(8,128)(2,1)S(1)}, bf16[28,32,128]{2,1,0:T(8,128)(2,1)S(1)}, u32[]{:S(2)}, u32[]{:S(2)}) collective-permute-start(bf16[28,32,128]{2,1,0:T(8,128)(2,1)S(1)} %get-tuple-element.43), channel_id=1, source_target_pairs={{0,8},{8,0},{16,24},{24,16},{1,9},{9,1},{17,25},{25,17},{2,10},{10... | collective-permute-start | bytes 688136 | tf_op jit(solution)/shard_map/ppermute | solution.py:325
  20.1 7.7 %collective-permute-start.11 = (bf16[28,32,128]{2,1,0:T(8,128)(2,1)S(1)}, bf16[28,32,128]{2,1,0:T(8,128)(2,1)S(1)}, u32[]{:S(2)}, u32[]{:S(2)}) collective-permute-start(bf16[28,32,128]{2,1,0:T(8,128)(2,1)S(1)} %add.28.own_ref), channel_id=1, source_target_pairs={{0,16},{8,24},{16,0},{24,8},{1,17},{9,25},{17,1},{25,9},{2,18},{10... | collective-permute-start | bytes 688136 | tf_op jit(solution)/shard_map/ppermute | solution.py:325
  24.2 1.4 %collective-permute-start.7 = (bf16[14,32,128]{2,1,0:T(8,128)(2,1)S(1)}, bf16[14,32,128]{2,1,0:T(8,128)(2,1)S(1)}, u32[]{:S(2)}, u32[]{:S(2)}) collective-permute-start(bf16[14,32,128]{2,1,0:T(8,128)(2,1)S(1)} %get-tuple-element.40), channel_id=1, source_target_pairs={{0,8},{8,0},{16,24},{24,16},{1,9},{9,1},{17,25},{25,17},{2,10},{10... | collective-permute-start | bytes 344072 | tf_op jit(solution)/shard_map/ppermute | solution.py:325
  24.3 1.5 %collective-permute-start.8 = (bf16[14,32,128]{2,1,0:T(8,128)(2,1)S(1)}, bf16[14,32,128]{2,1,0:T(8,128)(2,1)S(1)}, u32[]{:S(2)}, u32[]{:S(2)}) collective-permute-start(bf16[14,32,128]{2,1,0:T(8,128)(2,1)S(1)} %get-tuple-element.41), channel_id=1, source_target_pairs={{0,8},{8,0},{16,24},{24,16},{1,9},{9,1},{17,25},{25,17},{2,10},{10... | collective-permute-start | bytes 344072 | tf_op jit(solution)/shard_map/ppermute | solution.py:325
  25.8 7.9 %collective-permute-start.9 = (bf16[28,32,128]{2,1,0:T(8,128)(2,1)S(1)}, bf16[28,32,128]{2,1,0:T(8,128)(2,1)S(1)}, u32[]{:S(2)}, u32[]{:S(2)}) collective-permute-start(bf16[28,32,128]{2,1,0:T(8,128)(2,1)S(1)} %add.27.after_ref.own_ref), channel_id=1, source_target_pairs={{0,16},{8,24},{16,0},{24,8},{1,17},{9,25},{17,1},{25,9},{2,18},{10... | collective-permute-start | bytes 688136 | tf_op jit(solution)/shard_map/ppermute | solution.py:325
  28.2 1.4 %collective-permute-start.12 = (bf16[14,32,128]{2,1,0:T(8,128)(2,1)S(1)}, bf16[14,32,128]{2,1,0:T(8,128)(2,1)S(1)}, u32[]{:S(2)}, u32[]{:S(2)}) collective-permute-start(bf16[14,32,128]{2,1,0:T(8,128)(2,1)S(1)} %get-tuple-element.45.refs_0_), channel_id=1, source_target_pairs={{0,8},{8,0},{16,24},{24,16},{1,9},{9,1},{17,25},{25,17},{2,10},{10... | collective-permute-start | bytes 344072 | tf_op jit(solution)/shard_map/ppermute | solution.py:325
  28.3 1.5 %collective-permute-start.13 = (bf16[14,32,128]{2,1,0:T(8,128)(2,1)S(1)}, bf16[14,32,128]{2,1,0:T(8,128)(2,1)S(1)}, u32[]{:S(2)}, u32[]{:S(2)}) collective-permute-start(bf16[14,32,128]{2,1,0:T(8,128)(2,1)S(1)} %get-tuple-element.46.refs_2_), channel_id=1, source_target_pairs={{0,8},{8,0},{16,24},{24,16},{1,9},{9,1},{17,25},{25,17},{2,10},{10... | collective-permute-start | bytes 344072 | tf_op jit(solution)/shard_map/ppermute | solution.py:325
  33.8 1.6 %collective-permute-start.14 = (bf16[28,32,128]{2,1,0:T(8,128)(2,1)S(1)}, bf16[28,32,128]{2,1,0:T(8,128)(2,1)S(1)}, u32[]{:S(2)}, u32[]{:S(2)}) collective-permute-start(bf16[28,32,128]{2,1,0:T(8,128)(2,1)S(1)} %slope.1.own_ref), channel_id=1, source_target_pairs={{0,8},{8,0},{16,24},{24,16},{1,9},{9,1},{17,25},{25,17},{2,10},{10... | collective-permute-start | bytes 688136 | tf_op jit(solution)/shard_map/ppermute | solution.py:325
  37.8 5.6 %collective-permute-start.15 = (bf16[2,16,2048]{2,1,0:T(8,128)(2,1)S(1)}, bf16[2,16,2048]{2,1,0:T(8,128)(2,1)S(1)}, u32[]{:S(2)}, u32[]{:S(2)}) collective-permute-start(bf16[2,16,2048]{2,1,0:T(8,128)(2,1)S(1)} %get-tuple-element.51), channel_id=1, source_target_pairs={{0,1},{1,0},{2,3},{3,2},{4,5},{5,4},{6,7},{7,6},{8,9},{9,8},{10,11... | collective-permute-start | bytes 393224 | tf_op jit(solution)/shard_map/ppermute | solution.py:325
  42.3 10.8 %collective-permute-start.19 = (bf16[16,2048]{1,0:T(8,128)(2,1)S(1)}, bf16[16,2048]{1,0:T(8,128)(2,1)S(1)}, u32[]{:S(2)}, u32[]{:S(2)}) collective-permute-start(bf16[16,2048]{1,0:T(8,128)(2,1)S(1)} %get-tuple-element.63), channel_id=1, source_target_pairs={{0,2},{1,3},{2,0},{3,1},{4,6},{5,7},{6,4},{7,5},{8,10},{9,11},{10,... | collective-permute-start | bytes 196616 | tf_op jit(solution)/shard_map/ppermute | solution.py:325
  43.4 9.7 %collective-permute-start.16 = (bf16[16,2048]{1,0:T(8,128)(2,1)S(1)}, bf16[16,2048]{1,0:T(8,128)(2,1)S(1)}, u32[]{:S(2)}, u32[]{:S(2)}) collective-permute-start(bf16[16,2048]{1,0:T(8,128)(2,1)S(1)} %get-tuple-element.60), channel_id=1, source_target_pairs={{0,6},{1,7},{2,4},{3,5},{4,2},{5,3},{6,0},{7,1},{8,14},{9,15},{10,... | collective-permute-start | bytes 196616 | tf_op jit(solution)/shard_map/ppermute | solution.py:325
  46.1 7.0 %collective-permute-start.17 = (bf16[16,2048]{1,0:T(8,128)(2,1)S(1)}, bf16[16,2048]{1,0:T(8,128)(2,1)S(1)}, u32[]{:S(2)}, u32[]{:S(2)}) collective-permute-start(bf16[16,2048]{1,0:T(8,128)(2,1)S(1)} %get-tuple-element.61), channel_id=1, source_target_pairs={{0,4},{1,5},{2,6},{3,7},{4,0},{5,1},{6,2},{7,3},{8,12},{9,13},{10,... | collective-permute-start | bytes 196616 | tf_op jit(solution)/shard_map/ppermute | solution.py:325
  46.1 7.0 %collective-permute-start.18 = (bf16[16,2048]{1,0:T(8,128)(2,1)S(1)}, bf16[16,2048]{1,0:T(8,128)(2,1)S(1)}, u32[]{:S(2)}, u32[]{:S(2)}) collective-permute-start(bf16[16,2048]{1,0:T(8,128)(2,1)S(1)} %get-tuple-element.62), channel_id=1, source_target_pairs={{0,3},{1,2},{2,1},{3,0},{4,7},{5,6},{6,5},{7,4},{8,11},{9,10},{10,... | collective-permute-start | bytes 196616 | tf_op jit(solution)/shard_map/ppermute | solution.py:325
  48.7 4.4 %collective-permute-start.20 = (bf16[16,2048]{1,0:T(8,128)(2,1)S(1)}, bf16[16,2048]{1,0:T(8,128)(2,1)S(1)}, u32[]{:S(2)}, u32[]{:S(2)}) collective-permute-start(bf16[16,2048]{1,0:T(8,128)(2,1)S(1)} %get-tuple-element.64), channel_id=1, source_target_pairs={{0,1},{1,0},{2,3},{3,2},{4,5},{5,4},{6,7},{7,6},{8,9},{9,8},{10,11... | collective-permute-start | bytes 196616 | tf_op jit(solution)/shard_map/ppermute | solution.py:325

commit v7 on v6

--- a/solution.py
+++ b/solution.py
@@ -143,16 +143,8 @@
     return position("row") % 2
 
 
-def pack_kernel(tokens_ref, cot_ref, mine_ref, held, sems):
-    copies = [
-        pltpu.make_async_copy(source, held.at[at], sems.at[at])
-        for at, source in enumerate((tokens_ref, cot_ref))
-    ]
-    for copy in copies:
-        copy.start()
-    for copy in copies:
-        copy.wait()
-    mine_ref[...] = jnp.concatenate([held[0].astype(F32), held[1].astype(F32)]).astype(BF16)
+def pack_kernel(tokens_ref, cot_ref, mine_ref):
+    mine_ref[...] = jnp.concatenate([tokens_ref[...].astype(F32), cot_ref[...].astype(F32)]).astype(BF16)
 
 
 def fetch_kernel(index_hbm, blocks_hbm, after_ref, index_ref, blocks_ref, sems):
@@ -344,8 +336,8 @@
         pack_kernel,
         "pack",
         shape(2 * rows, width),
-        [HBM] * 2,
-        [pltpu.VMEM((2, rows, width), BF16), pltpu.SemaphoreType.DMA((2,))],
+        [pl.BlockSpec((rows, width), lambda: (0, 0))] * 2,
+        [],
         pltpu.with_memory_space_constraint(tokens, pltpu.HBM),
         pltpu.with_memory_space_constraint(out_cot, pltpu.HBM),
         cost_estimate=long,

time: 54 us -> 53.9 us (level)
  no operation moved by 1% of the time
where the time goes in v7:
time: 53.9 us; the launch traced here: 53.7 us
  starting transfers between devices  22.4 us (42%)
  Pallas kernels  20 us (37%)
  waiting for transfers between devices  9.79 us (18%)
  between operations  0.84 us (2%)
  local copies, waits for them, and re-layouts  0.64 us (1%)
    ppermute x21, starting transfers between devices, swap(): return lax.ppermute(values, axis, [(at, at ^ bit) for at in range(count)])  22.4 us
    pallas_call x14, Pallas kernels, call(): pl.pallas_call(body, out_shape=outs, in_specs=ins, out_specs=out_specs or...  20 us
    ppermute x21, waiting for transfers between devices, swap(): return lax.ppermute(values, axis, [(at, at ^ bit) for at in range(count)])  9.79 us
  transfers between devices with their start and end apart: 21, of which 10 were waited for; matrix products, arithmetic and copies ran while one was open for 0% of the time, Pallas kernels for 28%

profile of v7, /device:TPU:0, one launch (start us, length us, event | category | flops | bytes accessed | tf_op | source)
XLA Modules:
  0.0 53.7 jit_solution(9022102605328429910)
XLA Ops:
  0.6 0.8 %pack.1.refs_0_ = bf16[16,2048]{1,0:T(8,128)(2,1)S(1)} custom-call(bf16[8,2048]{1,0:T(8,128)(2,1)} %tokens_ref.1, bf16[8,2048]{1,0:T(8,128)(2,1)} %cot_ref.1), custom_call_target="tpu_custom_call" | custom-call | bytes 33554432 | tf_op jit(solution)/shard_map/pack/pallas_call | solution.py:320
  1.4 5.0 %collective-permute-start.5 = (bf16[16,2048]{1,0:T(8,128)(2,1)S(1)}, bf16[16,2048]{1,0:T(8,128)(2,1)S(1)}, u32[]{:S(2)}, u32[]{:S(2)}) collective-permute-start(bf16[16,2048]{1,0:T(8,128)(2,1)S(1)} %pack.1.refs_0_), channel_id=1, source_target_pairs={{0,6},{1,7},{2,4},{3,5},{4,2},{5,3},{6,0},{7,1},{8,14},{9,15},{10,... | collective-permute-start | bytes 196616 | tf_op jit(solution)/shard_map/ppermute | solution.py:317
  6.5 1.7 %collective-permute-start.3 = (bf16[16,2048]{1,0:T(8,128)(2,1)S(1)}, bf16[16,2048]{1,0:T(8,128)(2,1)S(1)}, u32[]{:S(2)}, u32[]{:S(2)}) collective-permute-start(bf16[16,2048]{1,0:T(8,128)(2,1)S(1)} %pack.1.refs_0_), channel_id=1, source_target_pairs={{0,3},{1,2},{2,1},{3,0},{4,7},{5,6},{6,5},{7,4},{8,11},{9,10},{10,... | collective-permute-start | bytes 196616 | tf_op jit(solution)/shard_map/ppermute | solution.py:317
  8.2 1.2 %collective-permute-start.2 = (bf16[16,2048]{1,0:T(8,128)(2,1)S(1)}, bf16[16,2048]{1,0:T(8,128)(2,1)S(1)}, u32[]{:S(2)}, u32[]{:S(2)}) collective-permute-start(bf16[16,2048]{1,0:T(8,128)(2,1)S(1)} %pack.1.refs_0_), channel_id=1, source_target_pairs={{0,2},{1,3},{2,0},{3,1},{4,6},{5,7},{6,4},{7,5},{8,10},{9,11},{10,... | collective-permute-start | bytes 196616 | tf_op jit(solution)/shard_map/ppermute | solution.py:317
  9.4 0.5 collective-permute-start.1
  10.0 1.5 %collective-permute-start.6 = (bf16[16,2048]{1,0:T(8,128)(2,1)S(1)}, bf16[16,2048]{1,0:T(8,128)(2,1)S(1)}, u32[]{:S(2)}, u32[]{:S(2)}) collective-permute-start(bf16[16,2048]{1,0:T(8,128)(2,1)S(1)} %collective-permute-done.5.refs_6_), channel_id=1, source_target_pairs={{0,1},{1,0},{2,3},{3,2},{4,5},{5,4},{6,7},{7,6},{8,9},{9,8},{10,11... | collective-permute-start | bytes 196616 | tf_op jit(solution)/shard_map/ppermute | solution.py:317
  11.4 0.7 %collective-permute-done.after_ref.refs_4_ = bf16[16,2048]{1,0:T(8,128)(2,1)S(1)} collective-permute-done((bf16[16,2048]{1,0:T(8,128)(2,1)S(1)}, bf16[16,2048]{1,0:T(8,128)(2,1)S(1)}, u32[]{:S(2)}, u32[]{:S(2)}) %collective-permute-start) | collective-permute-done | bytes 65568 | tf_op jit(solution)/shard_map/ppermute | solution.py:317
  12.2 1.5 %collective-permute-start.4 = (bf16[16,2048]{1,0:T(8,128)(2,1)S(1)}, bf16[16,2048]{1,0:T(8,128)(2,1)S(1)}, u32[]{:S(2)}, u32[]{:S(2)}) collective-permute-start(bf16[16,2048]{1,0:T(8,128)(2,1)S(1)} %collective-permute-done.after_ref.refs_4_), channel_id=1, source_target_pairs={{0,1},{1,0},{2,3},{3,2},{4,5},{5,4},{6,7},{7,6},{8,9},{9,8},{10,11... | collective-permute-start | bytes 196616 | tf_op jit(solution)/shard_map/ppermute | solution.py:317
  13.7 2.8 %fetch.1 = (s32[112]{0:T(128)S(1)}, bf16[112,128,128]{2,1,0:T(8,128)(2,1)S(1)}) custom-call(s32[112]{0:T(128)} %bitcast.12, bf16[112,128,128]{2,1,0:T(8,128)(2,1)} %bitcast.11, bf16[16,2048]{1,0:T(8,128)(2,1)S(1)} %collective-permute-done.after_ref.refs_4_), custom_call_target="tpu_custom_call" | custom-call | flops 234881024 | bytes 3670016 | tf_op jit(solution)/shard_map/fetch/pallas_call | solution.py:320
  16.5 1.9 %up.1 = (bf16[16,64,128]{2,1,0:T(8,128)(2,1)S(1)}, bf16[16,64,128]{2,1,0:T(8,128)(2,1)S(1)}, bf16[28,32,128]{2,1,0:T(8,128)(2,1)S(1)}, bf16[28,32,128]{2,1,0:T(8,128)(2,1)S(1)}) custom-call(s32[112]{0:T(128)S(1)} %get-tuple-element.36.index_ref, bf16[112,128,128]{2,1,0:T(8,128)(2,1)S(1)} %get-tuple-element.37.blocks_ref, bf16[16,2048]{1,0:T(8,128)(2,1)S(1)} %pack.1.refs_0_, ...), custom_call_target="tpu_custom_call" | custom-call | flops 234881024 | bytes 3670016 | tf_op jit(solution)/shard_map/up/pallas_call | solution.py:320
  18.5 1.5 %collective-permute-done.10.refs_0_ = bf16[28,32,128]{2,1,0:T(8,128)(2,1)S(1)} collective-permute-done((bf16[28,32,128]{2,1,0:T(8,128)(2,1)S(1)}, bf16[28,32,128]{2,1,0:T(8,128)(2,1)S(1)}, u32[]{:S(2)}, u32[]{:S(2)}) %collective-permute-start.10) | collective-permute-done | bytes 229408 | tf_op jit(solution)/shard_map/ppermute | solution.py:317
  20.0 1.6 %collective-permute-start.11 = (bf16[28,32,128]{2,1,0:T(8,128)(2,1)S(1)}, bf16[28,32,128]{2,1,0:T(8,128)(2,1)S(1)}, u32[]{:S(2)}, u32[]{:S(2)}) collective-permute-start(bf16[28,32,128]{2,1,0:T(8,128)(2,1)S(1)} %add.28.own_ref), channel_id=1, source_target_pairs={{0,16},{8,24},{16,0},{24,8},{1,17},{9,25},{17,1},{25,9},{2,18},{10... | collective-permute-start | bytes 688136 | tf_op jit(solution)/shard_map/ppermute | solution.py:317
  21.6 2.5 %act.1 = (bf16[28,32,128]{2,1,0:T(8,128)(2,1)S(1)}, bf16[14,32,128]{2,1,0:T(8,128)(2,1)S(1)}, bf16[14,32,128]{2,1,0:T(8,128)(2,1)S(1)}) custom-call(s32[112]{0:T(128)S(1)} %bitcast.8, bf16[112,128,128]{2,1,0:T(8,128)(2,1)S(1)} %bitcast.6, bf16[16,64,128]{2,1,0:T(8,128)(2,1)S(1)} %get-tuple-element.38.cot_ref.right_ref), custom_call_target="tpu_custom_call" | custom-call | flops 234881024 | bytes 3670016 | tf_op jit(solution)/shard_map/act/pallas_call | solution.py:320
  24.2 0.5 collective-permute-start.8
  24.7 0.8 %collective-permute-done.7.refs_0_ = bf16[14,32,128]{2,1,0:T(8,128)(2,1)S(1)} collective-permute-done((bf16[14,32,128]{2,1,0:T(8,128)(2,1)S(1)}, bf16[14,32,128]{2,1,0:T(8,128)(2,1)S(1)}, u32[]{:S(2)}, u32[]{:S(2)}) %collective-permute-start.7) | collective-permute-done | bytes 114720 | tf_op jit(solution)/shard_map/ppermute | solution.py:317
  25.7 0.6 %collective-permute-start.9 = (bf16[28,32,128]{2,1,0:T(8,128)(2,1)S(1)}, bf16[28,32,128]{2,1,0:T(8,128)(2,1)S(1)}, u32[]{:S(2)}, u32[]{:S(2)}) collective-permute-start(bf16[28,32,128]{2,1,0:T(8,128)(2,1)S(1)} %add.27.after_ref.own_ref), channel_id=1, source_target_pairs={{0,16},{8,24},{16,0},{24,8},{1,17},{9,25},{17,1},{25,9},{2,18},{10... | collective-permute-start | bytes 688136 | tf_op jit(solution)/shard_map/ppermute | solution.py:317
  26.3 1.5 %collective-permute-done.11.other_ref = bf16[28,32,128]{2,1,0:T(8,128)(2,1)S(1)} collective-permute-done((bf16[28,32,128]{2,1,0:T(8,128)(2,1)S(1)}, bf16[28,32,128]{2,1,0:T(8,128)(2,1)S(1)}, u32[]{:S(2)}, u32[]{:S(2)}) %collective-permute-start.11) | collective-permute-done | bytes 229408 | tf_op jit(solution)/shard_map/ppermute | solution.py:317
  28.2 0.5 collective-permute-start.13
  28.7 0.8 %collective-permute-done.12.refs_1_ = bf16[14,32,128]{2,1,0:T(8,128)(2,1)S(1)} collective-permute-done((bf16[14,32,128]{2,1,0:T(8,128)(2,1)S(1)}, bf16[14,32,128]{2,1,0:T(8,128)(2,1)S(1)}, u32[]{:S(2)}, u32[]{:S(2)}) %collective-permute-start.12) | collective-permute-done | bytes 114720 | tf_op jit(solution)/shard_map/ppermute | solution.py:317
  29.6 1.8 %down.1 = (bf16[28,64,128]{2,1,0:T(8,128)(2,1)S(1)}, bf16[16,64,128]{2,1,0:T(8,128)(2,1)S(1)}) custom-call(s32[112]{0:T(128)S(1)} %bitcast.9, bf16[112,128,128]{2,1,0:T(8,128)(2,1)S(1)} %bitcast.7, bf16[14,32,128]{2,1,0:T(8,128)(2,1)S(1)} %get-tuple-element.45.refs_0_, bf16[14,32,128]{2,1,0:T(8,128)(2,1)S(1)} %collective-permute-done.12.refs_1_, ...), custom_call_target="tpu_custom_call" | custom-call | flops 234881024 | bytes 3670016 | tf_op jit(solution)/shard_map/down/pallas_call | solution.py:320
  31.5 0.5 turn.1
  31.9 1.7 %collective-permute-done.9.other_ref = bf16[28,32,128]{2,1,0:T(8,128)(2,1)S(1)} collective-permute-done((bf16[28,32,128]{2,1,0:T(8,128)(2,1)S(1)}, bf16[28,32,128]{2,1,0:T(8,128)(2,1)S(1)}, u32[]{:S(2)}, u32[]{:S(2)}) %collective-permute-start.9) | collective-permute-done | bytes 229408 | tf_op jit(solution)/shard_map/ppermute | solution.py:317
  33.8 1.5 %collective-permute-done.14.other_ref = bf16[28,32,128]{2,1,0:T(8,128)(2,1)S(1)} collective-permute-done((bf16[28,32,128]{2,1,0:T(8,128)(2,1)S(1)}, bf16[28,32,128]{2,1,0:T(8,128)(2,1)S(1)}, u32[]{:S(2)}, u32[]{:S(2)}) %collective-permute-start.14) | collective-permute-done | bytes 229408 | tf_op jit(solution)/shard_map/ppermute | solution.py:317
  35.3 2.4 %input.1 = (bf16[28,64,128]{2,1,0:T(8,128)(2,1)S(1)}, bf16[2,16,2048]{2,1,0:T(8,128)(2,1)S(1)}, bf16[16,2048]{1,0:T(8,128)(2,1)S(1)}, bf16[16,2048]{1,0:T(8,128)...) custom-call(s32[112]{0:T(128)S(1)} %get-tuple-element.36.index_ref, ...), custom_call_target="tpu_custom_call" | custom-call | flops 234881024 | bytes 3670016 | tf_op jit(solution)/shard_map/input/pallas_call | solution.py:320
  37.7 1.4 %collective-permute-start.15 = (bf16[2,16,2048]{2,1,0:T(8,128)(2,1)S(1)}, bf16[2,16,2048]{2,1,0:T(8,128)(2,1)S(1)}, u32[]{:S(2)}, u32[]{:S(2)}) collective-permute-start(bf16[2,16,2048]{2,1,0:T(8,128)(2,1)S(1)} %get-tuple-element.51), channel_id=1, source_target_pairs={{0,1},{1,0},{2,3},{3,2},{4,5},{5,4},{6,7},{7,6},{8,9},{9,8},{10,11... | collective-permute-start | bytes 393224 | tf_op jit(solution)/shard_map/ppermute | solution.py:317
  39.1 3.1 %down_grad.1 = (bf16[112,128,128]{2,1,0:T(8,128)(2,1)}, f32[8,128]{1,0:T(8,128)S(1)}) custom-call(s32[112]{0:T(128)S(1)} %bitcast.10, bf16[28,128,64]{2,1,0:T(8,128)(2,1)S(1)} %get-tuple-element.52.turned_ref, bf16[16,64,128]{2,1,0:T(8,128)(2,1)S(1)} %get-tuple-element.38.cot_ref.right_ref), custom_call_target="tpu_custom_call" | custom-call | flops 234881024 | bytes 3670016 | tf_op jit(solution)/shard_map/down_grad/pallas_call | solution.py:320
  42.3 1.0 %collective-permute-done.15.refs_0_ = bf16[2,16,2048]{2,1,0:T(8,128)(2,1)S(1)} collective-permute-done((bf16[2,16,2048]{2,1,0:T(8,128)(2,1)S(1)}, bf16[2,16,2048]{2,1,0:T(8,128)(2,1)S(1)}, u32[]{:S(2)}, u32[]{:S(2)}) %collective-permute-start.15) | collective-permute-done | bytes 131104 | tf_op jit(solution)/shard_map/ppermute | solution.py:317
  43.3 2.7 %collective-permute-start.16 = (bf16[16,2048]{1,0:T(8,128)(2,1)S(1)}, bf16[16,2048]{1,0:T(8,128)(2,1)S(1)}, u32[]{:S(2)}, u32[]{:S(2)}) collective-permute-start(bf16[16,2048]{1,0:T(8,128)(2,1)S(1)} %get-tuple-element.60), channel_id=1, source_target_pairs={{0,6},{1,7},{2,4},{3,5},{4,2},{5,3},{6,0},{7,1},{8,14},{9,15},{10,... | collective-permute-start | bytes 196616 | tf_op jit(solution)/shard_map/ppermute | solution.py:317
  46.0 2.6 %collective-permute-start.18 = (bf16[16,2048]{1,0:T(8,128)(2,1)S(1)}, bf16[16,2048]{1,0:T(8,128)(2,1)S(1)}, u32[]{:S(2)}, u32[]{:S(2)}) collective-permute-start(bf16[16,2048]{1,0:T(8,128)(2,1)S(1)} %get-tuple-element.62), channel_id=1, source_target_pairs={{0,3},{1,2},{2,1},{3,0},{4,7},{5,6},{6,5},{7,4},{8,11},{9,10},{10,... | collective-permute-start | bytes 196616 | tf_op jit(solution)/shard_map/ppermute | solution.py:317
  48.6 0.6 %collective-permute-start.20 = (bf16[16,2048]{1,0:T(8,128)(2,1)S(1)}, bf16[16,2048]{1,0:T(8,128)(2,1)S(1)}, u32[]{:S(2)}, u32[]{:S(2)}) collective-permute-start(bf16[16,2048]{1,0:T(8,128)(2,1)S(1)} %get-tuple-element.64), channel_id=1, source_target_pairs={{0,1},{1,0},{2,3},{3,2},{4,5},{5,4},{6,7},{7,6},{8,9},{9,8},{10,11... | collective-permute-start | bytes 196616 | tf_op jit(solution)/shard_map/ppermute | solution.py:317
  49.3 3.7 %up_grad.1 = (bf16[112,128,128]{2,1,0:T(8,128)(2,1)}, f32[8,128]{1,0:T(8,128)}) custom-call(s32[112]{0:T(128)S(1)} %get-tuple-element.36.index_ref, bf16[16,128,64]{2,1,0:T(8,128)(2,1)S(1)} %get-tuple-element.49.after_ref.turned_ref, bf16[28,64,128]{2,1,0:T(8,128)(2,1)S(1)} %get-tuple-element.65.right_ref), custom_call_target="tpu_custom_call" | custom-call | flops 234881024 | bytes 3670016 | tf_op jit(solution)/shard_map/up_grad/pallas_call | solution.py:320
  53.1 0.6 %fusion = (bf16[8,2048]{1,0:T(8,128)(2,1)}, bf16[8,2048]{1,0:T(8,128)(2,1)}) fusion(bf16[16,2048]{1,0:T(8,128)(2,1)S(1)} %add_convert_fusion), kind=kLoop, calls=%fused_computation.1 | loop fusion | bytes 131072 | tf_op jit(solution)/shard_map/slice | solution.py:501
  (30 shorter events, 1.4 us)
Async XLA Ops:
  1.4 8.5 %collective-permute-start.5 = (bf16[16,2048]{1,0:T(8,128)(2,1)S(1)}, bf16[16,2048]{1,0:T(8,128)(2,1)S(1)}, u32[]{:S(2)}, u32[]{:S(2)}) collective-permute-start(bf16[16,2048]{1,0:T(8,128)(2,1)S(1)} %pack.1.refs_0_), channel_id=1, source_target_pairs={{0,6},{1,7},{2,4},{3,5},{4,2},{5,3},{6,0},{7,1},{8,14},{9,15},{10,... | collective-permute-start | bytes 196616 | tf_op jit(solution)/shard_map/ppermute | solution.py:317
  6.5 5.7 %collective-permute-start = (bf16[16,2048]{1,0:T(8,128)(2,1)S(1)}, bf16[16,2048]{1,0:T(8,128)(2,1)S(1)}, u32[]{:S(2)}, u32[]{:S(2)}) collective-permute-start(bf16[16,2048]{1,0:T(8,128)(2,1)S(1)} %pack.1.refs_0_), channel_id=1, source_target_pairs={{0,4},{1,5},{2,6},{3,7},{4,0},{5,1},{6,2},{7,3},{8,12},{9,13},{10,... | collective-permute-start | bytes 196616 | tf_op jit(solution)/shard_map/ppermute | solution.py:317
  6.5 10.0 %collective-permute-start.3 = (bf16[16,2048]{1,0:T(8,128)(2,1)S(1)}, bf16[16,2048]{1,0:T(8,128)(2,1)S(1)}, u32[]{:S(2)}, u32[]{:S(2)}) collective-permute-start(bf16[16,2048]{1,0:T(8,128)(2,1)S(1)} %pack.1.refs_0_), channel_id=1, source_target_pairs={{0,3},{1,2},{2,1},{3,0},{4,7},{5,6},{6,5},{7,4},{8,11},{9,10},{10,... | collective-permute-start | bytes 196616 | tf_op jit(solution)/shard_map/ppermute | solution.py:317
  8.2 8.3 %collective-permute-start.2 = (bf16[16,2048]{1,0:T(8,128)(2,1)S(1)}, bf16[16,2048]{1,0:T(8,128)(2,1)S(1)}, u32[]{:S(2)}, u32[]{:S(2)}) collective-permute-start(bf16[16,2048]{1,0:T(8,128)(2,1)S(1)} %pack.1.refs_0_), channel_id=1, source_target_pairs={{0,2},{1,3},{2,0},{3,1},{4,6},{5,7},{6,4},{7,5},{8,10},{9,11},{10,... | collective-permute-start | bytes 196616 | tf_op jit(solution)/shard_map/ppermute | solution.py:317
  9.4 7.1 %collective-permute-start.1 = (bf16[16,2048]{1,0:T(8,128)(2,1)S(1)}, bf16[16,2048]{1,0:T(8,128)(2,1)S(1)}, u32[]{:S(2)}, u32[]{:S(2)}) collective-permute-start(bf16[16,2048]{1,0:T(8,128)(2,1)S(1)} %pack.1.refs_0_), channel_id=1, source_target_pairs={{0,1},{1,0},{2,3},{3,2},{4,5},{5,4},{6,7},{7,6},{8,9},{9,8},{10,11... | collective-permute-start | bytes 196616 | tf_op jit(solution)/shard_map/ppermute | solution.py:317
  10.0 6.5 %collective-permute-start.6 = (bf16[16,2048]{1,0:T(8,128)(2,1)S(1)}, bf16[16,2048]{1,0:T(8,128)(2,1)S(1)}, u32[]{:S(2)}, u32[]{:S(2)}) collective-permute-start(bf16[16,2048]{1,0:T(8,128)(2,1)S(1)} %collective-permute-done.5.refs_6_), channel_id=1, source_target_pairs={{0,1},{1,0},{2,3},{3,2},{4,5},{5,4},{6,7},{7,6},{8,9},{9,8},{10,11... | collective-permute-start | bytes 196616 | tf_op jit(solution)/shard_map/ppermute | solution.py:317
  12.2 4.3 %collective-permute-start.4 = (bf16[16,2048]{1,0:T(8,128)(2,1)S(1)}, bf16[16,2048]{1,0:T(8,128)(2,1)S(1)}, u32[]{:S(2)}, u32[]{:S(2)}) collective-permute-start(bf16[16,2048]{1,0:T(8,128)(2,1)S(1)} %collective-permute-done.after_ref.refs_4_), channel_id=1, source_target_pairs={{0,1},{1,0},{2,3},{3,2},{4,5},{5,4},{6,7},{7,6},{8,9},{9,8},{10,11... | collective-permute-start | bytes 196616 | tf_op jit(solution)/shard_map/ppermute | solution.py:317
  13.7 8.0 %copy-start = (bf16[1,1,112,128,128]{4,3,2,1,0:T(8,128)(2,1)S(1)}, bf16[1,1,112,128,128]{4,3,2,1,0:T(8,128)(2,1)}, u32[]{:S(2)}) copy-start(bf16[1,1,112,128,128]{4,3,2,1,0:T(8,128)(2,1)} %param.9) | copy-start | bytes 11010052
  13.7 8.0 %copy-start.1 = (s32[1,1,112]{2,1,0:T(1,128)S(1)}, s32[1,1,112]{2,1,0:T(1,128)}, u32[]{:S(2)}) copy-start(s32[1,1,112]{2,1,0:T(1,128)} %param.10) | copy-start | bytes 1348
  18.4 1.6 %collective-permute-start.10 = (bf16[28,32,128]{2,1,0:T(8,128)(2,1)S(1)}, bf16[28,32,128]{2,1,0:T(8,128)(2,1)S(1)}, u32[]{:S(2)}, u32[]{:S(2)}) collective-permute-start(bf16[28,32,128]{2,1,0:T(8,128)(2,1)S(1)} %get-tuple-element.43), channel_id=1, source_target_pairs={{0,8},{8,0},{16,24},{24,16},{1,9},{9,1},{17,25},{25,17},{2,10},{10... | collective-permute-start | bytes 688136 | tf_op jit(solution)/shard_map/ppermute | solution.py:317
  20.0 7.7 %collective-permute-start.11 = (bf16[28,32,128]{2,1,0:T(8,128)(2,1)S(1)}, bf16[28,32,128]{2,1,0:T(8,128)(2,1)S(1)}, u32[]{:S(2)}, u32[]{:S(2)}) collective-permute-start(bf16[28,32,128]{2,1,0:T(8,128)(2,1)S(1)} %add.28.own_ref), channel_id=1, source_target_pairs={{0,16},{8,24},{16,0},{24,8},{1,17},{9,25},{17,1},{25,9},{2,18},{10... | collective-permute-start | bytes 688136 | tf_op jit(solution)/shard_map/ppermute | solution.py:317
  24.1 1.4 %collective-permute-start.7 = (bf16[14,32,128]{2,1,0:T(8,128)(2,1)S(1)}, bf16[14,32,128]{2,1,0:T(8,128)(2,1)S(1)}, u32[]{:S(2)}, u32[]{:S(2)}) collective-permute-start(bf16[14,32,128]{2,1,0:T(8,128)(2,1)S(1)} %get-tuple-element.40), channel_id=1, source_target_pairs={{0,8},{8,0},{16,24},{24,16},{1,9},{9,1},{17,25},{25,17},{2,10},{10... | collective-permute-start | bytes 344072 | tf_op jit(solution)/shard_map/ppermute | solution.py:317
  24.2 1.5 %collective-permute-start.8 = (bf16[14,32,128]{2,1,0:T(8,128)(2,1)S(1)}, bf16[14,32,128]{2,1,0:T(8,128)(2,1)S(1)}, u32[]{:S(2)}, u32[]{:S(2)}) collective-permute-start(bf16[14,32,128]{2,1,0:T(8,128)(2,1)S(1)} %get-tuple-element.41), channel_id=1, source_target_pairs={{0,8},{8,0},{16,24},{24,16},{1,9},{9,1},{17,25},{25,17},{2,10},{10... | collective-permute-start | bytes 344072 | tf_op jit(solution)/shard_map/ppermute | solution.py:317
  25.7 7.9 %collective-permute-start.9 = (bf16[28,32,128]{2,1,0:T(8,128)(2,1)S(1)}, bf16[28,32,128]{2,1,0:T(8,128)(2,1)S(1)}, u32[]{:S(2)}, u32[]{:S(2)}) collective-permute-start(bf16[28,32,128]{2,1,0:T(8,128)(2,1)S(1)} %add.27.after_ref.own_ref), channel_id=1, source_target_pairs={{0,16},{8,24},{16,0},{24,8},{1,17},{9,25},{17,1},{25,9},{2,18},{10... | collective-permute-start | bytes 688136 | tf_op jit(solution)/shard_map/ppermute | solution.py:317
  28.1 1.4 %collective-permute-start.12 = (bf16[14,32,128]{2,1,0:T(8,128)(2,1)S(1)}, bf16[14,32,128]{2,1,0:T(8,128)(2,1)S(1)}, u32[]{:S(2)}, u32[]{:S(2)}) collective-permute-start(bf16[14,32,128]{2,1,0:T(8,128)(2,1)S(1)} %get-tuple-element.45.refs_0_), channel_id=1, source_target_pairs={{0,8},{8,0},{16,24},{24,16},{1,9},{9,1},{17,25},{25,17},{2,10},{10... | collective-permute-start | bytes 344072 | tf_op jit(solution)/shard_map/ppermute | solution.py:317
  28.2 1.5 %collective-permute-start.13 = (bf16[14,32,128]{2,1,0:T(8,128)(2,1)S(1)}, bf16[14,32,128]{2,1,0:T(8,128)(2,1)S(1)}, u32[]{:S(2)}, u32[]{:S(2)}) collective-permute-start(bf16[14,32,128]{2,1,0:T(8,128)(2,1)S(1)} %get-tuple-element.46.refs_2_), channel_id=1, source_target_pairs={{0,8},{8,0},{16,24},{24,16},{1,9},{9,1},{17,25},{25,17},{2,10},{10... | collective-permute-start | bytes 344072 | tf_op jit(solution)/shard_map/ppermute | solution.py:317
  33.7 1.6 %collective-permute-start.14 = (bf16[28,32,128]{2,1,0:T(8,128)(2,1)S(1)}, bf16[28,32,128]{2,1,0:T(8,128)(2,1)S(1)}, u32[]{:S(2)}, u32[]{:S(2)}) collective-permute-start(bf16[28,32,128]{2,1,0:T(8,128)(2,1)S(1)} %slope.1.own_ref), channel_id=1, source_target_pairs={{0,8},{8,0},{16,24},{24,16},{1,9},{9,1},{17,25},{25,17},{2,10},{10... | collective-permute-start | bytes 688136 | tf_op jit(solution)/shard_map/ppermute | solution.py:317
  37.7 5.6 %collective-permute-start.15 = (bf16[2,16,2048]{2,1,0:T(8,128)(2,1)S(1)}, bf16[2,16,2048]{2,1,0:T(8,128)(2,1)S(1)}, u32[]{:S(2)}, u32[]{:S(2)}) collective-permute-start(bf16[2,16,2048]{2,1,0:T(8,128)(2,1)S(1)} %get-tuple-element.51), channel_id=1, source_target_pairs={{0,1},{1,0},{2,3},{3,2},{4,5},{5,4},{6,7},{7,6},{8,9},{9,8},{10,11... | collective-permute-start | bytes 393224 | tf_op jit(solution)/shard_map/ppermute | solution.py:317
  42.2 10.8 %collective-permute-start.19 = (bf16[16,2048]{1,0:T(8,128)(2,1)S(1)}, bf16[16,2048]{1,0:T(8,128)(2,1)S(1)}, u32[]{:S(2)}, u32[]{:S(2)}) collective-permute-start(bf16[16,2048]{1,0:T(8,128)(2,1)S(1)} %get-tuple-element.63), channel_id=1, source_target_pairs={{0,2},{1,3},{2,0},{3,1},{4,6},{5,7},{6,4},{7,5},{8,10},{9,11},{10,... | collective-permute-start | bytes 196616 | tf_op jit(solution)/shard_map/ppermute | solution.py:317
  43.3 9.6 %collective-permute-start.16 = (bf16[16,2048]{1,0:T(8,128)(2,1)S(1)}, bf16[16,2048]{1,0:T(8,128)(2,1)S(1)}, u32[]{:S(2)}, u32[]{:S(2)}) collective-permute-start(bf16[16,2048]{1,0:T(8,128)(2,1)S(1)} %get-tuple-element.60), channel_id=1, source_target_pairs={{0,6},{1,7},{2,4},{3,5},{4,2},{5,3},{6,0},{7,1},{8,14},{9,15},{10,... | collective-permute-start | bytes 196616 | tf_op jit(solution)/shard_map/ppermute | solution.py:317
  46.0 7.0 %collective-permute-start.17 = (bf16[16,2048]{1,0:T(8,128)(2,1)S(1)}, bf16[16,2048]{1,0:T(8,128)(2,1)S(1)}, u32[]{:S(2)}, u32[]{:S(2)}) collective-permute-start(bf16[16,2048]{1,0:T(8,128)(2,1)S(1)} %get-tuple-element.61), channel_id=1, source_target_pairs={{0,4},{1,5},{2,6},{3,7},{4,0},{5,1},{6,2},{7,3},{8,12},{9,13},{10,... | collective-permute-start | bytes 196616 | tf_op jit(solution)/shard_map/ppermute | solution.py:317
  46.0 7.0 %collective-permute-start.18 = (bf16[16,2048]{1,0:T(8,128)(2,1)S(1)}, bf16[16,2048]{1,0:T(8,128)(2,1)S(1)}, u32[]{:S(2)}, u32[]{:S(2)}) collective-permute-start(bf16[16,2048]{1,0:T(8,128)(2,1)S(1)} %get-tuple-element.62), channel_id=1, source_target_pairs={{0,3},{1,2},{2,1},{3,0},{4,7},{5,6},{6,5},{7,4},{8,11},{9,10},{10,... | collective-permute-start | bytes 196616 | tf_op jit(solution)/shard_map/ppermute | solution.py:317
  48.6 4.4 %collective-permute-start.20 = (bf16[16,2048]{1,0:T(8,128)(2,1)S(1)}, bf16[16,2048]{1,0:T(8,128)(2,1)S(1)}, u32[]{:S(2)}, u32[]{:S(2)}) collective-permute-start(bf16[16,2048]{1,0:T(8,128)(2,1)S(1)} %get-tuple-element.64), channel_id=1, source_target_pairs={{0,1},{1,0},{2,3},{3,2},{4,5},{5,4},{6,7},{7,6},{8,9},{9,8},{10,11... | collective-permute-start | bytes 196616 | tf_op jit(solution)/shard_map/ppermute | solution.py:317
